TPU v7x, 128 devices: a whole 4x4x4 slice. The times are simulated.
128 devices in a mesh: dp: 16 (over z, y), fsdp: 8 (over x, core).
Axes of the slice: x: 4, y: 4, z: 4, core: 2. Of those that a mesh axis runs over, the one named last changes fastest.
Arguments:
- inputs: bfloat16 [16, 8, 512, 1536], P('dp', 'fsdp'), may hold values from -40 to 40
- norm_gain: float32 [1536], replicated, may hold values from 0.4 to 1.6
- weight_in: bfloat16 [1536, 3072], P('fsdp'), may hold values from -0.15625 to 0.15625
- kernel: float32 [32, 1536], replicated, may hold values from -2.5 to 2.5
- conv_gain: float32 [1536], replicated, may hold values from 0.4 to 1.6
- weight_out: bfloat16 [1536, 1536], P('fsdp'), may hold values from -0.15625 to 0.15625
- out_grad: bfloat16 [16, 8, 512, 1536], P('dp', 'fsdp'), may hold values from -6 to 6
- pack_dest: int32 [8, 64], P('fsdp'), may hold values from 0 to 63, as said below
- utt_blocks: int32 [8, 32], P('fsdp'), may hold values from 1 to 4, 64 in all within a row
- tail_frames: int32 [8, 32], P('fsdp'), may hold values from 1 to 128
Outputs:
- module_out: bfloat16 [16, 8, 512, 1536], P('dp', 'fsdp')
- input_grad: bfloat16 [16, 8, 512, 1536], P('dp', 'fsdp')
- weight_out_grad: float32 [1536, 1536], P(('dp', 'fsdp'))
- kernel_grad: float32 [32, 1536], replicated
Inputs may be any that keep to these rules, and one draw needn't show every extreme that they name: `pack_dest`: each row is a permutation. For every device s the 4 entries s * 4 + k name blocks of 4 different devices (entry // 4), and for each k the entries of the 16 devices name 16 different devices.
All inputs are finite; a program needn't handle non-finite values.
Results may differ from a plain program's by a relative error of at most 0.0069.
Values may be sent and summed in bfloat16 or wider, within the bound.
No kernel may reach another device: no remote copies, remote signals or barrier semaphores. Data moves between devices by JAX's collectives and lax.ppermute only.
A program may use at most 128 MiB of HBM per device.

v0:
```python
import math

import jax
import jax.numpy as jnp
from jax import lax
from jax.sharding import PartitionSpec as P

BLOCK = 128


eps = 1e-05


def padded_2(block, sides, width):
    for axis, dim in sides:
        count = lax.axis_size(axis)
        forward = [(i, i + 1) for i in range(count - 1)]
        backward = [(target, source) for source, target in forward]
        low = lax.ppermute(
            lax.slice_in_dim(block, block.shape[dim] - width, None, axis=dim), axis, forward
        )
        high = lax.ppermute(lax.slice_in_dim(block, 0, width, axis=dim), axis, backward)
        block = jnp.concatenate([low, block, high], axis=dim)
    return block


def norm_forward(values, gain_vec):
    average = jnp.mean(values, axis=-1, keepdims=True)
    centered = values - average
    inverse = lax.rsqrt(jnp.mean(centered * centered, axis=-1, keepdims=True) + eps)
    normed = centered * inverse
    return (normed * gain_vec, normed, inverse)


def norm_backward(grad_in, normed, inverse):
    first_mean = jnp.mean(grad_in, axis=-1, keepdims=True)
    second_mean = jnp.mean(grad_in * normed, axis=-1, keepdims=True)
    return (grad_in - first_mean - normed * second_mean) * inverse


def frame_masks(counts, tail_counts, frames, block_len):
    block_ends = jnp.cumsum(counts)
    block_starts = block_ends - counts
    block_index = frames // block_len
    in_block = frames - block_index * block_len
    inside = (block_index[:, None] >= block_starts[None, :]) & (
        block_index[:, None] < block_ends[None, :]
    )
    number = jnp.arange(counts.shape[0], dtype=jnp.int32)
    owner_ids = jnp.sum(jnp.where(inside, number[None, :] + 1, 0), axis=1) - 1
    is_last = block_index[:, None] == block_ends[None, :] - 1
    valid_count = jnp.sum(
        jnp.where(inside, jnp.where(is_last, tail_counts[None, :], block_len), 0), axis=1
    )
    return (owner_ids, in_block < valid_count)


def depthwise(padded, owner_pad, owner_ids, kernel):
    row_count = owner_ids.shape[0]
    running = jnp.zeros((row_count, kernel.shape[1]), jnp.float32)
    for tap_index in range(kernel.shape[0]):
        same_utt = (owner_pad[tap_index : tap_index + row_count] == owner_ids)[:, None]
        running = (
            running
            + jnp.where(
                same_utt, padded[tap_index : tap_index + row_count].astype(jnp.float32), 0.0
            )
            * kernel[tap_index][None, :]
        )
    return running


def depthwise_transpose(padded, owner_pad, owner_ids, kernel):
    row_count = owner_ids.shape[0]
    tap_count = kernel.shape[0]
    running = jnp.zeros((row_count, kernel.shape[1]), jnp.float32)
    for tap_index in range(tap_count):
        begin = tap_count - tap_index
        same_utt = (owner_pad[begin : begin + row_count] == owner_ids)[:, None]
        running = (
            running
            + jnp.where(same_utt, padded[begin : begin + row_count].astype(jnp.float32), 0.0)
            * kernel[tap_index][None, :]
        )
    return running


def kernel_terms(grad_in, padded, owner_pad, owner_ids, tap_count):
    row_count = owner_ids.shape[0]
    grad_wide = grad_in.astype(jnp.float32)
    per_tap = []
    for tap_index in range(tap_count):
        same_utt = (owner_pad[tap_index : tap_index + row_count] == owner_ids)[:, None]
        per_tap.append(
            jnp.sum(
                jnp.where(
                    same_utt,
                    padded[tap_index : tap_index + row_count].astype(jnp.float32) * grad_wide,
                    0.0,
                ),
                axis=0,
            )
        )
    return jnp.stack(per_tap)


def add_rows(left, piece):
    return jnp.dot(left, piece, preferred_element_type=jnp.float32)


def times_rows(left, piece):
    return lax.dot_general(
        left, piece, (((1,), (1,)), ((), ())), preferred_element_type=jnp.float32
    )


def outer_rows(left, right, grad_scale):
    return (
        lax.dot_general(left, right, (((0,), (0,)), ((), ())), preferred_element_type=jnp.float32)
        * grad_scale
    )


def local(
    inputs,
    norm_gain,
    weight_in,
    kernel,
    conv_gain,
    weight_out,
    out_grad,
    pack_dest,
    utt_blocks,
    tail_frames,
):
    dp_count = lax.axis_size("dp")
    all_count = lax.axis_size(("dp", "fsdp"))
    dp_place = lax.axis_index("dp")
    row_count = inputs.shape[2]
    model_width = inputs.shape[3]
    local_blocks = row_count // BLOCK
    tap_count = kernel.shape[0]
    half_width = tap_count // 2
    packing = pack_dest[0]
    own_targets = (
        lax.dynamic_slice_in_dim(packing, dp_place * local_blocks, local_blocks) // local_blocks
    )
    peer_ids = jnp.arange(dp_count, dtype=jnp.int32)
    sender = (own_targets[None, :] == peer_ids[:, None]).astype(jnp.bfloat16)
    own_blocks = inputs[0, 0].reshape(local_blocks, BLOCK * model_width)
    outgoing = jnp.dot(sender, own_blocks, preferred_element_type=jnp.float32).astype(jnp.bfloat16)
    arrived = lax.all_to_all(
        outgoing.reshape(dp_count, BLOCK, model_width),
        "dp",
        split_axis=0,
        concat_axis=0,
        tiled=True,
    )
    wanted = dp_place * local_blocks + jnp.arange(local_blocks, dtype=jnp.int32)
    slot_ids = jnp.arange(packing.shape[0], dtype=jnp.int32)
    source = jnp.sum(
        jnp.where(packing[None, :] == wanted[:, None], slot_ids[None, :] // local_blocks, 0), axis=1
    )
    picker = (source[:, None] == peer_ids[None, :]).astype(jnp.bfloat16)
    packed = jnp.dot(
        picker, arrived.reshape(dp_count, BLOCK * model_width), preferred_element_type=jnp.float32
    )
    packed = packed.astype(jnp.bfloat16).reshape(row_count, model_width)
    first_frame = dp_place * row_count
    frame_ids = first_frame + jnp.arange(row_count, dtype=jnp.int32)
    pad_ids = first_frame - half_width + jnp.arange(row_count + 2 * half_width, dtype=jnp.int32)
    owner_ids, valid = frame_masks(utt_blocks[0], tail_frames[0], frame_ids, BLOCK)
    owner_pad = frame_masks(utt_blocks[0], tail_frames[0], pad_ids, BLOCK)[0]
    valid_col = valid[:, None]
    scaled_in, normed_in, inverse_in = norm_forward(packed.astype(jnp.float32), norm_gain)
    hidden_in = scaled_in.astype(jnp.bfloat16)
    projected = add_rows(hidden_in, lax.all_gather(weight_in, "fsdp", axis=0, tiled=True))
    linear_part = projected[:, :model_width]
    gate_vals = jax.nn.sigmoid(projected[:, model_width:])
    glu = jnp.where(valid_col, linear_part * gate_vals, 0.0).astype(jnp.bfloat16)
    glu_pad = padded_2(glu, (("dp", 0),), half_width)
    conv = jnp.where(valid_col, depthwise(glu_pad, owner_pad, owner_ids, kernel), 0.0)
    scaled_c, normed_c, inverse_c = norm_forward(conv, conv_gain)
    sigmoid_c = jax.nn.sigmoid(scaled_c)
    swished = (scaled_c * sigmoid_c).astype(jnp.bfloat16)
    mixed = add_rows(swished, lax.all_gather(weight_out, "fsdp", axis=0, tiled=True))
    module_out = mixed.astype(jnp.bfloat16)
    upstream = out_grad[0, 0]
    grad_s = times_rows(upstream, lax.all_gather(weight_out, "fsdp", axis=0, tiled=True))
    grad_scale = 1.0 / math.sqrt(row_count * all_count)
    weight_out_grad = lax.psum_scatter(
        outer_rows(swished, upstream, grad_scale), ("dp", "fsdp"), scatter_dimension=0, tiled=True
    )
    grad_n = grad_s * sigmoid_c * (1.0 + scaled_c * (1.0 - sigmoid_c))
    grad_conv = jnp.where(
        valid_col, norm_backward(grad_n * conv_gain, normed_c, inverse_c), 0.0
    ).astype(jnp.bfloat16)
    grad_pad = padded_2(grad_conv, (("dp", 0),), half_width)
    kernel_grad = lax.psum(
        kernel_terms(grad_conv, glu_pad, owner_pad, owner_ids, tap_count) * grad_scale,
        ("dp", "fsdp"),
    )
    grad_glu = jnp.where(
        valid_col, depthwise_transpose(grad_pad, owner_pad, owner_ids, kernel), 0.0
    )
    grad_proj = jnp.concatenate(
        [grad_glu * gate_vals, grad_glu * linear_part * gate_vals * (1.0 - gate_vals)], axis=1
    ).astype(jnp.bfloat16)
    grad_hidden = times_rows(grad_proj, lax.all_gather(weight_in, "fsdp", axis=0, tiled=True))
    input_grad = norm_backward(grad_hidden * norm_gain, normed_in, inverse_in).astype(jnp.bfloat16)
    return (
        module_out.reshape(1, 1, row_count, model_width),
        input_grad.reshape(1, 1, row_count, model_width),
        weight_out_grad,
        kernel_grad,
    )


def solution(mesh):
    in_specs = (
        P("dp", "fsdp", None, None),
        P(),
        P("fsdp", None),
        P(),
        P(),
        P("fsdp", None),
        P("dp", "fsdp", None, None),
        P("fsdp", None),
        P("fsdp", None),
        P("fsdp", None),
    )
    out_specs = (
        P("dp", "fsdp", None, None),
        P("dp", "fsdp", None, None),
        P(("dp", "fsdp"), None),
        P(),
    )
    return jax.shard_map(local, mesh=mesh, in_specs=in_specs, out_specs=out_specs, check_vma=False)
```

profile of v0, /device:TPU:1, one launch (start us, length us, event | category | flops | bytes accessed | tf_op | source)
XLA Modules:
  0.0 847.4 jit_solution(15710565592349081402)
XLA Ops:
  7.9 2.6 reshape_squeeze.3
  10.6 1.8 convolution_convert_fusion
  12.4 4.7 copy.18
  17.2 8.8 %all-to-all-start = ((bf16[16,128,1536]{2,1,0:T(8,128)(2,1)}), bf16[16,128,1536]{2,1,0:T(8,128)(2,1)}, u32[]{:S(2)}, u32[]{:S(2)}) async-start(bf16[16,128,1536]{2,1,0:T(8,128)(2,1)} %bitcast.35), calls=%async_computation | async-start | bytes 12582912 | tf_op jit(solution)/shard_map/all_to_all | solution.py:152
  30.1 88.1 %all-to-all-done = bf16[16,128,1536]{2,1,0:T(8,128)(2,1)} async-done(((bf16[16,128,1536]{2,1,0:T(8,128)(2,1)}), bf16[16,128,1536]{2,1,0:T(8,128)(2,1)}, u32[]{:S(2)}, u32[]{:S(2)}) %all-to-all-start) | async-done | bytes 6291488 | tf_op jit(solution)/shard_map/all_to_all | solution.py:152
  118.2 6.3 copy.19
  124.5 2.8 fusion.1
  127.3 5.7 reshape.214
  133.0 2.1 reduce_sum.400
  135.1 2.3 multiply_reduce_fusion.3
  137.5 8.7 %fusion.157 = f32[512,3072]{1,0:T(8,128)S(1)} fusion(bf16[1536,3072]{1,0:T(8,128)(2,1)} %all-gather.3.cloned.1.call-done, f32[512,1536]{1,0:T(8,128)} %reshape.214, f32[1536]{0:T(1024)S(1)} %copy-done.89, f32[512]{0:T(512)S(1)} %add_rsqrt_fusion.1, f32[512]{0:T(512)S(1)} %broadcast_multiply_fusion.6), kind=kOutput, calls=%fused_computation.300 | convolution fusion | flops 4834983936 | bytes 18884608 | tf_op jit(solution)/shard_map/dot_general | solution.py:108
  147.1 1.7 copy-done.3
  150.7 4.2 collective-permute-start
  156.3 34.6 %fusion.236 = (f32[512]{0:T(512)S(1)}, f32[512,1536]{1,0:T(8,128)}) fusion(f32[1536]{0:T(1024)} %get-tuple-element.70, bf16[16,1536]{1,0:T(8,128)(2,1)S(1)} %collective-permute-done.1, bf16[512,1536]{1,0:T(8,128)(2,1)S(1)} %select_convert_fusion.1, pred[512]{0:T(512)(128)(4,1)} %get-tuple-element.84, f32[1536]{0:T(1024)} %get-tuple-element.71, ...), kind=kLoop, calls=%fused_computation.508 | loop fusion | flops 174587392 | bytes 5032448 | tf_op jit(solution)/shard_map/reduce_sum | solution.py:28
  191.0 2.5 multiply_reduce_fusion.2
  194.1 5.4 convolution_multiply_fusion
  199.5 362.0 %fusion = f32[16,1536]{1,0:T(8,128)S(1)} fusion(f32[1536,1536]{1,0:T(8,128)} %convolution_multiply_fusion), kind=kCustom, calls=%all-reduce-scatter | all-reduce-scatter fusion | flops 3145729 | bytes 9535488
  561.5 1.3 collective-permute-start.34
  562.8 1.9 collective-permute-start.33
  564.8 6.9 fusion.234
  572.0 9.4 %fusion.146 = (f32[1536]{0:T(1024)S(1)}, f32[1536]{0:T(1024)S(1)}, f32[1536]{0:T(1024)S(1)}, f32[1536]{0:T(1024)S(1)}, f32[1536]{0:T(1024)S(1)}, /*index=5*/f32[1536]{0:T(1024)S(1)}, bf16[512,1536]{1,0:T(8,128)(2,1)S(1)}) fusion(pred[512]{0:T(512)(128)(4,1)S(1)} %copy-done.49, bf16[16,1536]{1,0:T(8,128)(2,1)S(1)} %collective-permute-done.1, ...), kind=kLoop, calls=%fused_computation.273 | loop fusion | flops 40098816 | bytes 9534976 | tf_op jit(solution)/shard_map/reduce_sum | solution.py:95
  582.1 1.9 collective-permute-start.3
  585.3 2.3 collective-permute-start.35
  587.6 3.2 fusion.92
  593.3 3.9 fusion.116
  599.0 3.4 fusion.114
  604.3 3.2 fusion.112
  611.1 5.3 fusion.144
  617.0 9.4 %fusion.148 = (f32[1536]{0:T(1024)S(1)}, f32[1536]{0:T(1024)S(1)}, f32[1536]{0:T(1024)S(1)}, f32[1536]{0:T(1024)S(1)}, f32[1536]{0:T(1024)S(1)}, /*index=5*/f32[1536]{0:T(1024)S(1)}) fusion(bf16[512,1536]{1,0:T(8,128)(2,1)S(1)} %get-tuple-element.74, bf16[16,1536]{1,0:T(8,128)(2,1)S(1)} %collective-permute-done.1, ...), kind=kLoop, calls=%fused_computation.275 | loop fusion | flops 33807360 | bytes 3234816 | tf_op jit(solution)/shard_map/reduce_sum | solution.py:95
  626.7 2.6 stack.131
  630.1 7.2 fusion.156
  637.3 1.9 collective-permute-start.32
  639.2 14.0 %collective-permute-start.31 = (f32[16,1536]{1,0:T(8,128)S(1)}, f32[16,1536]{1,0:T(8,128)}, u32[]{:S(2)}, u32[]{:S(2)}) collective-permute-start(f32[16,1536]{1,0:T(8,128)S(1)} %fusion), channel_id=1, source_target_pairs={{0,28},{1,29},{2,30},{3,31},{4,32},{5,33},{6,34},{7,35},{8,36},{9,... | collective-permute-start | bytes 294920
  653.2 1.6 collective-permute-start.30
  654.9 2.1 collective-permute-start.29
  657.0 43.8 %multiply_convert_fusion.2 = (bf16[512,1536]{1,0:T(8,128)(2,1)S(1)}, f32[512,1536]{1,0:T(8,128)}) fusion(f32[512,3072]{1,0:T(8,128)} %copy-done.3, f32[1536]{0:T(1024)} %get-tuple-element.70, bf16[512,1536]{1,0:T(8,128)(2,1)S(1)} %get-tuple-element.74, bf16[16,1536]{1,0:T(8,128)(2,1)} %collective-permute-done.3, pred[512]{0:T(512)(128)(4,1)} %get-tuple-element.115, ...), kind=kLoop, calls=%fused_computation.286 | loop fusion | flops 177733632 | bytes 9748992 | tf_op jit(solution)/shard_map/convert.1
  700.8 1.3 collective-permute-start.28
  702.1 1.3 collective-permute-start.27
  703.5 2.5 collective-permute-start.26
  706.0 5.8 collective-permute-start.25
  711.8 2.8 collective-permute-start.24
  714.7 5.1 multiply_convert_fusion.1
  719.8 2.2 collective-permute-start.23
  722.1 3.4 collective-permute-start.22
  726.8 3.7 collective-permute-start.20
  730.6 1.9 collective-permute-start.19
  732.6 8.0 fusion.233
  740.7 1.6 collective-permute-start.18
  742.3 1.7 collective-permute-start.17
  743.9 4.0 collective-permute-start.16
  747.9 3.4 collective-permute-start.15
  751.4 3.7 collective-permute-start.14
  756.5 3.3 collective-permute-start.12
  761.1 2.3 collective-permute-start.10
  763.4 3.5 collective-permute-start.9
  766.9 3.5 collective-permute-start.8
  770.5 3.2 collective-permute-start.7
  773.7 3.3 collective-permute-start.6
  777.0 2.0 collective-permute-start.5
  779.0 3.3 collective-permute-start.4
  782.3 2.0 fusion.158
  785.7 51.8 %concatenate.81 = f32[524,1536]{1,0:T(8,128)} concatenate(f32[12,1536]{1,0:T(8,128)} %collective-permute-done.35, f32[16,1536]{1,0:T(8,128)S(1)} %collective-permute-done.34, f32[16,1536]{1,0:T(8,128)} %collective-permute-done.33, f32[16,1536]{1,0:T(8,128)} %collective-permute-done.32, f32[16,1536]{1,0:T(8,128)} %collective-permute-done.31, ...), dimensions={0} | concatenate | bytes 6438912
  837.5 1.6 constant_dynamic-slice_fusion
  839.1 1.6 copy.21
  (295 shorter events, 28.0 us)
Async XLA Ops:
  7.2 186.9 %copy-start = (bf16[1,1,512,1536]{3,2,1,0:T(8,128)(2,1)S(1)}, bf16[1,1,512,1536]{3,2,1,0:T(8,128)(2,1)}, u32[]{:S(2)}) copy-start(bf16[1,1,512,1536]{3,2,1,0:T(8,128)(2,1)} %param.16) | copy-start | bytes 4718596
  7.2 130.3 %all-gather.3.cloned.1.call-start = ((), (), s32[]{:S(2)}) async-start(), calls=%async_computation.1 | async-start | bytes 10616832 | tf_op jit(solution)/shard_map/all_gather | solution.py:177
  17.2 101.1 %all-to-all-start = ((bf16[16,128,1536]{2,1,0:T(8,128)(2,1)}), bf16[16,128,1536]{2,1,0:T(8,128)(2,1)}, u32[]{:S(2)}, u32[]{:S(2)}) async-start(bf16[16,128,1536]{2,1,0:T(8,128)(2,1)} %bitcast.35), calls=%async_computation | async-start | bytes 12582912 | tf_op jit(solution)/shard_map/all_to_all | solution.py:152
  25.9 538.8 %all-gather.5.cloned.1.call-start = ((), (), s32[]{:S(2)}) async-start(), calls=%async_computation.2 | async-start | bytes 5308416 | tf_op jit(solution)/shard_map/all_gather | solution.py:186
  26.7 812.4 %all-reduce.4.cloned.1.call-start = ((), (), s32[]{:S(2)}) async-start(), calls=%async_computation.3 | async-start | bytes 393216 | tf_op jit(solution)/shard_map/psum | solution.py:199
  28.6 127.6 %copy-start.25 = (f32[1536]{0:T(1024)}, f32[1536]{0:T(1024)S(1)}, u32[]{:S(2)}) copy-start(f32[1536]{0:T(1024)S(1)} %get-tuple-element.42) | copy-start | bytes 18436
  28.6 127.6 %copy-start.27 = (f32[1536]{0:T(1024)}, f32[1536]{0:T(1024)S(1)}, u32[]{:S(2)}) copy-start(f32[1536]{0:T(1024)S(1)} %get-tuple-element.43) | copy-start | bytes 18436
  28.6 127.6 %copy-start.29 = (f32[1536]{0:T(1024)}, f32[1536]{0:T(1024)S(1)}, u32[]{:S(2)}) copy-start(f32[1536]{0:T(1024)S(1)} %get-tuple-element.44) | copy-start | bytes 18436
  28.6 127.6 %copy-start.31 = (f32[1536]{0:T(1024)}, f32[1536]{0:T(1024)S(1)}, u32[]{:S(2)}) copy-start(f32[1536]{0:T(1024)S(1)} %get-tuple-element.45) | copy-start | bytes 18436
  28.6 127.6 %copy-start.33 = (f32[1536]{0:T(1024)}, f32[1536]{0:T(1024)S(1)}, u32[]{:S(2)}) copy-start(f32[1536]{0:T(1024)S(1)} %get-tuple-element.46) | copy-start | bytes 18436
  28.6 127.7 %copy-start.35 = (f32[1536]{0:T(1024)}, f32[1536]{0:T(1024)S(1)}, u32[]{:S(2)}) copy-start(f32[1536]{0:T(1024)S(1)} %get-tuple-element.47) | copy-start | bytes 18436
  28.6 127.7 %copy-start.37 = (f32[1536]{0:T(1024)}, f32[1536]{0:T(1024)S(1)}, u32[]{:S(2)}) copy-start(f32[1536]{0:T(1024)S(1)} %get-tuple-element.48) | copy-start | bytes 18436
  28.6 127.7 %copy-start.38 = (f32[1536]{0:T(1024)}, f32[1536]{0:T(1024)S(1)}, u32[]{:S(2)}) copy-start(f32[1536]{0:T(1024)S(1)} %get-tuple-element.49) | copy-start | bytes 18436
  28.6 127.7 %copy-start.39 = (f32[1536]{0:T(1024)}, f32[1536]{0:T(1024)S(1)}, u32[]{:S(2)}) copy-start(f32[1536]{0:T(1024)S(1)} %get-tuple-element.50) | copy-start | bytes 18436
  28.6 127.7 %copy-start.40 = (f32[1536]{0:T(1024)}, f32[1536]{0:T(1024)S(1)}, u32[]{:S(2)}) copy-start(f32[1536]{0:T(1024)S(1)} %get-tuple-element.51) | copy-start | bytes 18436
  28.6 127.7 %copy-start.41 = (f32[1536]{0:T(1024)}, f32[1536]{0:T(1024)S(1)}, u32[]{:S(2)}) copy-start(f32[1536]{0:T(1024)S(1)} %get-tuple-element.52) | copy-start | bytes 18436
  28.6 127.7 %copy-start.42 = (f32[1536]{0:T(1024)}, f32[1536]{0:T(1024)S(1)}, u32[]{:S(2)}) copy-start(f32[1536]{0:T(1024)S(1)} %get-tuple-element.53) | copy-start | bytes 18436
  28.7 117.5 %copy-start.47 = (pred[512]{0:T(512)(128)(4,1)}, pred[512]{0:T(512)(128)(4,1)S(1)}, u32[]{:S(2)}) copy-start(pred[512]{0:T(512)(128)(4,1)S(1)} %subtract_compare_fusion) | copy-start | bytes 1540
  149.5 6.3 collective-permute-start.1
  150.7 5.5 collective-permute-start
  156.3 37.8 %copy-start.88 = (f32[1536]{0:T(1024)S(1)}, f32[1536]{0:T(1024)}, u32[]{:S(2)}) copy-start(f32[1536]{0:T(1024)} %param.14) | copy-start | bytes 18436
  561.5 93.3 %collective-permute-start.34 = (f32[16,1536]{1,0:T(8,128)S(1)}, f32[16,1536]{1,0:T(8,128)S(1)}, u32[]{:S(2)}, u32[]{:S(2)}) collective-permute-start(f32[16,1536]{1,0:T(8,128)S(1)} %fusion), channel_id=1, source_target_pairs={{0,31},{1,32},{2,33},{3,34},{4,35},{5,36},{6,37},{7,38},{8,39},{9,... | collective-permute-start | bytes 294920
  562.8 138.0 %collective-permute-start.33 = (f32[16,1536]{1,0:T(8,128)S(1)}, f32[16,1536]{1,0:T(8,128)}, u32[]{:S(2)}, u32[]{:S(2)}) collective-permute-start(f32[16,1536]{1,0:T(8,128)S(1)} %fusion), channel_id=1, source_target_pairs={{0,30},{1,31},{2,32},{3,33},{4,34},{5,35},{6,36},{7,37},{8,38},{9,... | collective-permute-start | bytes 294920
  582.1 55.2 %collective-permute-start.3 = (bf16[16,1536]{1,0:T(8,128)(2,1)}, bf16[16,1536]{1,0:T(8,128)(2,1)}, u32[]{:S(2)}, u32[]{:S(2)}) collective-permute-start(bf16[16,1536]{1,0:T(8,128)(2,1)} %get-tuple-element.80), channel_id=1, source_target_pairs={{0,8},{8,16},{16,24},{24,32},{32,40},{40,48},{48,56},{56,64},{64,7... | collective-permute-start | bytes 147464 | tf_op jit(solution)/shard_map/ppermute | solution.py:19
  584.0 55.2 %collective-permute-start.2 = (bf16[16,1536]{1,0:T(8,128)(2,1)}, bf16[16,1536]{1,0:T(8,128)(2,1)}, u32[]{:S(2)}, u32[]{:S(2)}) collective-permute-start(bf16[16,1536]{1,0:T(8,128)(2,1)} %get-tuple-element.79), channel_id=1, source_target_pairs={{8,0},{16,8},{24,16},{32,24},{40,32},{48,40},{56,48},{64,56},{72,6... | collective-permute-start | bytes 147464 | tf_op jit(solution)/shard_map/ppermute | solution.py:22
  585.3 68.0 %collective-permute-start.35 = (f32[12,1536]{1,0:T(8,128)S(1)}, f32[12,1536]{1,0:T(8,128)}, u32[]{:S(2)}, u32[]{:S(2)}) collective-permute-start(f32[12,1536]{1,0:T(8,128)S(1)} %slice.842), channel_id=1, source_target_pairs={{0,32},{1,33},{2,34},{3,35},{4,36},{5,37},{6,38},{7,39},{8,40},{9,... | collective-permute-start | bytes 221192
  630.0 26.9 %copy-start.26 = (f32[1536]{0:T(1024)S(1)}, f32[1536]{0:T(1024)}, u32[]{:S(2)}) copy-start(f32[1536]{0:T(1024)} %copy-done.25) | copy-start | bytes 18436
  630.0 26.9 %copy-start.28 = (f32[1536]{0:T(1024)S(1)}, f32[1536]{0:T(1024)}, u32[]{:S(2)}) copy-start(f32[1536]{0:T(1024)} %copy-done.27) | copy-start | bytes 18436
  630.0 26.9 %copy-start.30 = (f32[1536]{0:T(1024)S(1)}, f32[1536]{0:T(1024)}, u32[]{:S(2)}) copy-start(f32[1536]{0:T(1024)} %copy-done.29) | copy-start | bytes 18436
  637.3 64.8 %collective-permute-start.32 = (f32[16,1536]{1,0:T(8,128)S(1)}, f32[16,1536]{1,0:T(8,128)}, u32[]{:S(2)}, u32[]{:S(2)}) collective-permute-start(f32[16,1536]{1,0:T(8,128)S(1)} %fusion), channel_id=1, source_target_pairs={{0,29},{1,30},{2,31},{3,32},{4,33},{5,34},{6,35},{7,36},{8,37},{9,... | collective-permute-start | bytes 294920
  639.2 64.2 %collective-permute-start.31 = (f32[16,1536]{1,0:T(8,128)S(1)}, f32[16,1536]{1,0:T(8,128)}, u32[]{:S(2)}, u32[]{:S(2)}) collective-permute-start(f32[16,1536]{1,0:T(8,128)S(1)} %fusion), channel_id=1, source_target_pairs={{0,28},{1,29},{2,30},{3,31},{4,32},{5,33},{6,34},{7,35},{8,36},{9,... | collective-permute-start | bytes 294920
  653.2 52.8 %collective-permute-start.30 = (f32[16,1536]{1,0:T(8,128)S(1)}, f32[16,1536]{1,0:T(8,128)S(1)}, u32[]{:S(2)}, u32[]{:S(2)}) collective-permute-start(f32[16,1536]{1,0:T(8,128)S(1)} %fusion), channel_id=1, source_target_pairs={{0,27},{1,28},{2,29},{3,30},{4,31},{5,32},{6,33},{7,34},{8,35},{9,... | collective-permute-start | bytes 294920
  654.9 57.0 %collective-permute-start.29 = (f32[16,1536]{1,0:T(8,128)S(1)}, f32[16,1536]{1,0:T(8,128)}, u32[]{:S(2)}, u32[]{:S(2)}) collective-permute-start(f32[16,1536]{1,0:T(8,128)S(1)} %fusion), channel_id=1, source_target_pairs={{0,26},{1,27},{2,28},{3,29},{4,30},{5,31},{6,32},{7,33},{8,34},{9,... | collective-permute-start | bytes 294920
  700.8 19.0 %collective-permute-start.28 = (f32[16,1536]{1,0:T(8,128)S(1)}, f32[16,1536]{1,0:T(8,128)S(1)}, u32[]{:S(2)}, u32[]{:S(2)}) collective-permute-start(f32[16,1536]{1,0:T(8,128)S(1)} %fusion), channel_id=1, source_target_pairs={{0,25},{1,26},{2,27},{3,28},{4,29},{5,30},{6,31},{7,32},{8,33},{9,... | collective-permute-start | bytes 294920
  702.1 19.9 %collective-permute-start.27 = (f32[16,1536]{1,0:T(8,128)S(1)}, f32[16,1536]{1,0:T(8,128)S(1)}, u32[]{:S(2)}, u32[]{:S(2)}) collective-permute-start(f32[16,1536]{1,0:T(8,128)S(1)} %fusion), channel_id=1, source_target_pairs={{0,24},{1,25},{2,26},{3,27},{4,28},{5,29},{6,30},{7,31},{8,32},{9,... | collective-permute-start | bytes 294920
  703.5 22.0 %collective-permute-start.26 = (f32[16,1536]{1,0:T(8,128)S(1)}, f32[16,1536]{1,0:T(8,128)S(1)}, u32[]{:S(2)}, u32[]{:S(2)}) collective-permute-start(f32[16,1536]{1,0:T(8,128)S(1)} %fusion), channel_id=1, source_target_pairs={{0,23},{1,24},{2,25},{3,26},{4,27},{5,28},{6,29},{7,30},{8,31},{9,... | collective-permute-start | bytes 294920
  706.0 20.8 %collective-permute-start.25 = (f32[16,1536]{1,0:T(8,128)S(1)}, f32[16,1536]{1,0:T(8,128)S(1)}, u32[]{:S(2)}, u32[]{:S(2)}) collective-permute-start(f32[16,1536]{1,0:T(8,128)S(1)} %fusion), channel_id=1, source_target_pairs={{0,22},{1,23},{2,24},{3,25},{4,26},{5,27},{6,28},{7,29},{8,30},{9,... | collective-permute-start | bytes 294920
  711.8 18.8 %collective-permute-start.24 = (f32[16,1536]{1,0:T(8,128)S(1)}, f32[16,1536]{1,0:T(8,128)S(1)}, u32[]{:S(2)}, u32[]{:S(2)}) collective-permute-start(f32[16,1536]{1,0:T(8,128)S(1)} %fusion), channel_id=1, source_target_pairs={{0,21},{1,22},{2,23},{3,24},{4,25},{5,26},{6,27},{7,28},{8,29},{9,... | collective-permute-start | bytes 294920
  719.8 20.8 %collective-permute-start.23 = (f32[16,1536]{1,0:T(8,128)S(1)}, f32[16,1536]{1,0:T(8,128)S(1)}, u32[]{:S(2)}, u32[]{:S(2)}) collective-permute-start(f32[16,1536]{1,0:T(8,128)S(1)} %fusion), channel_id=1, source_target_pairs={{0,20},{1,21},{2,22},{3,23},{4,24},{5,25},{6,26},{7,27},{8,28},{9,... | collective-permute-start | bytes 294920
  722.1 20.2 %collective-permute-start.22 = (f32[16,1536]{1,0:T(8,128)S(1)}, f32[16,1536]{1,0:T(8,128)S(1)}, u32[]{:S(2)}, u32[]{:S(2)}) collective-permute-start(f32[16,1536]{1,0:T(8,128)S(1)} %fusion), channel_id=1, source_target_pairs={{0,19},{1,20},{2,21},{3,22},{4,23},{5,24},{6,25},{7,26},{8,27},{9,... | collective-permute-start | bytes 294920
  725.5 18.4 %collective-permute-start.21 = (f32[16,1536]{1,0:T(8,128)S(1)}, f32[16,1536]{1,0:T(8,128)S(1)}, u32[]{:S(2)}, u32[]{:S(2)}) collective-permute-start(f32[16,1536]{1,0:T(8,128)S(1)} %fusion), channel_id=1, source_target_pairs={{0,18},{1,19},{2,20},{3,21},{4,22},{5,23},{6,24},{7,25},{8,26},{9,... | collective-permute-start | bytes 294920
  726.8 21.1 %collective-permute-start.20 = (f32[16,1536]{1,0:T(8,128)S(1)}, f32[16,1536]{1,0:T(8,128)S(1)}, u32[]{:S(2)}, u32[]{:S(2)}) collective-permute-start(f32[16,1536]{1,0:T(8,128)S(1)} %fusion), channel_id=1, source_target_pairs={{0,17},{1,18},{2,19},{3,20},{4,21},{5,22},{6,23},{7,24},{8,25},{9,... | collective-permute-start | bytes 294920
  730.6 20.8 %collective-permute-start.19 = (f32[16,1536]{1,0:T(8,128)S(1)}, f32[16,1536]{1,0:T(8,128)S(1)}, u32[]{:S(2)}, u32[]{:S(2)}) collective-permute-start(f32[16,1536]{1,0:T(8,128)S(1)} %fusion), channel_id=1, source_target_pairs={{0,16},{1,17},{2,18},{3,19},{4,20},{5,21},{6,22},{7,23},{8,24},{9,... | collective-permute-start | bytes 294920
  740.6 43.7 %copy-start.17 = (f32[16,1536]{1,0:T(8,128)}, f32[16,1536]{1,0:T(8,128)S(1)}, u32[]{:S(2)}) copy-start(f32[16,1536]{1,0:T(8,128)S(1)} %collective-permute-done.23) | copy-start | bytes 294916
  740.7 14.5 %collective-permute-start.18 = (f32[16,1536]{1,0:T(8,128)S(1)}, f32[16,1536]{1,0:T(8,128)S(1)}, u32[]{:S(2)}, u32[]{:S(2)}) collective-permute-start(f32[16,1536]{1,0:T(8,128)S(1)} %fusion), channel_id=1, source_target_pairs={{0,15},{1,16},{2,17},{3,18},{4,19},{5,20},{6,21},{7,22},{8,23},{9,... | collective-permute-start | bytes 294920
  742.2 42.1 %copy-start.18 = (f32[16,1536]{1,0:T(8,128)}, f32[16,1536]{1,0:T(8,128)S(1)}, u32[]{:S(2)}) copy-start(f32[16,1536]{1,0:T(8,128)S(1)} %collective-permute-done.22) | copy-start | bytes 294916
  742.3 14.2 %collective-permute-start.17 = (f32[16,1536]{1,0:T(8,128)S(1)}, f32[16,1536]{1,0:T(8,128)S(1)}, u32[]{:S(2)}, u32[]{:S(2)}) collective-permute-start(f32[16,1536]{1,0:T(8,128)S(1)} %fusion), channel_id=1, source_target_pairs={{0,14},{1,15},{2,16},{3,17},{4,18},{5,19},{6,20},{7,21},{8,22},{9,... | collective-permute-start | bytes 294920
  743.9 40.4 %copy-start.19 = (f32[16,1536]{1,0:T(8,128)}, f32[16,1536]{1,0:T(8,128)S(1)}, u32[]{:S(2)}) copy-start(f32[16,1536]{1,0:T(8,128)S(1)} %collective-permute-done.21) | copy-start | bytes 294916
  743.9 15.8 %collective-permute-start.16 = (f32[16,1536]{1,0:T(8,128)S(1)}, f32[16,1536]{1,0:T(8,128)S(1)}, u32[]{:S(2)}, u32[]{:S(2)}) collective-permute-start(f32[16,1536]{1,0:T(8,128)S(1)} %fusion), channel_id=1, source_target_pairs={{0,13},{1,14},{2,15},{3,16},{4,17},{5,18},{6,19},{7,20},{8,21},{9,... | collective-permute-start | bytes 294920
  747.9 36.4 %copy-start.20 = (f32[16,1536]{1,0:T(8,128)}, f32[16,1536]{1,0:T(8,128)S(1)}, u32[]{:S(2)}) copy-start(f32[16,1536]{1,0:T(8,128)S(1)} %collective-permute-done.20) | copy-start | bytes 294916
  747.9 13.1 %collective-permute-start.15 = (f32[16,1536]{1,0:T(8,128)S(1)}, f32[16,1536]{1,0:T(8,128)S(1)}, u32[]{:S(2)}, u32[]{:S(2)}) collective-permute-start(f32[16,1536]{1,0:T(8,128)S(1)} %fusion), channel_id=1, source_target_pairs={{0,12},{1,13},{2,14},{3,15},{4,16},{5,17},{6,18},{7,19},{8,20},{9,... | collective-permute-start | bytes 294920
  751.4 32.9 %copy-start.21 = (f32[16,1536]{1,0:T(8,128)}, f32[16,1536]{1,0:T(8,128)S(1)}, u32[]{:S(2)}) copy-start(f32[16,1536]{1,0:T(8,128)S(1)} %collective-permute-done.19) | copy-start | bytes 294916
  751.4 12.0 %collective-permute-start.14 = (f32[16,1536]{1,0:T(8,128)S(1)}, f32[16,1536]{1,0:T(8,128)S(1)}, u32[]{:S(2)}, u32[]{:S(2)}) collective-permute-start(f32[16,1536]{1,0:T(8,128)S(1)} %fusion), channel_id=1, source_target_pairs={{0,11},{1,12},{2,13},{3,14},{4,15},{5,16},{6,17},{7,18},{8,19},{9,... | collective-permute-start | bytes 294920
  755.1 11.7 %collective-permute-start.13 = (f32[16,1536]{1,0:T(8,128)S(1)}, f32[16,1536]{1,0:T(8,128)S(1)}, u32[]{:S(2)}, u32[]{:S(2)}) collective-permute-start(f32[16,1536]{1,0:T(8,128)S(1)} %fusion), channel_id=1, source_target_pairs={{0,10},{1,11},{2,12},{3,13},{4,14},{5,15},{6,16},{7,17},{8,18},{9,... | collective-permute-start | bytes 294920
  756.5 14.0 %collective-permute-start.12 = (f32[16,1536]{1,0:T(8,128)S(1)}, f32[16,1536]{1,0:T(8,128)S(1)}, u32[]{:S(2)}, u32[]{:S(2)}) collective-permute-start(f32[16,1536]{1,0:T(8,128)S(1)} %fusion), channel_id=1, source_target_pairs={{0,9},{1,10},{2,11},{3,12},{4,13},{5,14},{6,15},{7,16},{8,17},{9,1... | collective-permute-start | bytes 294920
  759.8 13.9 %collective-permute-start.11 = (f32[16,1536]{1,0:T(8,128)S(1)}, f32[16,1536]{1,0:T(8,128)S(1)}, u32[]{:S(2)}, u32[]{:S(2)}) collective-permute-start(f32[16,1536]{1,0:T(8,128)S(1)} %fusion), channel_id=1, source_target_pairs={{0,8},{1,9},{2,10},{3,11},{4,12},{5,13},{6,14},{7,15},{8,16},{9,17... | collective-permute-start | bytes 294920
  761.1 15.9 %collective-permute-start.10 = (f32[16,1536]{1,0:T(8,128)S(1)}, f32[16,1536]{1,0:T(8,128)S(1)}, u32[]{:S(2)}, u32[]{:S(2)}) collective-permute-start(f32[16,1536]{1,0:T(8,128)S(1)} %fusion), channel_id=1, source_target_pairs={{0,7},{1,8},{2,9},{3,10},{4,11},{5,12},{6,13},{7,14},{8,15},{9,16}... | collective-permute-start | bytes 294920
  763.4 15.6 %collective-permute-start.9 = (f32[16,1536]{1,0:T(8,128)S(1)}, f32[16,1536]{1,0:T(8,128)S(1)}, u32[]{:S(2)}, u32[]{:S(2)}) collective-permute-start(f32[16,1536]{1,0:T(8,128)S(1)} %fusion), channel_id=1, source_target_pairs={{0,6},{1,7},{2,8},{3,9},{4,10},{5,11},{6,12},{7,13},{8,14},{9,15},... | collective-permute-start | bytes 294920
  766.9 17.4 %collective-permute-start.8 = (f32[16,1536]{1,0:T(8,128)S(1)}, f32[16,1536]{1,0:T(8,128)S(1)}, u32[]{:S(2)}, u32[]{:S(2)}) collective-permute-start(f32[16,1536]{1,0:T(8,128)S(1)} %fusion), channel_id=1, source_target_pairs={{0,5},{1,6},{2,7},{3,8},{4,9},{5,10},{6,11},{7,12},{8,13},{9,14},{... | collective-permute-start | bytes 294920
  770.5 13.9 %collective-permute-start.7 = (f32[16,1536]{1,0:T(8,128)S(1)}, f32[16,1536]{1,0:T(8,128)S(1)}, u32[]{:S(2)}, u32[]{:S(2)}) collective-permute-start(f32[16,1536]{1,0:T(8,128)S(1)} %fusion), channel_id=1, source_target_pairs={{0,4},{1,5},{2,6},{3,7},{4,8},{5,9},{6,10},{7,11},{8,12},{9,13},{1... | collective-permute-start | bytes 294920
  773.7 10.7 %collective-permute-start.6 = (f32[16,1536]{1,0:T(8,128)S(1)}, f32[16,1536]{1,0:T(8,128)S(1)}, u32[]{:S(2)}, u32[]{:S(2)}) collective-permute-start(f32[16,1536]{1,0:T(8,128)S(1)} %fusion), channel_id=1, source_target_pairs={{0,3},{1,4},{2,5},{3,6},{4,7},{5,8},{6,9},{7,10},{8,11},{9,12},{10... | collective-permute-start | bytes 294920
  777.0 7.4 collective-permute-start.5
  779.0 6.7 collective-permute-start.4
  782.3 58.4 %copy-start.1 = (bf16[1,1,512,1536]{3,2,1,0:T(8,128)(2,1)S(1)}, bf16[1,1,512,1536]{3,2,1,0:T(8,128)(2,1)}, u32[]{:S(2)}) copy-start(bf16[1,1,512,1536]{3,2,1,0:T(8,128)(2,1)} %param.16) | copy-start | bytes 4718596
  (67 other events, 685.9 us)
Sparse Core Ops, SparseCore 0:
  9.7 57.7 all-gather.2
  69.2 34.5 all-gather.4
  630.1 158.5 all-reduce.3
where the time goes:
time: 855 us; the launch traced here: 847 us
  blocking collectives  362 us (42%)
  other arithmetic  134 us (16%)
  starting transfers between devices  110 us (13%)
  local copies, waits for them, and re-layouts  94.2 us (11%)
  waiting for transfers between devices  90.1 us (11%)
  matrix products  40.8 us (5%)
  between operations  15.9 us (2%)
    unnamed x1, blocking collectives  362 us
    unnamed x32, starting transfers between devices  92.7 us
    all_to_all x1, waiting for transfers between devices, local(): lax.all_to_all(outgoing.reshape(dp_count, BLOCK, model_width), 'dp', spli...  88.1 us
    unnamed x188, local copies, waits for them, and re-layouts  69.9 us
    another operation x4, other arithmetic  49.1 us
    reduce_sum x7, other arithmetic, kernel_terms(): jnp.sum(jnp.where(same_utt, padded[tap_index:tap_index + row_count].astyp...  37.8 us
    reduce_sum x2, other arithmetic, norm_forward(): average = jnp.mean(values, axis=-1, keepdims=True)  36.8 us
  transfers between devices with their start and end apart: 40, of which 2 were waited for; matrix products, arithmetic and copies ran while one was open for 74% of the time, Pallas kernels for 0%

commit v1 on v0

v1 whole, which is shorter than its diff:
```python
import functools
import math

import jax
import jax.numpy as jnp
from jax import lax
from jax.experimental import pallas as pl
from jax.experimental.pallas import tpu as pltpu
from jax.sharding import PartitionSpec as P

BLOCK = 128
LANES = 128
HALF = 16
TAPS = 32
EPS = 1e-05
VMEM = 56 * 2**20
F32 = jnp.float32
BF16 = jnp.bfloat16

LEFT, RIGHT, COUNT, SLOT = 0, 4, 8, 12


def row_mean(values):
    return jnp.mean(values, axis=-1, keepdims=True)


def normalise(values):
    centered = values - row_mean(values)
    inverse = lax.rsqrt(row_mean(centered * centered) + EPS)
    return centered * inverse, inverse


def below(count, rows, first=0):
    return lax.broadcasted_iota(jnp.int32, (rows, 1), 0) + first < count


def params():
    return pltpu.CompilerParams(vmem_limit_bytes=VMEM)


def cost(flops, nbytes, transcendentals=0):
    return pl.CostEstimate(
        flops=flops, bytes_accessed=nbytes, transcendentals=transcendentals
    )


def whole(shape):
    return pl.BlockSpec(shape, lambda *_: (0,) * len(shape))


def reorder_kernel(order, x_ref, o_ref):
    for t in range(x_ref.shape[0]):
        o_ref[t] = x_ref[order[t]]


def reorder(order, x):
    return pl.pallas_call(
        reorder_kernel,
        out_shape=jax.ShapeDtypeStruct(x.shape, x.dtype),
        grid_spec=pltpu.PrefetchScalarGridSpec(
            num_scalar_prefetch=1,
            grid=(1,),
            in_specs=[whole(x.shape)],
            out_specs=whole(x.shape),
        ),
        compiler_params=params(),
        cost_estimate=cost(0, 2 * x.size * 2),
        name="reorder",
    )(order, x)


def project_kernel(
    meta, x_ref, gain_ref, wl_ref, wg_ref, lin_ref, gate_ref, glu_ref, low_ref, high_ref, hidden
):
    blocks = x_ref.shape[0]

    @pl.when(pl.program_id(0) == 0)
    def _():
        for j in range(blocks):
            normed, _ = normalise(x_ref[meta[SLOT + j]].astype(F32))
            hidden[j * BLOCK : (j + 1) * BLOCK] = (normed * gain_ref[...]).astype(BF16)

    held = hidden[...]
    lin = jnp.dot(held, wl_ref[...], preferred_element_type=F32)
    gate = jax.nn.sigmoid(jnp.dot(held, wg_ref[...], preferred_element_type=F32))
    lin_ref[...] = lin
    gate_ref[...] = gate
    for j in range(blocks):
        rows = slice(j * BLOCK, (j + 1) * BLOCK)
        glu = jnp.where(below(meta[COUNT + j], BLOCK), lin[rows] * gate[rows], 0.0).astype(BF16)
        glu_ref[rows] = glu
        if j == 0:
            low_ref[...] = glu[:HALF]
        if j == blocks - 1:
            high_ref[...] = glu[BLOCK - HALF :]


def project(meta, x, gain, weight, tile=256):
    blocks, _, width = x.shape
    rows = blocks * BLOCK
    steps = width // tile
    column = pl.BlockSpec((rows, tile), lambda n, _: (0, n))
    edge = pl.BlockSpec((HALF, tile), lambda n, _: (0, n))
    return pl.pallas_call(
        project_kernel,
        out_shape=[
            jax.ShapeDtypeStruct((rows, width), F32),
            jax.ShapeDtypeStruct((rows, width), F32),
            jax.ShapeDtypeStruct((rows, width), BF16),
            jax.ShapeDtypeStruct((HALF, width), BF16),
            jax.ShapeDtypeStruct((HALF, width), BF16),
        ],
        grid_spec=pltpu.PrefetchScalarGridSpec(
            num_scalar_prefetch=1,
            grid=(steps,),
            in_specs=[
                whole(x.shape),
                whole((1, width)),
                pl.BlockSpec((width, tile), lambda n, _: (0, n)),
                pl.BlockSpec((width, tile), lambda n, _: (0, n + steps)),
            ],
            out_specs=[column, column, column, edge, edge],
            scratch_shapes=[pltpu.VMEM((rows, width), BF16)],
        ),
        compiler_params=params(),
        cost_estimate=cost(4 * rows * width * width, 22 * 2**20),
        name="project",
    )(meta, x, gain, weight, weight)


def fill(pad, left, middle, right, left_ok, right_ok):
    pad[0:HALF] = jnp.where(left_ok > 0, left.astype(F32), 0.0)
    pad[HALF : HALF + BLOCK] = middle.astype(F32)
    pad[HALF + BLOCK :] = jnp.where(right_ok > 0, right.astype(F32), 0.0)


def fill_inner(pad, meta, b, src):
    at = pl.multiple_of(b * BLOCK, BLOCK)
    fill(
        pad,
        src[pl.ds(pl.multiple_of(at - HALF, HALF), HALF)],
        src[pl.ds(at, BLOCK)],
        src[pl.ds(pl.multiple_of(at + BLOCK, BLOCK), HALF)],
        meta[LEFT + b],
        meta[RIGHT + b],
    )


def fill_first(pad, meta, src, low):
    fill(pad, low[...], src[0:BLOCK], src[BLOCK : BLOCK + HALF], meta[LEFT], meta[RIGHT])


def fill_last(pad, meta, src, high):
    rows = src.shape[0]
    last = rows // BLOCK - 1
    fill(
        pad,
        src[rows - BLOCK - HALF : rows - BLOCK],
        src[rows - BLOCK :],
        high[...],
        meta[LEFT + last],
        meta[RIGHT + last],
    )


def slabs(pad, lanes, first):
    for p in range(8):
        offsets = [o for o in range(first, first + TAPS) if o % 8 == p]
        count = BLOCK + 8 * (offsets[-1] // 8)
        yield pad[pl.ds(p, count), lanes].reshape(count // 8, 8, LANES), offsets


def depthwise(pad, taps, lanes, first, tap_of):
    total = jnp.zeros((BLOCK // 8, 8, LANES), F32)
    for slab, offsets in slabs(pad, lanes, first):
        for o in offsets:
            i = tap_of(o)
            total = total + slab[o // 8 : o // 8 + BLOCK // 8] * taps[i : i + 1, lanes][None]
    return total.reshape(BLOCK, LANES)


def lane_tiles(width):
    return lambda body: pl.loop(0, width // LANES)(
        lambda c: body(pl.ds(pl.multiple_of(c * LANES, LANES), LANES))
    )


def pad_by_step(inner, meta, src, low, high, pad):
    step = pl.program_id(0)
    if inner:
        b = step + 1
        fill_inner(pad, meta, b, src)
        return b

    @pl.when(step == 0)
    def _():
        fill_first(pad, meta, src, low)

    @pl.when(step == 1)
    def _():
        fill_last(pad, meta, src, high)

    return step * (src.shape[0] // BLOCK - 1)


def conv_kernel(inner, meta, *refs):
    if inner:
        src, taps, gain, conv_ref, swished_ref, pad = refs
        low = high = None
    else:
        src, taps, gain, low, high, _, _, conv_ref, swished_ref, pad = refs
    b = pad_by_step(inner, meta, src, low, high, pad)
    valid = below(meta[COUNT + b], BLOCK)

    @lane_tiles(src.shape[1])
    def _(lanes):
        conv_ref[:, lanes] = jnp.where(valid, depthwise(pad, taps, lanes, 0, lambda o: o), 0.0)

    @pl.loop(0, BLOCK // 16)
    def _(r):
        rows = pl.ds(pl.multiple_of(r * 16, 16), 16)
        normed, _ = normalise(conv_ref[rows])
        scaled = normed * gain[...]
        swished_ref[rows] = (scaled * jax.nn.sigmoid(scaled)).astype(BF16)


def split_call(kernel, inner, meta, operands, edges, held, outs, width, flops):
    rows = operands[0].shape[0]
    last = rows // BLOCK - 1

    def place(n, _):
        return (n + 1 if inner else n * last, 0)

    in_specs = []
    for a in operands:
        if a.shape[0] == rows and a is not operands[0]:
            in_specs.append(pl.BlockSpec((BLOCK, a.shape[1]), place))
        else:
            in_specs.append(whole(a.shape))
    args = list(operands)
    aliases = {}
    if not inner:
        args += list(edges)
        in_specs += [whole(e.shape) for e in edges]
        for n, h in enumerate(held):
            aliases[1 + len(args)] = n
            args.append(h)
            in_specs.append(pl.BlockSpec(memory_space=pl.ANY))
    return pl.pallas_call(
        functools.partial(kernel, inner),
        out_shape=[jax.ShapeDtypeStruct(*o) for o in outs],
        grid_spec=pltpu.PrefetchScalarGridSpec(
            num_scalar_prefetch=1,
            grid=(2,),
            in_specs=in_specs,
            out_specs=[pl.BlockSpec((BLOCK, o[0][1]), place) for o in outs],
            scratch_shapes=[pltpu.VMEM((BLOCK + 2 * HALF, width), F32)],
        ),
        input_output_aliases=aliases,
        compiler_params=params(),
        cost_estimate=cost(flops, 6 * 2**20),
        name=kernel.__name__ + ("_inner" if inner else "_edges"),
    )(meta, *args)


def conv_forward(inner, meta, glu, taps, gain, edges=(), held=()):
    rows, width = glu.shape
    return split_call(
        conv_kernel,
        inner,
        meta,
        (glu, taps, gain),
        edges,
        held,
        [((rows, width), F32), ((rows, width), BF16)],
        width,
        4 * 10**9,
    )


def grad_conv_kernel(meta, conv_ref, grad_ref, gain_ref, out_ref, low_ref, high_ref):
    b = pl.program_id(0)

    @pl.loop(0, BLOCK // 16)
    def _(r):
        rows = pl.ds(pl.multiple_of(r * 16, 16), 16)
        gain = gain_ref[...]
        normed, inverse = normalise(conv_ref[rows])
        scaled = normed * gain
        sig = jax.nn.sigmoid(scaled)
        g = grad_ref[rows] * sig * (1.0 + scaled * (1.0 - sig)) * gain
        back = (g - row_mean(g) - normed * row_mean(g * normed)) * inverse
        out_ref[rows] = jnp.where(below(meta[COUNT + b], 16, r * 16), back, 0.0).astype(BF16)

    @pl.when(b == 0)
    def _():
        low_ref[...] = out_ref[0:HALF]

    @pl.when(b == pl.num_programs(0) - 1)
    def _():
        high_ref[...] = out_ref[BLOCK - HALF :]


def grad_conv_call(meta, conv, grad_s, gain):
    rows, width = conv.shape
    block = pl.BlockSpec((BLOCK, width), lambda n, _: (n, 0))
    return pl.pallas_call(
        grad_conv_kernel,
        out_shape=[
            jax.ShapeDtypeStruct((rows, width), BF16),
            jax.ShapeDtypeStruct((HALF, width), BF16),
            jax.ShapeDtypeStruct((HALF, width), BF16),
        ],
        grid_spec=pltpu.PrefetchScalarGridSpec(
            num_scalar_prefetch=1,
            grid=(rows // BLOCK,),
            in_specs=[block, block, whole((1, width))],
            out_specs=[block, whole((HALF, width)), whole((HALF, width))],
        ),
        compiler_params=params(),
        cost_estimate=cost(2 * 10**9, 8 * 2**20),
        name="grad_conv",
    )(meta, conv, grad_s, gain)


def taps_kernel(meta, src, grad_ref, low, high, out_ref, pad, total):
    b = pl.program_id(0)
    last = pl.num_programs(0) - 1
    width = src.shape[1]

    @pl.when(b == 0)
    def _():
        fill_first(pad, meta, src, low)
        total[...] = jnp.zeros_like(total)

    @pl.when(b == last)
    def _():
        fill_last(pad, meta, src, high)

    @pl.when((b > 0) & (b < last))
    def _():
        fill_inner(pad, meta, b, src)

    @lane_tiles(width)
    def _(lanes):
        grad = grad_ref[:, lanes].astype(F32).reshape(BLOCK // 8, 8, LANES)
        for slab, offsets in slabs(pad, lanes, 0):
            for o in offsets:
                total[o, :, lanes] += jnp.sum(
                    slab[o // 8 : o // 8 + BLOCK // 8] * grad, axis=0
                )

    @pl.when(b == last)
    def _():
        out_ref[...] = jnp.sum(total[...], axis=1)


def taps_gradient(meta, glu, grad_conv, edges):
    rows, width = glu.shape
    return pl.pallas_call(
        taps_kernel,
        out_shape=jax.ShapeDtypeStruct((TAPS, width), F32),
        grid_spec=pltpu.PrefetchScalarGridSpec(
            num_scalar_prefetch=1,
            grid=(rows // BLOCK,),
            in_specs=[
                whole(glu.shape),
                pl.BlockSpec((BLOCK, width), lambda n, _: (n, 0)),
                whole((HALF, width)),
                whole((HALF, width)),
            ],
            out_specs=whole((TAPS, width)),
            scratch_shapes=[
                pltpu.VMEM((BLOCK + 2 * HALF, width), F32),
                pltpu.VMEM((TAPS, 8, width), F32),
            ],
        ),
        compiler_params=params(),
        cost_estimate=cost(8 * 10**9, 4 * 2**20),
        name="taps_gradient",
    )(meta, glu, grad_conv, *edges)


def back_kernel(inner, meta, *refs):
    if inner:
        src, taps, lin_ref, gate_ref, out_ref, pad = refs
        low = high = None
    else:
        src, taps, lin_ref, gate_ref, low, high, _, out_ref, pad = refs
    width = src.shape[1]
    b = pad_by_step(inner, meta, src, low, high, pad)
    valid = below(meta[COUNT + b], BLOCK)

    @pl.loop(0, width // LANES)
    def _(c):
        at = pl.multiple_of(c * LANES, LANES)
        lanes = pl.ds(at, LANES)
        grad = jnp.where(valid, depthwise(pad, taps, lanes, 1, lambda o: TAPS - o), 0.0)
        gate = gate_ref[:, lanes]
        through = grad * gate
        out_ref[:, lanes] = through.astype(BF16)
        out_ref[:, pl.ds(pl.multiple_of(at + width, LANES), LANES)] = (
            through * lin_ref[:, lanes] * (1.0 - gate)
        ).astype(BF16)


def conv_backward(inner, meta, grad_conv, taps, lin, gate, edges=(), held=()):
    rows, width = grad_conv.shape
    return split_call(
        back_kernel,
        inner,
        meta,
        (grad_conv, taps, lin, gate),
        edges,
        held,
        [((rows, 2 * width), BF16)],
        width,
        4 * 10**9,
    )


def input_kernel(meta, x_ref, gain_ref, grad_ref, w_ref, out_ref, hidden):
    n = pl.program_id(0)
    tile = w_ref.shape[0]
    hidden[:, pl.ds(pl.multiple_of(n * tile, tile), tile)] = lax.dot_general(
        grad_ref[...], w_ref[...], (((1,), (1,)), ((), ())), preferred_element_type=F32
    )

    @pl.when(n == pl.num_programs(0) - 1)
    def _():
        for j in range(x_ref.shape[0]):
            rows = slice(j * BLOCK, (j + 1) * BLOCK)
            normed, inverse = normalise(x_ref[meta[SLOT + j]].astype(F32))
            g = hidden[rows] * gain_ref[...]
            out_ref[rows] = (
                (g - row_mean(g) - normed * row_mean(g * normed)) * inverse
            ).astype(BF16)


def input_gradient(meta, x, gain, grad_proj, weight, tile=256):
    rows = grad_proj.shape[0]
    width = weight.shape[0]
    return pl.pallas_call(
        input_kernel,
        out_shape=jax.ShapeDtypeStruct((rows, width), BF16),
        grid_spec=pltpu.PrefetchScalarGridSpec(
            num_scalar_prefetch=1,
            grid=(width // tile,),
            in_specs=[
                whole(x.shape),
                whole((1, width)),
                whole(grad_proj.shape),
                pl.BlockSpec((tile, weight.shape[1]), lambda n, _: (n, 0)),
            ],
            out_specs=whole((rows, width)),
            scratch_shapes=[pltpu.VMEM((rows, width), F32)],
        ),
        compiler_params=params(),
        cost_estimate=cost(4 * rows * width * width, 16 * 2**20),
        name="input_gradient",
    )(meta, x, gain, grad_proj, weight)


def halves_of_neighbours(low, high):
    count = lax.axis_size("dp")
    forward = [(i, i + 1) for i in range(count - 1)]
    backward = [(i + 1, i) for i in range(count - 1)]
    return lax.ppermute(high, "dp", forward), lax.ppermute(low, "dp", backward)


def swap(values, axis, bits):
    return lax.ppermute(values, axis, [(i, i ^ bits) for i in range(lax.axis_size(axis))])


def sum_of_four(values, axis, low_bit):
    one, two = low_bit, 2 * low_bit
    first, second, third = (swap(values, axis, b) for b in (one, two, one + two))
    return (values + first) + (second + third)


def sum_everywhere(values, core):
    half = values.shape[0] // 2
    own = lax.dynamic_slice_in_dim(values, core * half, half)
    other = lax.dynamic_slice_in_dim(values, (1 - core) * half, half)
    own = own + swap(other, "fsdp", 1)
    own = sum_of_four(own, "fsdp", 2)
    own = sum_of_four(own, "dp", 1)
    own = sum_of_four(own, "dp", 4)
    other = swap(own, "fsdp", 1)
    return jnp.where(
        core == 0, jnp.concatenate([own, other]), jnp.concatenate([other, own])
    )


def spread(values, axis):
    return lax.all_to_all(values, axis, split_axis=0, concat_axis=0, tiled=True)


def outer(left, right):
    return lax.dot_general(left, right, (((0,), (0,)), ((), ())), preferred_element_type=F32)


def summed_outer(left, right, core, scale):
    width = right.shape[1]
    half = width // 2
    dp_count, fsdp_count = lax.axis_size("dp"), lax.axis_size("fsdp")
    ours = lax.dynamic_slice_in_dim(right, core * half, half, axis=1)
    theirs = lax.dynamic_slice_in_dim(right, (1 - core) * half, half, axis=1)
    arrived = swap(outer(left, theirs).astype(BF16), "fsdp", 1)
    both = (outer(left, ours) + arrived.astype(F32)).astype(BF16)
    rows = left.shape[1] // dp_count
    over_dp = jnp.sum(spread(both.reshape(dp_count, rows, half), "dp").astype(F32), axis=0)
    rows //= fsdp_count
    pieces = spread((over_dp * scale).reshape(fsdp_count, rows, half), "fsdp")
    pieces = jnp.sum(pieces.reshape(fsdp_count // 2, 2, rows, half), axis=0)
    return jnp.concatenate([pieces[0], pieces[1]], axis=1)


def scalars(packing, counts, tails, place, blocks):
    mine = place * blocks + jnp.arange(blocks, dtype=jnp.int32)
    number = jnp.arange(counts.shape[0], dtype=jnp.int32)
    ends = jnp.sum(jnp.where(number[:, None] <= number[None, :], counts[:, None], 0), axis=0)
    opens = (ends - counts)[None, :] == mine[:, None]
    closes = (ends - 1)[None, :] == mine[:, None]
    left = 1 - jnp.sum(opens.astype(jnp.int32), axis=1)
    right = 1 - jnp.sum(closes.astype(jnp.int32), axis=1)
    valid = BLOCK + jnp.sum(jnp.where(closes, tails[None, :] - BLOCK, 0), axis=1)
    number = jnp.arange(packing.shape[0], dtype=jnp.int32)
    slot = jnp.sum(
        jnp.where(packing[None, :] == mine[:, None], number[None, :] % blocks, 0), axis=1
    )
    return jnp.concatenate([left, right, valid, slot]).astype(jnp.int32)


def target_order(packing, place, blocks):
    count = packing.shape[0] // blocks
    color = place // blocks
    number = jnp.arange(packing.shape[0], dtype=jnp.int32)
    chosen = (number % blocks == color)[None, :]
    goes = (packing // blocks)[None, :] == jnp.arange(count, dtype=jnp.int32)[:, None]
    return jnp.sum(jnp.where(chosen & goes, (number // blocks)[None, :], 0), axis=1)


def local(
    inputs,
    norm_gain,
    weight_in,
    kernel,
    conv_gain,
    weight_out,
    out_grad,
    pack_dest,
    utt_blocks,
    tail_frames,
):
    dp_count = lax.axis_size("dp")
    place = lax.axis_index("dp")
    core = lax.axis_index("fsdp") % 2
    rows, width = inputs.shape[2:]
    blocks = rows // BLOCK
    scale = 1.0 / math.sqrt(rows * lax.axis_size(("dp", "fsdp")))
    full_in = lax.all_gather(weight_in, "fsdp", axis=0, tiled=True)
    full_out = lax.all_gather(weight_out, "fsdp", axis=0, tiled=True)
    meta = scalars(pack_dest[0], utt_blocks[0], tail_frames[0], place, blocks)
    order = target_order(pack_dest[0], place, blocks)
    gain_in = norm_gain.reshape(1, width)
    gain_conv = conv_gain.reshape(1, width)

    quarters = spread(inputs.reshape(dp_count, rows // dp_count, width), "dp")
    arrived = spread(reorder(order, quarters), "dp").reshape(blocks, BLOCK, width)

    lin, gate, glu, low, high = project(meta, arrived, gain_in, full_in)
    glu_edges = halves_of_neighbours(low, high)
    held = conv_forward(True, meta, glu, kernel, gain_conv)
    conv, swished = conv_forward(False, meta, glu, kernel, gain_conv, glu_edges, held)

    upstream = out_grad[0, 0]
    weight_out_grad = summed_outer(swished, upstream, core, scale)
    grad_s = lax.dot_general(
        upstream, full_out, (((1,), (1,)), ((), ())), preferred_element_type=F32
    )
    grad_conv, low, high = grad_conv_call(meta, conv, grad_s, gain_conv)
    edges = halves_of_neighbours(low, high)
    taps_grad = taps_gradient(meta, glu, grad_conv, glu_edges)
    kernel_grad = sum_everywhere(taps_grad * scale, core)
    held = conv_backward(True, meta, grad_conv, kernel, lin, gate)
    [grad_proj] = conv_backward(False, meta, grad_conv, kernel, lin, gate, edges, held)
    input_grad = input_gradient(meta, arrived, gain_in, grad_proj, full_in)
    module_out = jnp.dot(swished, full_out, preferred_element_type=F32).astype(BF16)
    return (
        module_out.reshape(1, 1, rows, width),
        input_grad.reshape(1, 1, rows, width),
        weight_out_grad,
        kernel_grad,
    )


def solution(mesh):
    in_specs = (
        P("dp", "fsdp", None, None),
        P(),
        P("fsdp", None),
        P(),
        P(),
        P("fsdp", None),
        P("dp", "fsdp", None, None),
        P("fsdp", None),
        P("fsdp", None),
        P("fsdp", None),
    )
    out_specs = (
        P("dp", "fsdp", None, None),
        P("dp", "fsdp", None, None),
        P(("dp", "fsdp"), None),
        P(),
    )
    return jax.shard_map(local, mesh=mesh, in_specs=in_specs, out_specs=out_specs, check_vma=False)
```

time: 855 us -> 259 us (0.30)
  blocking collectives: 362 us -> 0 us
  other arithmetic: 134 us -> 6.25 us
  Pallas kernels: 0 us -> 98.1 us
  local copies, waits for them, and re-layouts: 94.2 us -> 6.23 us
  starting transfers between devices: 110 us -> 54.4 us
  waiting for transfers between devices: 90.1 us -> 55.6 us
  matrix products: 40.8 us -> 22.4 us
    unnamed x1 -> x0, blocking collectives: 362 us -> none
    pallas_call x0 -> x9, Pallas kernels: none -> 98.1 us  [the longest x4 42.5 us: split_call(): pl.pallas_call(functools.partial(kernel, inner), out_shape=[jax.ShapeDtyp...]
    unnamed x32 -> x0, starting transfers between devices: 92.7 us -> none
    reduce_sum x14 -> x6, other arithmetic: 79.8 us -> 3.15 us  [the longest x1 2.02 us: summed_outer(): jnp.sum(spread(both.reshape(dp_count, rows, half), 'dp').astype(F32), axi...]
    unnamed x188 -> x28, local copies, waits for them, and re-layouts: 69.9 us -> 4.19 us
    another operation x4 -> x0, other arithmetic: 49.1 us -> none
    all_to_all x1 -> x4, waiting for transfers between devices: 88.1 us -> 40.8 us  [spread(): return lax.all_to_all(values, axis, split_axis=0, concat_axis=0, tiled=True)]
    ppermute x4 -> x16, starting transfers between devices: 8.66 us -> 27.4 us  [the longest x12 18.4 us: swap(): lax.ppermute(values, axis, [(i, i ^ bits) for i in range(lax.axis_size(ax...]
  transfers between devices with their start and end apart: 40 -> 22, of which waited for: 2 -> 3; matrix products, arithmetic and copies ran while one was open for 74% -> 12% of each run, Pallas kernels for 0% -> 38%
where the time goes in v1:
time: 259 us; the launch traced here: 257 us
  Pallas kernels  98.1 us (38%)
  waiting for transfers between devices  55.6 us (21%)
  starting transfers between devices  54.4 us (21%)
  matrix products  22.4 us (9%)
  between operations  14.4 us (6%)
  other arithmetic  6.25 us (2%)
  local copies, waits for them, and re-layouts  6.23 us (2%)
    pallas_call x4, Pallas kernels, split_call(): pl.pallas_call(functools.partial(kernel, inner), out_shape=[jax.ShapeDtyp...  42.5 us
    all_to_all x4, waiting for transfers between devices, spread(): return lax.all_to_all(values, axis, split_axis=0, concat_axis=0, tiled=True)  40.8 us
    all_to_all x4, starting transfers between devices, spread(): return lax.all_to_all(values, axis, split_axis=0, concat_axis=0, tiled=True)  26.9 us
    ppermute x12, starting transfers between devices, swap(): lax.ppermute(values, axis, [(i, i ^ bits) for i in range(lax.axis_size(ax...  18.4 us
    pallas_call x1, Pallas kernels, input_gradient(): pl.pallas_call(input_kernel, out_shape=jax.ShapeDtypeStruct((rows, width)...  13.7 us
    ppermute x12, waiting for transfers between devices, swap(): lax.ppermute(values, axis, [(i, i ^ bits) for i in range(lax.axis_size(ax...  13.4 us
    pallas_call x1, Pallas kernels, grad_conv_call(): pl.pallas_call(grad_conv_kernel, out_shape=[jax.ShapeDtypeStruct((rows, w...  13.1 us
    pallas_call x1, Pallas kernels, project(): pl.pallas_call(project_kernel, out_shape=[jax.ShapeDtypeStruct((rows, wid...  12.8 us
  transfers between devices with their start and end apart: 22, of which 3 were waited for; matrix products, arithmetic and copies ran while one was open for 12% of the time, Pallas kernels for 38%

profile of v1, /device:TPU:1, one launch (start us, length us, event | category | flops | bytes accessed | tf_op | source)
XLA Modules:
  0.0 257.4 jit_solution(18400578888478800205)
XLA Ops:
  7.2 0.0 copy-start
  7.2 0.0 all-gather.3.cloned.1.call-start
  7.2 0.7 all-gather.3.cloned.1.call-update
  7.9 0.0 all-gather.5.cloned.1.call-start
  8.0 0.7 all-gather.5.cloned.1.call-update
  8.7 8.6 %all-to-all-start = ((bf16[16,32,1536]{2,1,0:T(8,128)(2,1)}), bf16[16,32,1536]{2,1,0:T(8,128)(2,1)S(1)}, u32[]{:S(2)}, u32[]{:S(2)}) async-start(bf16[16,32,1536]{2,1,0:T(8,128)(2,1)} %bitcast.40), calls=%async_computation | async-start | bytes 3145728 | tf_op jit(solution)/shard_map/all_to_all | solution.py:496
  17.4 0.6 select_reduce_fusion.1.order
  18.0 0.1 select_reduce_fusion
  18.1 22.1 %all-to-all-done.x_ref = bf16[16,32,1536]{2,1,0:T(8,128)(2,1)S(1)} async-done(((bf16[16,32,1536]{2,1,0:T(8,128)(2,1)}), bf16[16,32,1536]{2,1,0:T(8,128)(2,1)S(1)}, u32[]{:S(2)}, u32[]{:S(2)}) %all-to-all-start) | async-done | bytes 1572896 | tf_op jit(solution)/shard_map/all_to_all | solution.py:496
  40.2 1.1 copy-done.2
  41.3 3.3 %reorder.1 = bf16[16,32,1536]{2,1,0:T(8,128)(2,1)} custom-call(s32[16]{0:T(128)} %select_reduce_fusion.1.order, bf16[16,32,1536]{2,1,0:T(8,128)(2,1)} %copy-done.2), custom_call_target="tpu_custom_call" | custom-call | bytes 3145728 | tf_op jit(solution)/shard_map/reorder/pallas_call | solution.py:57
  44.6 4.9 %all-to-all-start.1 = ((bf16[16,32,1536]{2,1,0:T(8,128)(2,1)}), bf16[16,32,1536]{2,1,0:T(8,128)(2,1)S(1)}, u32[]{:S(2)}, u32[]{:S(2)}) async-start(bf16[16,32,1536]{2,1,0:T(8,128)(2,1)} %reorder.1), calls=%async_computation.1 | async-start | bytes 3145728 | tf_op jit(solution)/shard_map/all_to_all | solution.py:496
  49.6 0.6 reshape.80.gain_ref
  50.2 0.6 reshape.81.refs_2_.gain_ref
  50.8 0.2 select_reduce_fusion.2
  51.0 0.2 fusion.8
  51.2 0.7 pad_add_fusion.meta
  51.9 18.7 %all-to-all-done.1 = bf16[16,32,1536]{2,1,0:T(8,128)(2,1)S(1)} async-done(((bf16[16,32,1536]{2,1,0:T(8,128)(2,1)}), bf16[16,32,1536]{2,1,0:T(8,128)(2,1)S(1)}, u32[]{:S(2)}, u32[]{:S(2)}) %all-to-all-start.1) | async-done | bytes 1572896 | tf_op jit(solution)/shard_map/all_to_all | solution.py:496
  70.6 1.2 copy-done.1
  71.8 12.8 %project.1 = (f32[512,1536]{1,0:T(8,128)}, f32[512,1536]{1,0:T(8,128)}, bf16[512,1536]{1,0:T(8,128)(2,1)}, bf16[16,1536]{1,0:T(8,128)(2,1)}, bf16[16,1536]{1,0:T(8,128)(2,1)}) custom-call(s32[16]{0:T(128)} %pad_add_fusion.meta, bf16[4,128,1536]{2,1,0:T(8,128)(2,1)} %bitcast.37, f32[1,1536]{1,0:T(1,128)} %reshape.80.gain_ref, ...), custom_call_target="tpu_custom_call" | custom-call | flops 4831838208 | bytes 23068672 | tf_op jit(solution)/shard_map/project/pallas_call | solution.py:104
  84.6 2.2 collective-permute-start
  86.8 1.3 collective-permute-start.1
  88.1 11.9 %conv_kernel_inner.1 = (f32[512,1536]{1,0:T(8,128)}, bf16[512,1536]{1,0:T(8,128)(2,1)}) custom-call(s32[16]{0:T(128)} %pad_add_fusion.meta, bf16[512,1536]{1,0:T(8,128)(2,1)} %get-tuple-element.16.refs_0_.src, f32[32,1536]{1,0:T(8,128)} %refs_1_.7, f32[1,1536]{1,0:T(1,128)} %reshape.81.refs_2_.gain_ref), custom_call_target="tpu_custom_call" | custom-call | flops 4000000000 | bytes 6291456 | tf_op jit(solution)/shard_map/conv_kernel_inner/pallas_call | solution.py:249
  100.0 0.0 collective-permute-done.refs_3_.low
  100.0 0.0 collective-permute-done.1.refs_4_.high
  100.0 0.0 copy-start.11
  100.0 0.6 copy-done.10
  100.6 0.0 copy-done.11
  100.6 11.9 %conv_kernel_edges.1 = (f32[512,1536]{1,0:T(8,128)}, bf16[512,1536]{1,0:T(8,128)(2,1)}) custom-call(s32[16]{0:T(128)} %pad_add_fusion.meta, bf16[512,1536]{1,0:T(8,128)(2,1)} %get-tuple-element.16.refs_0_.src, f32[32,1536]{1,0:T(8,128)} %refs_1_.7, f32[1,1536]{1,0:T(1,128)} %reshape.81.refs_2_.gain_ref, ...), custom_call_target="tpu_custom_call", output_to_operand_aliasing={{0}: (6, {}), {1}: (7, {})} | custom-call | flops 4000000000 | bytes 6291456 | tf_op jit(solution)/shard_map/conv_kernel_edges/pallas_call | solution.py:249
  112.5 4.2 %convolution_convert_fusion = bf16[1536,768]{1,0:T(8,128)(2,1)} fusion(bf16[512,1536]{1,0:T(8,128)(2,1)} %get-tuple-element.21, bf16[1,1,512,1536]{3,2,1,0:T(8,128)(2,1)S(1)} %copy-done, s32[]{:T(128)S(6)} %select_n.90), kind=kOutput, calls=%fused_computation.2 | convolution fusion | flops 1209139200 | bytes 4718596 | tf_op jit(solution)/shard_map/dot_general | solution.py:500
  116.8 3.3 %collective-permute-start.4 = (bf16[1536,768]{1,0:T(8,128)(2,1)}, bf16[1536,768]{1,0:T(8,128)(2,1)}, u32[]{:S(2)}, u32[]{:S(2)}) collective-permute-start(bf16[1536,768]{1,0:T(8,128)(2,1)} %convolution_convert_fusion), channel_id=1, source_target_pairs={{0,1},{1,0},{2,3},{3,2},{4,5},{5,4},{6,7},{7,6},{8,9},{9,8},{10,11... | collective-permute-start | bytes 7077896 | tf_op jit(solution)/shard_map/ppermute | solution.py:472
  120.1 6.6 %fusion.1.grad_ref = f32[512,1536]{1,0:T(8,128)} fusion(bf16[1536,1536]{1,0:T(8,128)(2,1)} %all-gather.5.cloned.1.call-done, bf16[1,1,512,1536]{3,2,1,0:T(8,128)(2,1)S(1)} %copy-done), kind=kOutput, calls=%fused_computation.5 | convolution fusion | flops 2415919104 | bytes 9437184 | tf_op jit(solution)/shard_map/dot_general | solution.py:579
  126.7 13.1 %grad_conv.1 = (bf16[512,1536]{1,0:T(8,128)(2,1)}, bf16[16,1536]{1,0:T(8,128)(2,1)}, bf16[16,1536]{1,0:T(8,128)(2,1)}) custom-call(s32[16]{0:T(128)} %pad_add_fusion.meta, f32[512,1536]{1,0:T(8,128)} %get-tuple-element.22.conv_ref, f32[512,1536]{1,0:T(8,128)} %fusion.1.grad_ref, f32[1,1536]{1,0:T(1,128)} %reshape.81.refs_2_.gain_ref), custom_call_target="tpu_custom_call" | custom-call | flops 2000000000 | bytes 8388608 | tf_op jit(solution)/shard_map/grad_conv/pallas_call | solution.py:307
  139.8 12.7 %taps_gradient.1 = f32[32,1536]{1,0:T(8,128)} custom-call(s32[16]{0:T(128)} %pad_add_fusion.meta, bf16[512,1536]{1,0:T(8,128)(2,1)} %get-tuple-element.16.refs_0_.src, bf16[512,1536]{1,0:T(8,128)(2,1)} %get-tuple-element.23.refs_0_.grad_ref, bf16[16,1536]{1,0:T(8,128)(2,1)} %copy-done.10, bf16[16,1536]{1,0:T(8,128)(2,1)} %copy-done.11), custom_call_target="tpu_custom_call" | custom-call | flops 8000000000 | bytes 4194304 | tf_op jit(solution)/shard_map/taps_gradient/pallas_call | solution.py:360
  152.6 0.9 broadcast_multiply_fusion.1
  153.5 0.1 collective-permute-start.5
  153.6 4.3 %collective-permute-start.2 = (bf16[16,1536]{1,0:T(8,128)(2,1)S(1)}, bf16[16,1536]{1,0:T(8,128)(2,1)S(1)}, u32[]{:S(2)}, u32[]{:S(2)}) collective-permute-start(bf16[16,1536]{1,0:T(8,128)(2,1)S(1)} %copy-done.7), channel_id=1, source_target_pairs={{0,8},{8,16},{16,24},{24,32},{32,40},{40,48},{48,56},{56,64},{64,7... | collective-permute-start | bytes 147464 | tf_op jit(solution)/shard_map/ppermute | solution.py:468
  158.0 1.3 collective-permute-start.3
  159.3 0.0 collective-permute-done.5
  159.3 2.6 collective-permute-start.7
  161.9 0.9 collective-permute-start.8
  162.8 5.0 %add_convert_fusion = bf16[1536,768]{1,0:T(8,128)(2,1)} fusion(bf16[1536,768]{1,0:T(8,128)(2,1)} %collective-permute-done.4, bf16[512,1536]{1,0:T(8,128)(2,1)} %get-tuple-element.21, bf16[1,1,512,1536]{3,2,1,0:T(8,128)(2,1)S(1)} %copy-done, s32[]{:T(128)S(6)} %select_n.89), kind=kOutput, calls=%fused_computation.1 | convolution fusion | flops 1211498496 | bytes 7077892 | tf_op jit(solution)/shard_map/dot_general | solution.py:500
  167.8 9.1 %all-to-all-start.2 = ((bf16[16,96,768]{2,1,0:T(8,128)(2,1)}), bf16[16,96,768]{2,1,0:T(8,128)(2,1)}, u32[]{:S(2)}, u32[]{:S(2)}) async-start(bf16[16,96,768]{2,1,0:T(8,128)(2,1)} %bitcast.39), calls=%async_computation.2 | async-start | bytes 4718592 | tf_op jit(solution)/shard_map/all_to_all | solution.py:496
  176.8 6.6 %fusion = bf16[1,1,512,1536]{3,2,1,0:T(8,128)(2,1)} fusion(bf16[512,1536]{1,0:T(8,128)(2,1)} %get-tuple-element.21, bf16[1536,1536]{1,0:T(8,128)(2,1)} %all-gather.5.cloned.1.call-done), kind=kOutput, calls=%fused_computation.4 | convolution fusion | flops 2416705536 | bytes 7864320 | tf_op jit(solution)/shard_map/dot_general | solution.py:589
  183.4 2.9 %collective-permute-start.10 = (f32[16,1536]{1,0:T(8,128)S(1)}, f32[16,1536]{1,0:T(8,128)S(1)}, u32[]{:S(2)}, u32[]{:S(2)}) collective-permute-start(f32[16,1536]{1,0:T(8,128)S(1)} %add_add_fusion.2), channel_id=1, source_target_pairs={{0,16},{8,24},{16,0},{24,8},{32,48},{40,56},{48,32},{56,40},{64,80... | collective-permute-start | bytes 294920 | tf_op jit(solution)/shard_map/ppermute | solution.py:472
  186.3 0.9 collective-permute-start.11
  187.2 0.0 collective-permute-start.9
  187.2 9.3 %back_kernel_inner.1.refs_6_ = bf16[512,3072]{1,0:T(8,128)(2,1)} custom-call(s32[16]{0:T(128)} %pad_add_fusion.meta, bf16[512,1536]{1,0:T(8,128)(2,1)} %get-tuple-element.23.refs_0_.grad_ref, f32[32,1536]{1,0:T(8,128)} %refs_1_.7, f32[512,1536]{1,0:T(8,128)} %get-tuple-element.24.refs_2_, f32[512,1536]{1,0:T(8,128)} %get-tuple-element.25.refs_3_), custom_call_target="tpu_custom_call" | custom-call | flops 4000000000 | bytes 6291456 | tf_op jit(solution)/shard_map/back_kernel_inner/pallas_call | solution.py:249
  196.5 13.3 %collective-permute-done.10 = f32[16,1536]{1,0:T(8,128)S(1)} collective-permute-done((f32[16,1536]{1,0:T(8,128)S(1)}, f32[16,1536]{1,0:T(8,128)S(1)}, u32[]{:S(2)}, u32[]{:S(2)}) %collective-permute-start.10) | collective-permute-done | bytes 98336 | tf_op jit(solution)/shard_map/ppermute | solution.py:472
  209.9 0.0 collective-permute-done.11
  209.9 2.9 %collective-permute-start.13 = (f32[16,1536]{1,0:T(8,128)S(1)}, f32[16,1536]{1,0:T(8,128)S(1)}, u32[]{:S(2)}, u32[]{:S(2)}) collective-permute-start(f32[16,1536]{1,0:T(8,128)S(1)} %add_add_fusion.1), channel_id=1, source_target_pairs={{0,64},{8,72},{16,80},{24,88},{32,96},{40,104},{48,112},{56,120},{... | collective-permute-start | bytes 294920 | tf_op jit(solution)/shard_map/ppermute | solution.py:472
  212.8 0.9 collective-permute-start.14
  213.8 0.6 copy-done.8
  214.4 0.6 copy-done.9
  215.0 9.4 %back_kernel_edges.1.grad_ref = bf16[512,3072]{1,0:T(8,128)(2,1)} custom-call(s32[16]{0:T(128)} %pad_add_fusion.meta, bf16[512,1536]{1,0:T(8,128)(2,1)} %get-tuple-element.23.refs_0_.grad_ref, f32[32,1536]{1,0:T(8,128)} %refs_1_.7, f32[512,1536]{1,0:T(8,128)} %get-tuple-element.24.refs_2_, ...), custom_call_target="tpu_custom_call", output_to_operand_aliasing={{}: (7, {})} | custom-call | flops 4000000000 | bytes 6291456 | tf_op jit(solution)/shard_map/back_kernel_edges/pallas_call | solution.py:249
  224.4 0.0 collective-permute-done.14
  224.4 3.9 %collective-permute-start.15 = (f32[16,1536]{1,0:T(8,128)S(1)}, f32[16,1536]{1,0:T(8,128)S(1)}, u32[]{:S(2)}, u32[]{:S(2)}) collective-permute-start(f32[16,1536]{1,0:T(8,128)S(1)} %add_add_fusion), channel_id=1, source_target_pairs={{0,1},{1,0},{2,3},{3,2},{4,5},{5,4},{6,7},{7,6},{8,9},{9,8},{10,11... | collective-permute-start | bytes 294920 | tf_op jit(solution)/shard_map/ppermute | solution.py:472
  228.3 2.0 convert_reduce_fusion
  230.4 0.8 mul.36
  231.2 4.3 %all-to-all-start.3 = ((f32[8,12,768]{2,1,0:T(8,128)}), f32[8,12,768]{2,1,0:T(8,128)S(1)}, u32[]{:S(2)}, u32[]{:S(2)}) async-start(f32[8,12,768]{2,1,0:T(8,128)} %mul.36), calls=%async_computation.3 | async-start | bytes 786432 | tf_op jit(solution)/shard_map/all_to_all | solution.py:496
  235.5 13.7 %input_gradient.1 = bf16[512,1536]{1,0:T(8,128)(2,1)} custom-call(s32[16]{0:T(128)} %pad_add_fusion.meta, bf16[4,128,1536]{2,1,0:T(8,128)(2,1)} %bitcast.38, f32[1,1536]{1,0:T(1,128)} %reshape.80.gain_ref, bf16[512,3072]{1,0:T(8,128)(2,1)} %back_kernel_edges.1.grad_ref, bf16[1536,3072]{1,0:T(8,128)(2,1)} %all-gather.3.cloned.1.call-done.wl_ref.wg_ref.w_ref), custom_call_target="tpu_custom_call" | custom-call | flops 4831838208 | bytes 16777216 | tf_op jit(solution)/shard_map/input_gradient/pallas_call | solution.py:443
  249.2 0.7 maximum_select_fusion
  249.9 0.0 all-to-all-done.3
  249.9 0.6 pad_maximum_fusion
  (53 shorter events, 0.3 us)
Async XLA Ops:
  7.2 105.4 %copy-start = (bf16[1,1,512,1536]{3,2,1,0:T(8,128)(2,1)S(1)}, bf16[1,1,512,1536]{3,2,1,0:T(8,128)(2,1)}, u32[]{:S(2)}) copy-start(bf16[1,1,512,1536]{3,2,1,0:T(8,128)(2,1)} %param.16) | copy-start | bytes 4718596
  7.2 10.2 %copy-start.5 = (s32[1,64]{1,0:T(1,128)S(1)}, s32[1,64]{1,0:T(1,128)}, u32[]{:S(2)}) copy-start(s32[1,64]{1,0:T(1,128)} %param.17) | copy-start | bytes 772
  7.2 10.8 %copy-start.13 = (s32[1,32]{1,0:T(1,128)S(1)}, s32[1,32]{1,0:T(1,128)}, u32[]{:S(2)}) copy-start(s32[1,32]{1,0:T(1,128)} %param.18) | copy-start | bytes 388
  7.2 63.4 %all-gather.3.cloned.1.call-start = ((), (), s32[]{:S(2)}) async-start(), calls=%async_computation.4 | async-start | bytes 10616832 | tf_op jit(solution)/shard_map/all_gather | solution.py:562
  7.9 112.1 %all-gather.5.cloned.1.call-start = ((), (), s32[]{:S(2)}) async-start(), calls=%async_computation.5 | async-start | bytes 5308416 | tf_op jit(solution)/shard_map/all_gather | solution.py:563
  8.7 31.5 %all-to-all-start = ((bf16[16,32,1536]{2,1,0:T(8,128)(2,1)}), bf16[16,32,1536]{2,1,0:T(8,128)(2,1)S(1)}, u32[]{:S(2)}, u32[]{:S(2)}) async-start(bf16[16,32,1536]{2,1,0:T(8,128)(2,1)} %bitcast.40), calls=%async_computation | async-start | bytes 3145728 | tf_op jit(solution)/shard_map/all_to_all | solution.py:496
  40.2 1.1 copy-start.2
  44.6 4.9 %copy-start.3 = (f32[1536]{0:T(1024)S(1)}, f32[1536]{0:T(1024)}, u32[]{:S(2)}) copy-start(f32[1536]{0:T(1024)} %param.11) | copy-start | bytes 18436
  44.6 5.6 %copy-start.4 = (f32[1536]{0:T(1024)S(1)}, f32[1536]{0:T(1024)}, u32[]{:S(2)}) copy-start(f32[1536]{0:T(1024)} %param.14) | copy-start | bytes 18436
  44.6 6.3 %copy-start.12 = (s32[1,32]{1,0:T(1,128)S(1)}, s32[1,32]{1,0:T(1,128)}, u32[]{:S(2)}) copy-start(s32[1,32]{1,0:T(1,128)} %param.19) | copy-start | bytes 388
  44.6 26.0 %all-to-all-start.1 = ((bf16[16,32,1536]{2,1,0:T(8,128)(2,1)}), bf16[16,32,1536]{2,1,0:T(8,128)(2,1)S(1)}, u32[]{:S(2)}, u32[]{:S(2)}) async-start(bf16[16,32,1536]{2,1,0:T(8,128)(2,1)} %reorder.1), calls=%async_computation.1 | async-start | bytes 3145728 | tf_op jit(solution)/shard_map/all_to_all | solution.py:496
  70.6 1.2 copy-start.1
  84.6 15.4 %collective-permute-start = (bf16[16,1536]{1,0:T(8,128)(2,1)}, bf16[16,1536]{1,0:T(8,128)(2,1)S(1)}, u32[]{:S(2)}, u32[]{:S(2)}) collective-permute-start(bf16[16,1536]{1,0:T(8,128)(2,1)} %get-tuple-element.17), channel_id=1, source_target_pairs={{0,8},{8,16},{16,24},{24,32},{32,40},{40,48},{48,56},{56,64},{64,7... | collective-permute-start | bytes 147464 | tf_op jit(solution)/shard_map/ppermute | solution.py:468
  86.8 13.2 %collective-permute-start.1 = (bf16[16,1536]{1,0:T(8,128)(2,1)}, bf16[16,1536]{1,0:T(8,128)(2,1)S(1)}, u32[]{:S(2)}, u32[]{:S(2)}) collective-permute-start(bf16[16,1536]{1,0:T(8,128)(2,1)} %get-tuple-element.18), channel_id=1, source_target_pairs={{8,0},{16,8},{24,16},{32,24},{40,32},{48,40},{56,48},{64,56},{72,6... | collective-permute-start | bytes 147464 | tf_op jit(solution)/shard_map/ppermute | solution.py:468
  100.0 0.6 copy-start.10
  100.0 0.6 copy-start.11
  116.8 46.0 %collective-permute-start.4 = (bf16[1536,768]{1,0:T(8,128)(2,1)}, bf16[1536,768]{1,0:T(8,128)(2,1)}, u32[]{:S(2)}, u32[]{:S(2)}) collective-permute-start(bf16[1536,768]{1,0:T(8,128)(2,1)} %convolution_convert_fusion), channel_id=1, source_target_pairs={{0,1},{1,0},{2,3},{3,2},{4,5},{5,4},{6,7},{7,6},{8,9},{9,8},{10,11... | collective-permute-start | bytes 7077896 | tf_op jit(solution)/shard_map/ppermute | solution.py:472
  139.8 13.8 %copy-start.7 = (bf16[16,1536]{1,0:T(8,128)(2,1)S(1)}, bf16[16,1536]{1,0:T(8,128)(2,1)}, u32[]{:S(2)}) copy-start(bf16[16,1536]{1,0:T(8,128)(2,1)} %get-tuple-element.26) | copy-start | bytes 147460
  139.8 18.2 %copy-start.6 = (bf16[16,1536]{1,0:T(8,128)(2,1)S(1)}, bf16[16,1536]{1,0:T(8,128)(2,1)}, u32[]{:S(2)}) copy-start(bf16[16,1536]{1,0:T(8,128)(2,1)} %get-tuple-element.27) | copy-start | bytes 147460
  153.5 5.7 %collective-permute-start.5 = (f32[16,1536]{1,0:T(8,128)S(1)}, f32[16,1536]{1,0:T(8,128)S(1)}, u32[]{:S(2)}, u32[]{:S(2)}) collective-permute-start(f32[16,1536]{1,0:T(8,128)S(1)} %constant_dynamic-slice_fusion), channel_id=1, source_target_pairs={{0,1},{1,0},{2,3},{3,2},{4,5},{5,4},{6,7},{7,6},{8,9},{9,8},{10,11... | collective-permute-start | bytes 294920 | tf_op jit(solution)/shard_map/ppermute | solution.py:472
  153.6 60.1 %collective-permute-start.2 = (bf16[16,1536]{1,0:T(8,128)(2,1)S(1)}, bf16[16,1536]{1,0:T(8,128)(2,1)S(1)}, u32[]{:S(2)}, u32[]{:S(2)}) collective-permute-start(bf16[16,1536]{1,0:T(8,128)(2,1)S(1)} %copy-done.7), channel_id=1, source_target_pairs={{0,8},{8,16},{16,24},{24,32},{32,40},{40,48},{48,56},{56,64},{64,7... | collective-permute-start | bytes 147464 | tf_op jit(solution)/shard_map/ppermute | solution.py:468
  158.0 55.8 %collective-permute-start.3 = (bf16[16,1536]{1,0:T(8,128)(2,1)S(1)}, bf16[16,1536]{1,0:T(8,128)(2,1)S(1)}, u32[]{:S(2)}, u32[]{:S(2)}) collective-permute-start(bf16[16,1536]{1,0:T(8,128)(2,1)S(1)} %copy-done.6), channel_id=1, source_target_pairs={{8,0},{16,8},{24,16},{32,24},{40,32},{48,40},{56,48},{64,56},{72,6... | collective-permute-start | bytes 147464 | tf_op jit(solution)/shard_map/ppermute | solution.py:468
  159.3 24.1 %collective-permute-start.7 = (f32[16,1536]{1,0:T(8,128)S(1)}, f32[16,1536]{1,0:T(8,128)S(1)}, u32[]{:S(2)}, u32[]{:S(2)}) collective-permute-start(f32[16,1536]{1,0:T(8,128)S(1)} %dynamic-slice_add_fusion), channel_id=1, source_target_pairs={{0,4},{1,5},{2,6},{3,7},{4,0},{5,1},{6,2},{7,3},{8,12},{9,13},{10,... | collective-permute-start | bytes 294920 | tf_op jit(solution)/shard_map/ppermute | solution.py:472
  161.9 21.5 %collective-permute-start.8 = (f32[16,1536]{1,0:T(8,128)S(1)}, f32[16,1536]{1,0:T(8,128)S(1)}, u32[]{:S(2)}, u32[]{:S(2)}) collective-permute-start(f32[16,1536]{1,0:T(8,128)S(1)} %dynamic-slice_add_fusion), channel_id=1, source_target_pairs={{0,6},{1,7},{2,4},{3,5},{4,2},{5,3},{6,0},{7,1},{8,14},{9,15},{10,... | collective-permute-start | bytes 294920 | tf_op jit(solution)/shard_map/ppermute | solution.py:472
  162.8 20.6 %collective-permute-start.6 = (f32[16,1536]{1,0:T(8,128)S(1)}, f32[16,1536]{1,0:T(8,128)S(1)}, u32[]{:S(2)}, u32[]{:S(2)}) collective-permute-start(f32[16,1536]{1,0:T(8,128)S(1)} %dynamic-slice_add_fusion), channel_id=1, source_target_pairs={{0,2},{1,3},{2,0},{3,1},{4,6},{5,7},{6,4},{7,5},{8,10},{9,11},{10,... | collective-permute-start | bytes 294920 | tf_op jit(solution)/shard_map/ppermute | solution.py:472
  167.8 60.6 %all-to-all-start.2 = ((bf16[16,96,768]{2,1,0:T(8,128)(2,1)}), bf16[16,96,768]{2,1,0:T(8,128)(2,1)}, u32[]{:S(2)}, u32[]{:S(2)}) async-start(bf16[16,96,768]{2,1,0:T(8,128)(2,1)} %bitcast.39), calls=%async_computation.2 | async-start | bytes 4718592 | tf_op jit(solution)/shard_map/all_to_all | solution.py:496
  183.4 26.5 %collective-permute-start.10 = (f32[16,1536]{1,0:T(8,128)S(1)}, f32[16,1536]{1,0:T(8,128)S(1)}, u32[]{:S(2)}, u32[]{:S(2)}) collective-permute-start(f32[16,1536]{1,0:T(8,128)S(1)} %add_add_fusion.2), channel_id=1, source_target_pairs={{0,16},{8,24},{16,0},{24,8},{32,48},{40,56},{48,32},{56,40},{64,80... | collective-permute-start | bytes 294920 | tf_op jit(solution)/shard_map/ppermute | solution.py:472
  186.3 23.6 %collective-permute-start.11 = (f32[16,1536]{1,0:T(8,128)S(1)}, f32[16,1536]{1,0:T(8,128)S(1)}, u32[]{:S(2)}, u32[]{:S(2)}) collective-permute-start(f32[16,1536]{1,0:T(8,128)S(1)} %add_add_fusion.2), channel_id=1, source_target_pairs={{0,24},{8,16},{16,8},{24,0},{32,56},{40,48},{48,40},{56,32},{64,88... | collective-permute-start | bytes 294920 | tf_op jit(solution)/shard_map/ppermute | solution.py:472
  187.2 22.7 %collective-permute-start.9 = (f32[16,1536]{1,0:T(8,128)S(1)}, f32[16,1536]{1,0:T(8,128)S(1)}, u32[]{:S(2)}, u32[]{:S(2)}) collective-permute-start(f32[16,1536]{1,0:T(8,128)S(1)} %add_add_fusion.2), channel_id=1, source_target_pairs={{0,8},{8,0},{16,24},{24,16},{32,40},{40,32},{48,56},{56,48},{64,72... | collective-permute-start | bytes 294920 | tf_op jit(solution)/shard_map/ppermute | solution.py:472
  209.9 14.5 %collective-permute-start.13 = (f32[16,1536]{1,0:T(8,128)S(1)}, f32[16,1536]{1,0:T(8,128)S(1)}, u32[]{:S(2)}, u32[]{:S(2)}) collective-permute-start(f32[16,1536]{1,0:T(8,128)S(1)} %add_add_fusion.1), channel_id=1, source_target_pairs={{0,64},{8,72},{16,80},{24,88},{32,96},{40,104},{48,112},{56,120},{... | collective-permute-start | bytes 294920 | tf_op jit(solution)/shard_map/ppermute | solution.py:472
  212.8 11.6 %collective-permute-start.14 = (f32[16,1536]{1,0:T(8,128)S(1)}, f32[16,1536]{1,0:T(8,128)S(1)}, u32[]{:S(2)}, u32[]{:S(2)}) collective-permute-start(f32[16,1536]{1,0:T(8,128)S(1)} %add_add_fusion.1), channel_id=1, source_target_pairs={{0,96},{8,104},{16,112},{24,120},{32,64},{40,72},{48,80},{56,88},{... | collective-permute-start | bytes 294920 | tf_op jit(solution)/shard_map/ppermute | solution.py:472
  213.8 10.6 %collective-permute-start.12 = (f32[16,1536]{1,0:T(8,128)S(1)}, f32[16,1536]{1,0:T(8,128)S(1)}, u32[]{:S(2)}, u32[]{:S(2)}) collective-permute-start(f32[16,1536]{1,0:T(8,128)S(1)} %add_add_fusion.1), channel_id=1, source_target_pairs={{0,32},{8,40},{16,48},{24,56},{32,0},{40,8},{48,16},{56,24},{64,96... | collective-permute-start | bytes 294920 | tf_op jit(solution)/shard_map/ppermute | solution.py:472
  213.8 0.6 copy-start.8
  214.4 0.6 copy-start.9
  224.4 24.8 %collective-permute-start.15 = (f32[16,1536]{1,0:T(8,128)S(1)}, f32[16,1536]{1,0:T(8,128)S(1)}, u32[]{:S(2)}, u32[]{:S(2)}) collective-permute-start(f32[16,1536]{1,0:T(8,128)S(1)} %add_add_fusion), channel_id=1, source_target_pairs={{0,1},{1,0},{2,3},{3,2},{4,5},{5,4},{6,7},{7,6},{8,9},{9,8},{10,11... | collective-permute-start | bytes 294920 | tf_op jit(solution)/shard_map/ppermute | solution.py:472
  231.2 18.7 %all-to-all-start.3 = ((f32[8,12,768]{2,1,0:T(8,128)}), f32[8,12,768]{2,1,0:T(8,128)S(1)}, u32[]{:S(2)}, u32[]{:S(2)}) async-start(f32[8,12,768]{2,1,0:T(8,128)} %mul.36), calls=%async_computation.3 | async-start | bytes 786432 | tf_op jit(solution)/shard_map/all_to_all | solution.py:496
Sparse Core Ops, SparseCore 0:
  9.7 57.7 all-gather.2
  69.2 34.5 all-gather.4

commit v2 on v1

v2 whole, which is shorter than its diff:
```python
import functools
import math

import jax
import jax.numpy as jnp
from jax import lax
from jax.experimental import pallas as pl
from jax.experimental.pallas import tpu as pltpu
from jax.sharding import PartitionSpec as P

BLOCK = 128
LANES = 128
HALF = 16
TAPS = 32
EPS = 1e-05
VMEM = 28 * 2**20
F32 = jnp.float32
BF16 = jnp.bfloat16

LEFT, RIGHT, COUNT, SLOT = 0, 4, 8, 12


def row_mean(values):
    return jnp.mean(values, axis=-1, keepdims=True)


def normalise(values):
    centered = values - row_mean(values)
    inverse = lax.rsqrt(row_mean(centered * centered) + EPS)
    return centered * inverse, inverse


def below(count, rows, first=0):
    return lax.broadcasted_iota(jnp.int32, (rows, 1), 0) + first < count


def in_hbm(x):
    return pltpu.with_memory_space_constraint(x, pltpu.HBM)


def in_vmem(x):
    return pltpu.with_memory_space_constraint(x, pltpu.VMEM)


def params():
    return pltpu.CompilerParams(vmem_limit_bytes=VMEM)


def cost():
    return pl.CostEstimate(flops=1000, bytes_accessed=1000, transcendentals=0)


def whole(shape):
    return pl.BlockSpec(shape, lambda *_: (0,) * len(shape))


def reorder_kernel(order, x_ref, o_ref):
    for t in range(x_ref.shape[0]):
        o_ref[t] = x_ref[order[t]]


def reorder(order, x):
    return pl.pallas_call(
        reorder_kernel,
        out_shape=pltpu.HBM(x.shape, x.dtype),
        grid_spec=pltpu.PrefetchScalarGridSpec(
            num_scalar_prefetch=1,
            grid=(1,),
            in_specs=[whole(x.shape)],
            out_specs=whole(x.shape),
        ),
        compiler_params=params(),
        cost_estimate=cost(),
        name="reorder",
    )(order, in_vmem(x))


def tiles(width):
    return [slice(at, at + LANES) for at in range(0, width, LANES)]


def row_total(parts):
    return jnp.sum(functools.reduce(lambda a, b: a + b, parts), axis=1, keepdims=True)


def row_stats(load, width):
    mean = row_total(load(t) for t in tiles(width)) * (1.0 / width)

    def squared(t):
        centered = load(t) - mean
        return centered * centered

    var = row_total(squared(t) for t in tiles(width)) * (1.0 / width)
    return mean, lax.rsqrt(var + EPS)


def project_kernel(
    meta, x_ref, gain_ref, wl_ref, wg_ref,
    normed_ref, inverse_ref, gate_ref, slope_ref, glu_ref, low_ref, high_ref, hidden,
):
    count, quarter, width = x_ref.shape
    blocks = count * quarter // BLOCK
    quarters = count // blocks

    @pl.when(pl.program_id(0) == 0)
    def _():
        for j in range(blocks):
            rows = slice(j * BLOCK, (j + 1) * BLOCK)
            first = meta[SLOT + j] * quarters

            def load(t, first=first):
                return jnp.concatenate([x_ref[first + q, :, t] for q in range(quarters)]).astype(F32)

            mean, inverse = row_stats(load, width)
            inverse_ref[rows] = inverse
            for t in tiles(width):
                normed = (load(t) - mean) * inverse
                normed_ref[rows, t] = normed.astype(BF16)
                hidden[rows, t] = (normed * gain_ref[:, t]).astype(BF16)

    held = hidden[...]
    lin = jnp.dot(held, wl_ref[...], preferred_element_type=F32)
    gate = jax.nn.sigmoid(jnp.dot(held, wg_ref[...], preferred_element_type=F32))
    product = lin * gate
    gate_ref[...] = gate
    slope_ref[...] = product * (1.0 - gate)
    for j in range(blocks):
        rows = slice(j * BLOCK, (j + 1) * BLOCK)
        glu = jnp.where(below(meta[COUNT + j], BLOCK), product[rows], 0.0).astype(BF16)
        glu_ref[rows] = glu
        if j == 0:
            low_ref[...] = glu[:HALF]
        if j == blocks - 1:
            high_ref[...] = glu[BLOCK - HALF :]


def project(meta, x, gain, weight, tile=512):
    count, quarter, width = x.shape
    rows = count * quarter
    steps = width // tile
    column = pl.BlockSpec((rows, tile), lambda n, _: (0, n))
    edge = pl.BlockSpec((HALF, tile), lambda n, _: (0, n))
    return pl.pallas_call(
        project_kernel,
        out_shape=[
            pltpu.HBM((rows, width), BF16),
            jax.ShapeDtypeStruct((rows, 1), F32),
            pltpu.HBM((rows, width), F32),
            pltpu.HBM((rows, width), F32),
            jax.ShapeDtypeStruct((rows, width), BF16),
            jax.ShapeDtypeStruct((HALF, width), BF16),
            jax.ShapeDtypeStruct((HALF, width), BF16),
        ],
        grid_spec=pltpu.PrefetchScalarGridSpec(
            num_scalar_prefetch=1,
            grid=(steps,),
            in_specs=[
                whole(x.shape),
                whole((1, width)),
                pl.BlockSpec((width, tile), lambda n, _: (0, n)),
                pl.BlockSpec((width, tile), lambda n, _: (0, n + steps)),
            ],
            out_specs=[whole((rows, width)), whole((rows, 1)), column, column, column, edge, edge],
            scratch_shapes=[pltpu.VMEM((rows, width), BF16)],
        ),
        compiler_params=params(),
        cost_estimate=cost(),
        name="project",
    )(meta, in_hbm(x), gain, in_hbm(weight), in_hbm(weight))


def fill(pad, left, middle, right, left_ok, right_ok):
    pad[0:HALF] = jnp.where(left_ok > 0, left.astype(F32), 0.0)
    pad[HALF : HALF + BLOCK] = middle.astype(F32)
    pad[HALF + BLOCK :] = jnp.where(right_ok > 0, right.astype(F32), 0.0)


def fill_inner(pad, meta, b, src):
    at = pl.multiple_of(b * BLOCK, BLOCK)
    fill(
        pad,
        src[pl.ds(pl.multiple_of(at - HALF, HALF), HALF)],
        src[pl.ds(at, BLOCK)],
        src[pl.ds(pl.multiple_of(at + BLOCK, BLOCK), HALF)],
        meta[LEFT + b],
        meta[RIGHT + b],
    )


def fill_first(pad, meta, src, low):
    fill(pad, low[...], src[0:BLOCK], src[BLOCK : BLOCK + HALF], meta[LEFT], meta[RIGHT])


def fill_last(pad, meta, src, high):
    rows = src.shape[0]
    last = rows // BLOCK - 1
    fill(
        pad,
        src[rows - BLOCK - HALF : rows - BLOCK],
        src[rows - BLOCK :],
        high[...],
        meta[LEFT + last],
        meta[RIGHT + last],
    )


def slabs(pad, lanes, first):
    for p in range(8):
        offsets = [o for o in range(first, first + TAPS) if o % 8 == p]
        count = BLOCK + 8 * (offsets[-1] // 8)
        yield pad[pl.ds(p, count), lanes].reshape(count // 8, 8, LANES), offsets


def depthwise(pad, taps, lanes, first, tap_of):
    total = jnp.zeros((BLOCK // 8, 8, LANES), F32)
    for slab, offsets in slabs(pad, lanes, first):
        for o in offsets:
            i = tap_of(o)
            total = total + slab[o // 8 : o // 8 + BLOCK // 8] * taps[i : i + 1, lanes][None]
    return total.reshape(BLOCK, LANES)


def lane_tiles(width):
    return lambda body: pl.loop(0, width // LANES)(
        lambda c: body(pl.ds(pl.multiple_of(c * LANES, LANES), LANES))
    )


def pad_by_step(inner, meta, src, low, high, pad):
    step = pl.program_id(0)
    if inner:
        b = step + 1
        fill_inner(pad, meta, b, src)
        return b

    @pl.when(step == 0)
    def _():
        fill_first(pad, meta, src, low)

    @pl.when(step == 1)
    def _():
        fill_last(pad, meta, src, high)

    return step * (src.shape[0] // BLOCK - 1)


def conv_kernel(inner, meta, *refs):
    if inner:
        src, taps, gain, normed_ref, inverse_ref, slope_ref, swished_ref, pad, conv = refs
        low = high = None
    else:
        src, taps, gain, low, high, _, _, _, _, *refs = refs
        normed_ref, inverse_ref, slope_ref, swished_ref, pad, conv = refs
    width = src.shape[1]
    b = pad_by_step(inner, meta, src, low, high, pad)
    valid = below(meta[COUNT + b], BLOCK)

    @lane_tiles(width)
    def _(lanes):
        conv[:, lanes] = jnp.where(valid, depthwise(pad, taps, lanes, 0, lambda o: o), 0.0)

    mean, inverse = row_stats(lambda t: conv[:, t], width)
    inverse_ref[...] = inverse
    for t in tiles(width):
        normed = (conv[:, t] - mean) * inverse
        scaled = normed * gain[:, t]
        sig = jax.nn.sigmoid(scaled)
        swished = scaled * sig
        normed_ref[:, t] = normed.astype(BF16)
        swished_ref[:, t] = swished.astype(BF16)
        slope_ref[:, t] = (sig + swished * (1.0 - sig)) * gain[:, t]


def split_call(kernel, inner, meta, operands, edges, held, outs, width, flops):
    rows = operands[0].shape[0]
    last = rows // BLOCK - 1

    def place(n, _):
        return (n + 1 if inner else n * last, 0)

    in_specs = []
    for a in operands:
        if a.shape[0] == rows and a is not operands[0]:
            in_specs.append(pl.BlockSpec((BLOCK, a.shape[1]), place))
        else:
            in_specs.append(whole(a.shape))
    args = list(operands)
    aliases = {}
    if not inner:
        args += list(edges)
        in_specs += [whole(e.shape) for e in edges]
        for n, h in enumerate(held):
            aliases[1 + len(args)] = n
            args.append(h)
            in_specs.append(pl.BlockSpec(memory_space=pl.ANY))
    return pl.pallas_call(
        functools.partial(kernel, inner),
        out_shape=[jax.ShapeDtypeStruct(*o) for o in outs],
        grid_spec=pltpu.PrefetchScalarGridSpec(
            num_scalar_prefetch=1,
            grid=(2,),
            in_specs=in_specs,
            out_specs=[pl.BlockSpec((BLOCK, o[0][1]), place) for o in outs],
            scratch_shapes=[
                pltpu.VMEM((BLOCK + 2 * HALF, width), F32),
                pltpu.VMEM((BLOCK, width), F32),
            ],
        ),
        input_output_aliases=aliases,
        compiler_params=params(),
        cost_estimate=cost(),
        name=kernel.__name__ + ("_inner" if inner else "_edges"),
    )(meta, *args)


def conv_forward(inner, meta, glu, taps, gain, edges=(), held=()):
    rows, width = glu.shape
    return split_call(
        conv_kernel,
        inner,
        meta,
        (glu, taps, gain),
        edges,
        held,
        [((rows, width), BF16), ((rows, 1), F32), ((rows, width), F32), ((rows, width), BF16)],
        width,
        4 * 10**9,
    )


def multiply_kernel(x_ref, w_ref, out_ref):
    out_ref[...] = jnp.dot(x_ref[...], w_ref[...], preferred_element_type=F32).astype(BF16)


def multiply(x, weight, tile=512):
    rows, depth = x.shape
    width = weight.shape[1]
    return pl.pallas_call(
        multiply_kernel,
        out_shape=jax.ShapeDtypeStruct((rows, width), BF16),
        grid=(width // tile,),
        in_specs=[whole((rows, depth)), pl.BlockSpec((depth, tile), lambda n: (0, n))],
        out_specs=pl.BlockSpec((rows, tile), lambda n: (0, n)),
        compiler_params=params(),
        cost_estimate=cost(),
        name="multiply",
    )(x, in_hbm(weight))


def norm_back(load, normed_ref, inverse_ref, rows, width):
    normed = {t.start: normed_ref[rows, t].astype(F32) for t in tiles(width)}
    first = row_total(load(t) for t in tiles(width)) * (1.0 / width)
    second = row_total(load(t) * normed[t.start] for t in tiles(width)) * (1.0 / width)
    inverse = inverse_ref[rows]
    for t in tiles(width):
        yield t, (load(t) - first - normed[t.start] * second) * inverse


def grad_conv_kernel(
    meta, normed_ref, inverse_ref, slope_ref, grad_ref, out_ref, low_ref, high_ref
):
    b = pl.program_id(0)
    valid = below(meta[COUNT + b], BLOCK)
    for t, back in norm_back(
        lambda t: grad_ref[:, t] * slope_ref[:, t],
        normed_ref,
        inverse_ref,
        slice(None),
        normed_ref.shape[1],
    ):
        out_ref[:, t] = jnp.where(valid, back, 0.0).astype(BF16)

    @pl.when(b == 0)
    def _():
        low_ref[...] = out_ref[0:HALF]

    @pl.when(b == pl.num_programs(0) - 1)
    def _():
        high_ref[...] = out_ref[BLOCK - HALF :]


def grad_conv_call(meta, normed, inverse, slope, grad_s):
    rows, width = normed.shape
    block = pl.BlockSpec((BLOCK, width), lambda n, _: (n, 0))
    return pl.pallas_call(
        grad_conv_kernel,
        out_shape=[
            jax.ShapeDtypeStruct((rows, width), BF16),
            jax.ShapeDtypeStruct((HALF, width), BF16),
            jax.ShapeDtypeStruct((HALF, width), BF16),
        ],
        grid_spec=pltpu.PrefetchScalarGridSpec(
            num_scalar_prefetch=1,
            grid=(rows // BLOCK,),
            in_specs=[block, pl.BlockSpec((BLOCK, 1), lambda n, _: (n, 0)), block, block],
            out_specs=[block, whole((HALF, width)), whole((HALF, width))],
        ),
        compiler_params=params(),
        cost_estimate=cost(),
        name="grad_conv",
    )(meta, normed, inverse, slope, grad_s)


def pad_by_block(meta, src, low, high, pad):
    b = pl.program_id(0)
    last = pl.num_programs(0) - 1

    @pl.when(b == 0)
    def _():
        fill_first(pad, meta, src, low)

    @pl.when(b == last)
    def _():
        fill_last(pad, meta, src, high)

    @pl.when((b > 0) & (b < last))
    def _():
        fill_inner(pad, meta, b, src)


def taps_kernel(scale, meta, src, grad_ref, low, high, out_ref, pad, total):
    b = pl.program_id(0)
    last = pl.num_programs(0) - 1
    width = src.shape[1]
    pad_by_block(meta, src, low, high, pad)

    @pl.when(b == 0)
    def _():
        total[...] = jnp.zeros_like(total)

    @lane_tiles(width)
    def _(lanes):
        grad = grad_ref[:, lanes].astype(F32).reshape(BLOCK // 8, 8, LANES)
        for slab, offsets in slabs(pad, lanes, 0):
            for o in offsets:
                total[o, :, lanes] += jnp.sum(
                    slab[o // 8 : o // 8 + BLOCK // 8] * grad, axis=0
                )

    @pl.when(b == last)
    def _():
        groups, few = out_ref.shape[0], out_ref.shape[1] // 2
        half = width // 2
        for g in range(groups):
            own = jnp.sum(total[g * few : (g + 1) * few], axis=1) * scale
            out_ref[g, :few] = own[:, :half]
            out_ref[g, few:] = own[:, half:]


def taps_gradient(meta, glu, grad_conv, edges, groups, scale):
    rows, width = glu.shape
    return pl.pallas_call(
        functools.partial(taps_kernel, scale),
        out_shape=jax.ShapeDtypeStruct((groups, 2 * TAPS // groups, width // 2), F32),
        grid_spec=pltpu.PrefetchScalarGridSpec(
            num_scalar_prefetch=1,
            grid=(rows // BLOCK,),
            in_specs=[
                whole(glu.shape),
                pl.BlockSpec((BLOCK, width), lambda n, _: (n, 0)),
                whole((HALF, width)),
                whole((HALF, width)),
            ],
            out_specs=whole((groups, 2 * TAPS // groups, width // 2)),
            scratch_shapes=[
                pltpu.VMEM((BLOCK + 2 * HALF, width), F32),
                pltpu.VMEM((TAPS, 8, width), F32),
            ],
        ),
        compiler_params=params(),
        cost_estimate=cost(),
        name="taps_gradient",
    )(meta, glu, grad_conv, *edges)


def back_kernel(meta, src, taps, gate_ref, slope_ref, low, high, out_ref, pad):
    b = pl.program_id(0)
    width = src.shape[1]
    pad_by_block(meta, src, low, high, pad)
    valid = below(meta[COUNT + b], BLOCK)

    @pl.loop(0, width // LANES)
    def _(c):
        at = pl.multiple_of(c * LANES, LANES)
        lanes = pl.ds(at, LANES)
        grad = jnp.where(valid, depthwise(pad, taps, lanes, 1, lambda o: TAPS - o), 0.0)
        out_ref[:, lanes] = (grad * gate_ref[:, lanes]).astype(BF16)
        out_ref[:, pl.ds(pl.multiple_of(at + width, LANES), LANES)] = (
            grad * slope_ref[:, lanes]
        ).astype(BF16)


def conv_backward(meta, grad_conv, taps, gate, slope, edges):
    rows, width = grad_conv.shape
    block = pl.BlockSpec((BLOCK, width), lambda n, _: (n, 0))
    return pl.pallas_call(
        back_kernel,
        out_shape=pltpu.HBM((rows, 2 * width), BF16),
        grid_spec=pltpu.PrefetchScalarGridSpec(
            num_scalar_prefetch=1,
            grid=(rows // BLOCK,),
            in_specs=[
                whole(grad_conv.shape),
                whole(taps.shape),
                block,
                block,
                whole((HALF, width)),
                whole((HALF, width)),
            ],
            out_specs=pl.BlockSpec((BLOCK, 2 * width), lambda n, _: (n, 0)),
            scratch_shapes=[pltpu.VMEM((BLOCK + 2 * HALF, width), F32)],
        ),
        compiler_params=params(),
        cost_estimate=cost(),
        name="conv_backward",
    )(meta, grad_conv, taps, in_hbm(gate), in_hbm(slope), *edges)


def input_kernel(gain_ref, grad_ref, w_ref, normed_ref, inverse_ref, out_ref, hidden):
    n = pl.program_id(0)
    rows, width = hidden.shape
    tile = w_ref.shape[0]
    at = pl.ds(pl.multiple_of(n * tile, tile), tile)
    hidden[:, at] = gain_ref[:, at] * lax.dot_general(
        grad_ref[...], w_ref[...], (((1,), (1,)), ((), ())), preferred_element_type=F32
    )

    @pl.when(n == pl.num_programs(0) - 1)
    def _():
        for at in range(0, rows, BLOCK):
            part = slice(at, at + BLOCK)
            for t, back in norm_back(
                lambda t, part=part: hidden[part, t], normed_ref, inverse_ref, part, width
            ):
                out_ref[part, t] = back.astype(BF16)


def input_gradient(gain, grad_proj, weight, normed, inverse, tile=512):
    rows = grad_proj.shape[0]
    width = weight.shape[0]
    return pl.pallas_call(
        input_kernel,
        out_shape=jax.ShapeDtypeStruct((rows, width), BF16),
        grid=(width // tile,),
        in_specs=[
            whole((1, width)),
            whole(grad_proj.shape),
            pl.BlockSpec((tile, weight.shape[1]), lambda n: (n, 0)),
            whole(normed.shape),
            whole(inverse.shape),
        ],
        out_specs=whole((rows, width)),
        scratch_shapes=[pltpu.VMEM((rows, width), F32)],
        compiler_params=params(),
        cost_estimate=cost(),
        name="input_gradient",
    )(gain, in_hbm(grad_proj), in_hbm(weight), in_hbm(normed), inverse)


def halves_of_neighbours(low, high):
    count = lax.axis_size("dp")
    forward = [(i, i + 1) for i in range(count - 1)]
    backward = [(i + 1, i) for i in range(count - 1)]
    return lax.ppermute(high, "dp", forward), lax.ppermute(low, "dp", backward)


def swap(values, axis, bits):
    return lax.ppermute(values, axis, [(i, i ^ bits) for i in range(lax.axis_size(axis))])


def sum_of_four(values, axis, low_bit):
    one, two = low_bit, 2 * low_bit
    first, second, third = (swap(values, axis, b) for b in (one, two, one + two))
    return (values + first) + (second + third)


def sum_of_chip(groups, core):
    groups = groups.reshape((groups.shape[0] // 2, 2) + groups.shape[1:])
    other = lax.dynamic_index_in_dim(groups, 1 - core, axis=1, keepdims=False)
    own = lax.dynamic_index_in_dim(groups, core, axis=1, keepdims=False)
    return own + swap(other, "fsdp", 1)


def sum_along_x(groups):
    mine = lax.axis_index("fsdp") // 2
    total = lax.dynamic_index_in_dim(groups, mine, keepdims=False)
    for bits in range(1, groups.shape[0]):
        theirs = lax.dynamic_index_in_dim(groups, mine ^ bits, keepdims=False)
        total = total + swap(theirs, "fsdp", 2 * bits)
    return total


def spread(values, axis):
    return lax.all_to_all(values, axis, split_axis=0, concat_axis=0, tiled=True)


def outer(left, right):
    return lax.dot_general(left, right, (((0,), (0,)), ((), ())), preferred_element_type=F32)


def outer_of_chip(left, right, core):
    half = right.shape[1] // 2
    ours = lax.dynamic_slice_in_dim(right, core * half, half, axis=1)
    theirs = lax.dynamic_slice_in_dim(right, (1 - core) * half, half, axis=1)
    arrived = swap(outer(left, theirs).astype(BF16), "fsdp", 1)
    return (outer(left, ours) + arrived.astype(F32)).astype(BF16)


def send_over_dp(both):
    count = lax.axis_size("dp")
    return spread(both.reshape((count, both.shape[0] // count) + both.shape[1:]), "dp")


def summed_over_dp(sent, scale):
    total = jnp.sum(sent.astype(F32), axis=0) * scale
    count = lax.axis_size("fsdp")
    return total.reshape((count, total.shape[0] // count) + total.shape[1:])


def last_exchange(taps_rows, pieces):
    taps_rows = jnp.broadcast_to(taps_rows[None], pieces.shape[:1] + taps_rows.shape)
    return spread(jnp.concatenate([taps_rows, pieces], axis=1), "fsdp")


def after_exchange(got, few):
    count, _, half = got.shape
    left = got[:, :few].reshape(count * few, half)
    right = got[:, few : 2 * few].reshape(count * few, half)
    pieces = got[:, 2 * few :]
    pieces = jnp.sum(pieces.reshape((count // 2, 2) + pieces.shape[1:]), axis=0)
    return (
        jnp.concatenate([left, right], axis=1),
        jnp.concatenate([pieces[0], pieces[1]], axis=1),
    )


def scalars(packing, counts, tails, place, blocks):
    mine = place * blocks + jnp.arange(blocks, dtype=jnp.int32)
    number = jnp.arange(counts.shape[0], dtype=jnp.int32)
    ends = jnp.sum(jnp.where(number[:, None] <= number[None, :], counts[:, None], 0), axis=0)
    opens = (ends - counts)[None, :] == mine[:, None]
    closes = (ends - 1)[None, :] == mine[:, None]
    left = 1 - jnp.sum(opens.astype(jnp.int32), axis=1)
    right = 1 - jnp.sum(closes.astype(jnp.int32), axis=1)
    valid = BLOCK + jnp.sum(jnp.where(closes, tails[None, :] - BLOCK, 0), axis=1)
    number = jnp.arange(packing.shape[0], dtype=jnp.int32)
    slot = jnp.sum(
        jnp.where(packing[None, :] == mine[:, None], number[None, :] % blocks, 0), axis=1
    )
    return jnp.concatenate([left, right, valid, slot]).astype(jnp.int32)


def target_order(packing, place, blocks):
    count = packing.shape[0] // blocks
    color = place // blocks
    number = jnp.arange(packing.shape[0], dtype=jnp.int32)
    chosen = (number % blocks == color)[None, :]
    goes = (packing // blocks)[None, :] == jnp.arange(count, dtype=jnp.int32)[:, None]
    return jnp.sum(jnp.where(chosen & goes, (number // blocks)[None, :], 0), axis=1)


def local(
    inputs,
    norm_gain,
    weight_in,
    kernel,
    conv_gain,
    weight_out,
    out_grad,
    pack_dest,
    utt_blocks,
    tail_frames,
):
    dp_count = lax.axis_size("dp")
    place = lax.axis_index("dp")
    core = lax.axis_index("fsdp") % 2
    rows, width = inputs.shape[2:]
    blocks = rows // BLOCK
    scale = 1.0 / math.sqrt(rows * lax.axis_size(("dp", "fsdp")))
    full_in = lax.all_gather(weight_in, "fsdp", axis=0, tiled=True)
    full_out = lax.all_gather(weight_out, "fsdp", axis=0, tiled=True)
    meta = scalars(pack_dest[0], utt_blocks[0], tail_frames[0], place, blocks)
    order = target_order(pack_dest[0], place, blocks)
    gain_in = norm_gain.reshape(1, width)
    gain_conv = conv_gain.reshape(1, width)

    quarters = spread(inputs.reshape(dp_count, rows // dp_count, width), "dp")
    arrived = spread(reorder(order, quarters), "dp")

    normed_in, inverse_in, gate, gate_slope, glu, low, high = project(
        meta, arrived, gain_in, full_in
    )
    glu_edges = halves_of_neighbours(low, high)
    held = conv_forward(True, meta, glu, kernel, gain_conv)
    normed, inverse, slope, swished = conv_forward(
        False, meta, glu, kernel, gain_conv, glu_edges, held
    )

    upstream = out_grad[0, 0]
    grad_s = lax.dot_general(
        upstream, full_out, (((1,), (1,)), ((), ())), preferred_element_type=F32
    )
    both = outer_of_chip(swished, upstream, core)
    both, grad_s = lax.optimization_barrier((both, grad_s))
    grad_conv, low, high = grad_conv_call(meta, normed, inverse, slope, grad_s)
    edges = halves_of_neighbours(low, high)
    both, grad_conv, edges = lax.optimization_barrier((both, grad_conv, edges))
    sent = send_over_dp(both)
    fsdp_count = lax.axis_size("fsdp")
    taps_rows = taps_gradient(meta, glu, grad_conv, glu_edges, fsdp_count, scale)
    taps_rows = sum_of_chip(taps_rows, core)
    taps_rows, grad_conv = lax.optimization_barrier((taps_rows, grad_conv))
    grad_proj = conv_backward(meta, grad_conv, kernel, gate, gate_slope, edges)
    taps_rows = sum_along_x(taps_rows)
    taps_rows, grad_proj, swished = lax.optimization_barrier((taps_rows, grad_proj, swished))
    module_out = multiply(swished, full_out)
    taps_rows, sent, module_out = lax.optimization_barrier((taps_rows, sent, module_out))
    pieces = summed_over_dp(sent, scale)
    taps_rows = sum_of_four(taps_rows, "dp", 1)
    taps_rows = sum_of_four(taps_rows, "dp", 4)
    taps_rows, pieces, grad_proj = lax.optimization_barrier((taps_rows, pieces, grad_proj))
    got = last_exchange(taps_rows, pieces)
    kernel_grad, weight_out_grad = after_exchange(got, TAPS // fsdp_count)
    input_grad = input_gradient(gain_in, grad_proj, full_in, normed_in, inverse_in)
    return (
        module_out.reshape(1, 1, rows, width),
        input_grad.reshape(1, 1, rows, width),
        weight_out_grad,
        kernel_grad,
    )


def solution(mesh):
    in_specs = (
        P("dp", "fsdp", None, None),
        P(),
        P("fsdp", None),
        P(),
        P(),
        P("fsdp", None),
        P("dp", "fsdp", None, None),
        P("fsdp", None),
        P("fsdp", None),
        P("fsdp", None),
    )
    out_specs = (
        P("dp", "fsdp", None, None),
        P("dp", "fsdp", None, None),
        P(("dp", "fsdp"), None),
        P(),
    )
    return jax.shard_map(local, mesh=mesh, in_specs=in_specs, out_specs=out_specs, check_vma=False)
```

time: 259 us -> 226 us (0.87)
  Pallas kernels: 98.1 us -> 72.2 us
  matrix products: 22.4 us -> 12.8 us
  local copies, waits for them, and re-layouts: 6.23 us -> 9.92 us
  starting transfers between devices: 54.4 us -> 57.6 us
  waiting for transfers between devices: 55.6 us -> 52.8 us
    pallas_call x4 -> x2, Pallas kernels: 42.5 us -> 13.9 us  [split_call(): pl.pallas_call(functools.partial(kernel, inner), out_shape=[jax.ShapeDtyp...]
    pallas_call x3 -> x5, Pallas kernels: 28.8 us -> 44.6 us  [the longest x1 14.3 us: conv_backward(): pl.pallas_call(back_kernel, out_shape=pltpu.HBM((rows, 2 * width), BF16),...]
    pallas_call x1, Pallas kernels: 13.1 us -> 2.46 us  [grad_conv_call(): pl.pallas_call(grad_conv_kernel, out_shape=[jax.ShapeDtypeStruct((rows, w...]
    ppermute x12 -> x11, waiting for transfers between devices: 13.4 us -> 4.85 us  [swap(): lax.ppermute(values, axis, [(i, i ^ bits) for i in range(lax.axis_size(ax...]
    dot_general x1 -> x0, matrix products: 6.56 us -> none  [local(): jnp.dot(swished, full_out, preferred_element_type=F32).astype(BF16)]
    unnamed x28 -> x60, local copies, waits for them, and re-layouts: 4.19 us -> 9.69 us
    all_to_all x4, starting transfers between devices: 26.9 us -> 32.1 us  [spread(): return lax.all_to_all(values, axis, split_axis=0, concat_axis=0, tiled=True)]
    ppermute x2, waiting for transfers between devices: 0.01 us -> 3.51 us  [halves_of_neighbours(): lax.ppermute(low, 'dp', backward)]
  transfers between devices with their start and end apart: 22 -> 21, of which waited for: 3 -> 7; matrix products, arithmetic and copies ran while one was open for 12% -> 5% of each run, Pallas kernels for 38% -> 31%
where the time goes in v2:
time: 226 us; the launch traced here: 225 us
  Pallas kernels  72.2 us (32%)
  starting transfers between devices  57.6 us (25%)
  waiting for transfers between devices  52.8 us (23%)
  between operations  14.7 us (7%)
  matrix products  12.8 us (6%)
  local copies, waits for them, and re-layouts  9.92 us (4%)
  other arithmetic  5.04 us (2%)
    all_to_all x4, waiting for transfers between devices, spread(): return lax.all_to_all(values, axis, split_axis=0, concat_axis=0, tiled=True)  43 us
    all_to_all x4, starting transfers between devices, spread(): return lax.all_to_all(values, axis, split_axis=0, concat_axis=0, tiled=True)  32.1 us
    ppermute x11, starting transfers between devices, swap(): lax.ppermute(values, axis, [(i, i ^ bits) for i in range(lax.axis_size(ax...  16.5 us
    pallas_call x1, Pallas kernels, conv_backward(): pl.pallas_call(back_kernel, out_shape=pltpu.HBM((rows, 2 * width), BF16),...  14.3 us
    pallas_call x2, Pallas kernels, split_call(): pl.pallas_call(functools.partial(kernel, inner), out_shape=[jax.ShapeDtyp...  13.9 us
    pallas_call x1, Pallas kernels, project(): pl.pallas_call(project_kernel, out_shape=[pltpu.HBM((rows, width), BF16),...  12.5 us
    pallas_call x1, Pallas kernels, input_gradient(): pl.pallas_call(input_kernel, out_shape=jax.ShapeDtypeStruct((rows, width)...  11.3 us
    pallas_call x1, Pallas kernels, taps_gradient(): pl.pallas_call(functools.partial(taps_kernel, scale), out_shape=jax.Shape...  10.3 us
  transfers between devices with their start and end apart: 21, of which 7 were waited for; matrix products, arithmetic and copies ran while one was open for 5% of the time, Pallas kernels for 31%

profile of v2, /device:TPU:1, one launch (start us, length us, event | category | flops | bytes accessed | tf_op | source)
XLA Modules:
  0.0 225.0 jit_solution(5240639903684711908)
XLA Ops:
  7.2 0.0 copy-start
  7.2 0.0 all-gather.3.cloned.1.call-start
  7.2 0.7 all-gather.3.cloned.1.call-update
  7.9 0.0 all-gather.5.cloned.1.call-start
  8.0 0.7 all-gather.5.cloned.1.call-update
  8.7 8.7 %all-to-all-start = ((bf16[16,32,1536]{2,1,0:T(8,128)(2,1)}), bf16[16,32,1536]{2,1,0:T(8,128)(2,1)S(1)}, u32[]{:S(2)}, u32[]{:S(2)}) async-start(bf16[16,32,1536]{2,1,0:T(8,128)(2,1)} %bitcast.54), calls=%async_computation | async-start | bytes 3145728 | tf_op jit(solution)/shard_map/all_to_all | solution.py:594
  17.5 0.1 select_reduce_fusion.1.order
  17.6 0.1 select_reduce_fusion
  17.7 22.6 %all-to-all-done.x_ref = bf16[16,32,1536]{2,1,0:T(8,128)(2,1)S(1)} async-done(((bf16[16,32,1536]{2,1,0:T(8,128)(2,1)}), bf16[16,32,1536]{2,1,0:T(8,128)(2,1)S(1)}, u32[]{:S(2)}, u32[]{:S(2)}) %all-to-all-start) | async-done | bytes 1572896 | tf_op jit(solution)/shard_map/all_to_all | solution.py:594
  40.3 1.8 reorder.1
  42.1 4.8 %all-to-all-start.1 = ((bf16[16,32,1536]{2,1,0:T(8,128)(2,1)}), bf16[16,32,1536]{2,1,0:T(8,128)(2,1)S(1)}, u32[]{:S(2)}, u32[]{:S(2)}) async-start(bf16[16,32,1536]{2,1,0:T(8,128)(2,1)} %reorder.1), calls=%async_computation.1 | async-start | bytes 3145728 | tf_op jit(solution)/shard_map/all_to_all | solution.py:594
  47.0 0.2 select_reduce_fusion.2
  47.2 0.2 fusion.9
  47.4 0.1 pad_add_fusion.meta
  47.5 20.4 %all-to-all-done.1.x_ref = bf16[16,32,1536]{2,1,0:T(8,128)(2,1)S(1)} async-done(((bf16[16,32,1536]{2,1,0:T(8,128)(2,1)}), bf16[16,32,1536]{2,1,0:T(8,128)(2,1)S(1)}, u32[]{:S(2)}, u32[]{:S(2)}) %all-to-all-start.1) | async-done | bytes 1572896 | tf_op jit(solution)/shard_map/all_to_all | solution.py:594
  67.9 1.1 copy-done.24
  69.1 12.5 %project.1 = (bf16[512,1536]{1,0:T(8,128)(2,1)}, f32[512,1]{1,0:T(8,128)S(1)}, f32[512,1536]{1,0:T(8,128)}, f32[512,1536]{1,0:T(8,128)}, bf16[512,1536]{1,0:T(8,...) custom-call(s32[16]{0:T(128)S(1)} %pad_add_fusion.meta, bf16[16,32,1536]{2,1,0:T(8,128)(2,1)} %copy-done.24, ...), custom_call_target="tpu_custom_call" | custom-call | flops 1000 | bytes 1000 | tf_op jit(solution)/shard_map/project/pallas_call | solution.py:143
  81.6 0.7 copy-done.14
  82.3 2.1 collective-permute-start
  84.4 1.3 collective-permute-start.1
  85.7 6.9 %conv_kernel_inner.1 = (bf16[512,1536]{1,0:T(8,128)(2,1)S(1)}, f32[512,1]{1,0:T(8,128)S(1)}, f32[512,1536]{1,0:T(8,128)S(1)}, bf16[512,1536]{1,0:T(8,128)(2,1)S(1)}) custom-call(s32[16]{0:T(128)S(1)} %pad_add_fusion.meta, bf16[512,1536]{1,0:T(8,128)(2,1)S(1)} %get-tuple-element.39.refs_0_.src, f32[32,1536]{1,0:T(8,128)S(1)} %copy-done.11, ...), custom_call_target="tpu_custom_call" | custom-call | flops 1000 | bytes 1000 | tf_op jit(solution)/shard_map/conv_kernel_inner/pallas_call | solution.py:296
  92.7 7.0 %conv_kernel_edges.1 = (bf16[512,1536]{1,0:T(8,128)(2,1)S(1)}, f32[512,1]{1,0:T(8,128)S(1)}, f32[512,1536]{1,0:T(8,128)S(1)}, bf16[512,1536]{1,0:T(8,128)(2,1)S(1)}) custom-call(s32[16]{0:T(128)S(1)} %pad_add_fusion.meta, ...), custom_call_target="tpu_custom_call", output_to_operand_aliasing={{0}: (6, {}), {1}: (7, {}), {2}: (8, {}), {3}: (9, {})} | custom-call | flops 1000 | bytes 1000 | tf_op jit(solution)/shard_map/conv_kernel_edges/pallas_call | solution.py:296
  99.7 0.0 copy-start.3
  99.7 3.4 %convolution_convert_fusion = bf16[1536,768]{1,0:T(8,128)(2,1)} fusion(bf16[512,1536]{1,0:T(8,128)(2,1)S(1)} %get-tuple-element.64.x_ref, bf16[1,1,512,1536]{3,2,1,0:T(8,128)(2,1)S(1)} %copy-done, s32[]{:T(128)S(6)} %select_n.99), kind=kOutput, calls=%fused_computation.2 | convolution fusion | flops 1209139200 | bytes 4718596 | tf_op jit(solution)/shard_map/dot_general | solution.py:598
  103.1 0.0 copy-done.12
  103.1 3.4 %collective-permute-start.2 = (bf16[1536,768]{1,0:T(8,128)(2,1)}, bf16[1536,768]{1,0:T(8,128)(2,1)}, u32[]{:S(2)}, u32[]{:S(2)}) collective-permute-start(bf16[1536,768]{1,0:T(8,128)(2,1)} %convolution_convert_fusion), channel_id=1, source_target_pairs={{0,1},{1,0},{2,3},{3,2},{4,5},{5,4},{6,7},{7,6},{8,9},{9,8},{10,11... | collective-permute-start | bytes 7077896 | tf_op jit(solution)/shard_map/ppermute | solution.py:568
  106.5 4.6 %fusion.grad_ref = f32[512,1536]{1,0:T(8,128)S(1)} fusion(bf16[1536,1536]{1,0:T(8,128)(2,1)} %all-gather.5.cloned.1.call-done.w_ref, bf16[1,1,512,1536]{3,2,1,0:T(8,128)(2,1)S(1)} %copy-done), kind=kOutput, calls=%fused_computation.3 | convolution fusion | flops 2415919104 | bytes 9437184 | tf_op jit(solution)/shard_map/dot_general | solution.py:700
  111.2 4.8 %add_convert_fusion = bf16[1536,768]{1,0:T(8,128)(2,1)} fusion(bf16[1536,768]{1,0:T(8,128)(2,1)} %collective-permute-done.2, bf16[512,1536]{1,0:T(8,128)(2,1)S(1)} %copy-done.6, bf16[1,1,512,1536]{3,2,1,0:T(8,128)(2,1)S(1)} %copy-done, s32[]{:T(128)S(6)} %select_n.98), kind=kOutput, calls=%fused_computation.1 | convolution fusion | flops 1211498496 | bytes 7077892 | tf_op jit(solution)/shard_map/dot_general | solution.py:598
  116.0 2.5 %grad_conv.1 = (bf16[512,1536]{1,0:T(8,128)(2,1)S(1)}, bf16[16,1536]{1,0:T(8,128)(2,1)S(1)}, bf16[16,1536]{1,0:T(8,128)(2,1)S(1)}) custom-call(s32[16]{0:T(128)S(1)} %pad_add_fusion.meta, bf16[512,1536]{1,0:T(8,128)(2,1)S(1)} %copy-done.4, f32[512,1]{1,0:T(8,128)S(1)} %copy-done.13, f32[512,1536]{1,0:T(8,128)S(1)} %copy-done.2, f32[512,1536]{1,0:T(8,128)S(1)} %fusion.grad_ref), custom_call_target="tpu_custom_call" | custom-call | flops 1000 | bytes 1000 | tf_op jit(solution)/shard_map/grad_conv/pallas_call | solution.py:385
  118.5 1.1 copy-done.8
  119.6 4.2 %collective-permute-start.3 = (bf16[16,1536]{1,0:T(8,128)(2,1)S(1)}, bf16[16,1536]{1,0:T(8,128)(2,1)S(1)}, u32[]{:S(2)}, u32[]{:S(2)}) collective-permute-start(bf16[16,1536]{1,0:T(8,128)(2,1)S(1)} %get-tuple-element.53), channel_id=1, source_target_pairs={{0,8},{8,16},{16,24},{24,32},{32,40},{40,48},{48,56},{56,64},{64,7... | collective-permute-start | bytes 147464 | tf_op jit(solution)/shard_map/ppermute | solution.py:564
  123.9 1.3 collective-permute-start.4
  125.2 0.0 copy-start.20
  125.2 3.5 %collective-permute-done.4.high = bf16[16,1536]{1,0:T(8,128)(2,1)S(1)} collective-permute-done((bf16[16,1536]{1,0:T(8,128)(2,1)S(1)}, bf16[16,1536]{1,0:T(8,128)(2,1)S(1)}, u32[]{:S(2)}, u32[]{:S(2)}) %collective-permute-start.4) | collective-permute-done | bytes 49184 | tf_op jit(solution)/shard_map/ppermute | solution.py:564
  128.7 0.6 copy-done.22
  129.3 10.5 %all-to-all-start.2 = ((bf16[16,96,768]{2,1,0:T(8,128)(2,1)}), bf16[16,96,768]{2,1,0:T(8,128)(2,1)}, u32[]{:S(2)}, u32[]{:S(2)}) async-start(bf16[16,96,768]{2,1,0:T(8,128)(2,1)} %bitcast.52), calls=%async_computation.2 | async-start | bytes 4718592 | tf_op jit(solution)/shard_map/all_to_all | solution.py:594
  139.8 0.0 copy-start.9
  139.8 1.4 copy-done.9
  141.2 0.8 copy-done.17
  142.0 0.8 copy-done.19
  142.8 10.3 %taps_gradient.1 = f32[8,8,768]{2,1,0:T(8,128)S(1)} custom-call(s32[16]{0:T(128)S(1)} %pad_add_fusion.meta, bf16[512,1536]{1,0:T(8,128)(2,1)S(1)} %get-tuple-element.39.refs_0_.src, bf16[512,1536]{1,0:T(8,128)(2,1)S(1)} %copy-done.9, bf16[16,1536]{1,0:T(8,128)(2,1)S(1)} %copy-done.17, bf16[16,1536]{1,0:T(8,128)(2,1)S(1)} %copy-done.19), custom_call_target="tpu_custom_call" | custom-call | flops 1000 | bytes 1000 | tf_op jit(solution)/shard_map/taps_gradient/pallas_call | solution.py:452
  153.1 2.0 collective-permute-start.5
  155.1 0.9 collective-permute-done.5
  156.1 2.7 %collective-permute-start.8 = (f32[8,768]{1,0:T(8,128)S(1)}, f32[8,768]{1,0:T(8,128)S(1)}, u32[]{:S(2)}, u32[]{:S(2)}) collective-permute-start(f32[8,768]{1,0:T(8,128)S(1)} %get-tuple-element.82), channel_id=1, source_target_pairs={{0,6},{1,7},{2,4},{3,5},{4,2},{5,3},{6,0},{7,1},{8,14},{9,15},{10,... | collective-permute-start | bytes 73736 | tf_op jit(solution)/shard_map/ppermute | solution.py:568
  158.8 0.2 collective-permute-start.7
  159.0 0.6 collective-permute-start.6
  159.6 1.4 copy-done.10
  161.0 0.8 copy-done.21
  161.8 0.8 copy-done.23
  162.6 14.3 %conv_backward.1.grad_ref = bf16[512,3072]{1,0:T(8,128)(2,1)} custom-call(s32[16]{0:T(128)S(1)} %pad_add_fusion.meta, bf16[512,1536]{1,0:T(8,128)(2,1)S(1)} %copy-done.10, f32[32,1536]{1,0:T(8,128)S(1)} %copy-done.11, f32[512,1536]{1,0:T(8,128)} %get-tuple-element.58.gate_ref, f32[512,1536]{1,0:T(8,128)} %get-tuple-element.59.slope_ref, ...), custom_call_target="tpu_custom_call" | custom-call | flops 1000 | bytes 1000 | tf_op jit(solution)/shard_map/conv_backward/pallas_call | solution.py:496
  177.0 5.8 %multiply.1 = bf16[512,1536]{1,0:T(8,128)(2,1)} custom-call(bf16[512,1536]{1,0:T(8,128)(2,1)S(1)} %copy-done.7, bf16[1536,1536]{1,0:T(8,128)(2,1)} %all-gather.5.cloned.1.call-done.w_ref), custom_call_target="tpu_custom_call" | custom-call | flops 1000 | bytes 1000 | tf_op jit(solution)/shard_map/multiply/pallas_call | solution.py:338
  182.7 3.1 %collective-permute-start.10 = (f32[8,768]{1,0:T(8,128)S(1)}, f32[8,768]{1,0:T(8,128)S(1)}, u32[]{:S(2)}, u32[]{:S(2)}) collective-permute-start(f32[8,768]{1,0:T(8,128)S(1)} %fusion.7), channel_id=1, source_target_pairs={{0,16},{8,24},{16,0},{24,8},{32,48},{40,56},{48,32},{56,40},{64,80... | collective-permute-start | bytes 73736 | tf_op jit(solution)/shard_map/ppermute | solution.py:568
  185.8 0.9 collective-permute-start.11
  186.7 2.0 convert_reduce_fusion
  188.7 1.0 collective-permute-done.11
  189.7 2.8 %collective-permute-start.13 = (f32[8,768]{1,0:T(8,128)S(1)}, f32[8,768]{1,0:T(8,128)S(1)}, u32[]{:S(2)}, u32[]{:S(2)}) collective-permute-start(f32[8,768]{1,0:T(8,128)S(1)} %add_add_fusion.1), channel_id=1, source_target_pairs={{0,64},{8,72},{16,80},{24,88},{32,96},{40,104},{48,112},{56,120},{... | collective-permute-start | bytes 73736 | tf_op jit(solution)/shard_map/ppermute | solution.py:568
  192.5 0.9 collective-permute-start.14
  193.5 0.5 collective-permute-done.13
  194.0 2.4 %collective-permute-done.14 = f32[8,768]{1,0:T(8,128)S(1)} collective-permute-done((f32[8,768]{1,0:T(8,128)S(1)}, f32[8,768]{1,0:T(8,128)S(1)}, u32[]{:S(2)}, u32[]{:S(2)}) %collective-permute-start.14) | collective-permute-done | bytes 24608 | tf_op jit(solution)/shard_map/ppermute | solution.py:568
  196.4 0.9 pad_maximum_fusion
  197.3 8.1 %all-to-all-start.3 = ((f32[8,20,768]{2,1,0:T(8,128)}), f32[8,20,768]{2,1,0:T(8,128)S(1)}, u32[]{:S(2)}, u32[]{:S(2)}) async-start(f32[8,20,768]{2,1,0:T(8,128)} %pad_maximum_fusion), calls=%async_computation.3 | async-start | bytes 1179648 | tf_op jit(solution)/shard_map/all_to_all | solution.py:594
  205.3 11.3 %input_gradient.1 = bf16[512,1536]{1,0:T(8,128)(2,1)} custom-call(f32[1,1536]{1,0:T(1,128)S(1)} %reshape.86.gain_ref, bf16[512,3072]{1,0:T(8,128)(2,1)} %conv_backward.1.grad_ref, bf16[1536,3072]{1,0:T(8,128)(2,1)} %all-gather.3.cloned.1.call-done.wl_ref.wg_ref.w_ref, bf16[512,1536]{1,0:T(8,128)(2,1)} %get-tuple-element.70.normed_ref, f32[512,1]{1,0:T(8,128)S(1)} %copy-done.15), custom_call_target="tpu_custom_call" | custom-call | flops 1000 | bytes 1000 | tf_op jit(solution)/shard_map/input_gradient/pallas_call | solution.py:541
  216.8 0.6 pad_maximum_fusion.2
  217.5 0.7 pad_maximum_fusion.1
  (88 shorter events, 0.5 us)
Async XLA Ops:
  7.2 92.6 %copy-start = (bf16[1,1,512,1536]{3,2,1,0:T(8,128)(2,1)S(1)}, bf16[1,1,512,1536]{3,2,1,0:T(8,128)(2,1)}, u32[]{:S(2)}) copy-start(bf16[1,1,512,1536]{3,2,1,0:T(8,128)(2,1)} %param.16) | copy-start | bytes 4718596
  7.2 61.9 %all-gather.3.cloned.1.call-start = ((), (), s32[]{:S(2)}) async-start(), calls=%async_computation.4 | async-start | bytes 10616832 | tf_op jit(solution)/shard_map/all_gather | solution.py:680
  7.9 98.6 %all-gather.5.cloned.1.call-start = ((), (), s32[]{:S(2)}) async-start(), calls=%async_computation.5 | async-start | bytes 5308416 | tf_op jit(solution)/shard_map/all_gather | solution.py:681
  8.7 8.8 %copy-start.27 = (s32[1,64]{1,0:T(1,128)S(1)}, s32[1,64]{1,0:T(1,128)}, u32[]{:S(2)}) copy-start(s32[1,64]{1,0:T(1,128)} %param.17) | copy-start | bytes 772
  8.7 9.0 %copy-start.29 = (s32[1,32]{1,0:T(1,128)S(1)}, s32[1,32]{1,0:T(1,128)}, u32[]{:S(2)}) copy-start(s32[1,32]{1,0:T(1,128)} %param.18) | copy-start | bytes 388
  8.7 31.6 %all-to-all-start = ((bf16[16,32,1536]{2,1,0:T(8,128)(2,1)}), bf16[16,32,1536]{2,1,0:T(8,128)(2,1)S(1)}, u32[]{:S(2)}, u32[]{:S(2)}) async-start(bf16[16,32,1536]{2,1,0:T(8,128)(2,1)} %bitcast.54), calls=%async_computation | async-start | bytes 3145728 | tf_op jit(solution)/shard_map/all_to_all | solution.py:594
  42.1 4.8 %copy-start.25 = (f32[1536]{0:T(1024)S(1)}, f32[1536]{0:T(1024)}, u32[]{:S(2)}) copy-start(f32[1536]{0:T(1024)} %param.11) | copy-start | bytes 18436
  42.1 5.0 %copy-start.28 = (s32[1,32]{1,0:T(1,128)S(1)}, s32[1,32]{1,0:T(1,128)}, u32[]{:S(2)}) copy-start(s32[1,32]{1,0:T(1,128)} %param.19) | copy-start | bytes 388
  42.1 25.8 %all-to-all-start.1 = ((bf16[16,32,1536]{2,1,0:T(8,128)(2,1)}), bf16[16,32,1536]{2,1,0:T(8,128)(2,1)S(1)}, u32[]{:S(2)}, u32[]{:S(2)}) async-start(bf16[16,32,1536]{2,1,0:T(8,128)(2,1)} %reorder.1), calls=%async_computation.1 | async-start | bytes 3145728 | tf_op jit(solution)/shard_map/all_to_all | solution.py:594
  47.5 38.2 %copy-start.26 = (f32[1536]{0:T(1024)S(1)}, f32[1536]{0:T(1024)}, u32[]{:S(2)}) copy-start(f32[1536]{0:T(1024)} %param.14) | copy-start | bytes 18436
  47.5 38.2 %copy-start.11 = (f32[32,1536]{1,0:T(8,128)S(1)}, f32[32,1536]{1,0:T(8,128)}, u32[]{:S(2)}) copy-start(f32[32,1536]{1,0:T(8,128)} %taps.1) | copy-start | bytes 589828
  67.9 1.1 copy-start.24
  81.6 0.7 copy-start.14
  82.3 10.4 %collective-permute-start = (bf16[16,1536]{1,0:T(8,128)(2,1)}, bf16[16,1536]{1,0:T(8,128)(2,1)S(1)}, u32[]{:S(2)}, u32[]{:S(2)}) collective-permute-start(bf16[16,1536]{1,0:T(8,128)(2,1)} %get-tuple-element.40), channel_id=1, source_target_pairs={{0,8},{8,16},{16,24},{24,32},{32,40},{40,48},{48,56},{56,64},{64,7... | collective-permute-start | bytes 147464 | tf_op jit(solution)/shard_map/ppermute | solution.py:564
  84.4 8.3 %collective-permute-start.1 = (bf16[16,1536]{1,0:T(8,128)(2,1)S(1)}, bf16[16,1536]{1,0:T(8,128)(2,1)S(1)}, u32[]{:S(2)}, u32[]{:S(2)}) collective-permute-start(bf16[16,1536]{1,0:T(8,128)(2,1)S(1)} %get-tuple-element.41), channel_id=1, source_target_pairs={{8,0},{16,8},{24,16},{32,24},{40,32},{48,40},{56,48},{64,56},{72,6... | collective-permute-start | bytes 147464 | tf_op jit(solution)/shard_map/ppermute | solution.py:564
  92.7 7.0 %copy-start.16 = (bf16[16,1536]{1,0:T(8,128)(2,1)}, bf16[16,1536]{1,0:T(8,128)(2,1)S(1)}, u32[]{:S(2)}) copy-start(bf16[16,1536]{1,0:T(8,128)(2,1)S(1)} %collective-permute-done.refs_3_.low) | copy-start | bytes 147460
  92.7 7.0 %copy-start.18 = (bf16[16,1536]{1,0:T(8,128)(2,1)}, bf16[16,1536]{1,0:T(8,128)(2,1)S(1)}, u32[]{:S(2)}) copy-start(bf16[16,1536]{1,0:T(8,128)(2,1)S(1)} %collective-permute-done.1.refs_4_.high) | copy-start | bytes 147460
  99.7 3.4 %copy-start.1 = (f32[512,1536]{1,0:T(8,128)}, f32[512,1536]{1,0:T(8,128)S(1)}, u32[]{:S(2)}) copy-start(f32[512,1536]{1,0:T(8,128)S(1)} %get-tuple-element.50.slope_ref) | copy-start | bytes 9437188
  99.7 3.4 %copy-start.3 = (bf16[512,1536]{1,0:T(8,128)(2,1)}, bf16[512,1536]{1,0:T(8,128)(2,1)S(1)}, u32[]{:S(2)}) copy-start(bf16[512,1536]{1,0:T(8,128)(2,1)S(1)} %get-tuple-element.48.normed_ref) | copy-start | bytes 4718596
  99.7 3.4 %copy-start.5 = (bf16[512,1536]{1,0:T(8,128)(2,1)}, bf16[512,1536]{1,0:T(8,128)(2,1)S(1)}, u32[]{:S(2)}) copy-start(bf16[512,1536]{1,0:T(8,128)(2,1)S(1)} %get-tuple-element.64.x_ref) | copy-start | bytes 4718596
  99.7 3.4 %copy-start.12 = (f32[512,1]{1,0:T(8,128)}, f32[512,1]{1,0:T(8,128)S(1)}, u32[]{:S(2)}) copy-start(f32[512,1]{1,0:T(8,128)S(1)} %get-tuple-element.49.inverse_ref) | copy-start | bytes 6148
  103.1 8.1 %collective-permute-start.2 = (bf16[1536,768]{1,0:T(8,128)(2,1)}, bf16[1536,768]{1,0:T(8,128)(2,1)}, u32[]{:S(2)}, u32[]{:S(2)}) collective-permute-start(bf16[1536,768]{1,0:T(8,128)(2,1)} %convolution_convert_fusion), channel_id=1, source_target_pairs={{0,1},{1,0},{2,3},{3,2},{4,5},{5,4},{6,7},{7,6},{8,9},{9,8},{10,11... | collective-permute-start | bytes 7077896 | tf_op jit(solution)/shard_map/ppermute | solution.py:568
  106.5 4.7 %copy-start.6 = (bf16[512,1536]{1,0:T(8,128)(2,1)S(1)}, bf16[512,1536]{1,0:T(8,128)(2,1)}, u32[]{:S(2)}) copy-start(bf16[512,1536]{1,0:T(8,128)(2,1)} %copy-done.5) | copy-start | bytes 4718596
  111.2 4.8 %copy-start.4 = (bf16[512,1536]{1,0:T(8,128)(2,1)S(1)}, bf16[512,1536]{1,0:T(8,128)(2,1)}, u32[]{:S(2)}) copy-start(bf16[512,1536]{1,0:T(8,128)(2,1)} %copy-done.3) | copy-start | bytes 4718596
  111.2 4.8 %copy-start.13 = (f32[512,1]{1,0:T(8,128)S(1)}, f32[512,1]{1,0:T(8,128)}, u32[]{:S(2)}) copy-start(f32[512,1]{1,0:T(8,128)} %copy-done.12) | copy-start | bytes 6148
  111.2 4.8 %copy-start.2 = (f32[512,1536]{1,0:T(8,128)S(1)}, f32[512,1536]{1,0:T(8,128)}, u32[]{:S(2)}) copy-start(f32[512,1536]{1,0:T(8,128)} %copy-done.1) | copy-start | bytes 9437188
  118.5 1.1 copy-start.8
  119.6 5.6 %collective-permute-start.3 = (bf16[16,1536]{1,0:T(8,128)(2,1)S(1)}, bf16[16,1536]{1,0:T(8,128)(2,1)S(1)}, u32[]{:S(2)}, u32[]{:S(2)}) collective-permute-start(bf16[16,1536]{1,0:T(8,128)(2,1)S(1)} %get-tuple-element.53), channel_id=1, source_target_pairs={{0,8},{8,16},{16,24},{24,32},{32,40},{40,48},{48,56},{56,64},{64,7... | collective-permute-start | bytes 147464 | tf_op jit(solution)/shard_map/ppermute | solution.py:564
  123.9 4.8 %collective-permute-start.4 = (bf16[16,1536]{1,0:T(8,128)(2,1)S(1)}, bf16[16,1536]{1,0:T(8,128)(2,1)S(1)}, u32[]{:S(2)}, u32[]{:S(2)}) collective-permute-start(bf16[16,1536]{1,0:T(8,128)(2,1)S(1)} %get-tuple-element.54), channel_id=1, source_target_pairs={{8,0},{16,8},{24,16},{32,24},{40,32},{48,40},{56,48},{64,56},{72,6... | collective-permute-start | bytes 147464 | tf_op jit(solution)/shard_map/ppermute | solution.py:564
  125.2 3.5 %copy-start.20 = (bf16[16,1536]{1,0:T(8,128)(2,1)}, bf16[16,1536]{1,0:T(8,128)(2,1)S(1)}, u32[]{:S(2)}) copy-start(bf16[16,1536]{1,0:T(8,128)(2,1)S(1)} %collective-permute-done.3.low) | copy-start | bytes 147460
  128.7 0.6 copy-start.22
  129.3 53.4 %all-to-all-start.2 = ((bf16[16,96,768]{2,1,0:T(8,128)(2,1)}), bf16[16,96,768]{2,1,0:T(8,128)(2,1)}, u32[]{:S(2)}, u32[]{:S(2)}) async-start(bf16[16,96,768]{2,1,0:T(8,128)(2,1)} %bitcast.52), calls=%async_computation.2 | async-start | bytes 4718592 | tf_op jit(solution)/shard_map/all_to_all | solution.py:594
  139.8 1.4 copy-start.9
  141.2 0.8 copy-start.17
  142.0 0.8 copy-start.19
  153.1 2.9 %collective-permute-start.5 = (f32[4,8,768]{2,1,0:T(8,128)S(1)}, f32[4,8,768]{2,1,0:T(8,128)S(1)}, u32[]{:S(2)}, u32[]{:S(2)}) collective-permute-start(f32[4,8,768]{2,1,0:T(8,128)S(1)} %dynamic-slice_bitcast_fusion), channel_id=1, source_target_pairs={{0,1},{1,0},{2,3},{3,2},{4,5},{5,4},{6,7},{7,6},{8,9},{9,8},{10,11... | collective-permute-start | bytes 294920 | tf_op jit(solution)/shard_map/ppermute | solution.py:568
  156.1 20.8 %collective-permute-start.8 = (f32[8,768]{1,0:T(8,128)S(1)}, f32[8,768]{1,0:T(8,128)S(1)}, u32[]{:S(2)}, u32[]{:S(2)}) collective-permute-start(f32[8,768]{1,0:T(8,128)S(1)} %get-tuple-element.82), channel_id=1, source_target_pairs={{0,6},{1,7},{2,4},{3,5},{4,2},{5,3},{6,0},{7,1},{8,14},{9,15},{10,... | collective-permute-start | bytes 73736 | tf_op jit(solution)/shard_map/ppermute | solution.py:568
  158.8 18.1 %collective-permute-start.7 = (f32[8,768]{1,0:T(8,128)S(1)}, f32[8,768]{1,0:T(8,128)S(1)}, u32[]{:S(2)}, u32[]{:S(2)}) collective-permute-start(f32[8,768]{1,0:T(8,128)S(1)} %get-tuple-element.83), channel_id=1, source_target_pairs={{0,4},{1,5},{2,6},{3,7},{4,0},{5,1},{6,2},{7,3},{8,12},{9,13},{10,... | collective-permute-start | bytes 73736 | tf_op jit(solution)/shard_map/ppermute | solution.py:568
  159.0 18.0 %collective-permute-start.6 = (f32[8,768]{1,0:T(8,128)S(1)}, f32[8,768]{1,0:T(8,128)S(1)}, u32[]{:S(2)}, u32[]{:S(2)}) collective-permute-start(f32[8,768]{1,0:T(8,128)S(1)} %get-tuple-element.81), channel_id=1, source_target_pairs={{0,2},{1,3},{2,0},{3,1},{4,6},{5,7},{6,4},{7,5},{8,10},{9,11},{10,... | collective-permute-start | bytes 73736 | tf_op jit(solution)/shard_map/ppermute | solution.py:568
  159.6 1.4 copy-start.10
  161.0 0.8 copy-start.21
  161.8 0.8 copy-start.23
  162.6 14.4 %copy-start.7 = (bf16[512,1536]{1,0:T(8,128)(2,1)S(1)}, bf16[512,1536]{1,0:T(8,128)(2,1)}, u32[]{:S(2)}) copy-start(bf16[512,1536]{1,0:T(8,128)(2,1)} %copy-done.5) | copy-start | bytes 4718596
  182.7 6.0 %collective-permute-start.10 = (f32[8,768]{1,0:T(8,128)S(1)}, f32[8,768]{1,0:T(8,128)S(1)}, u32[]{:S(2)}, u32[]{:S(2)}) collective-permute-start(f32[8,768]{1,0:T(8,128)S(1)} %fusion.7), channel_id=1, source_target_pairs={{0,16},{8,24},{16,0},{24,8},{32,48},{40,56},{48,32},{56,40},{64,80... | collective-permute-start | bytes 73736 | tf_op jit(solution)/shard_map/ppermute | solution.py:568
  185.8 3.9 %collective-permute-start.11 = (f32[8,768]{1,0:T(8,128)S(1)}, f32[8,768]{1,0:T(8,128)S(1)}, u32[]{:S(2)}, u32[]{:S(2)}) collective-permute-start(f32[8,768]{1,0:T(8,128)S(1)} %fusion.7), channel_id=1, source_target_pairs={{0,24},{8,16},{16,8},{24,0},{32,56},{40,48},{48,40},{56,32},{64,88... | collective-permute-start | bytes 73736 | tf_op jit(solution)/shard_map/ppermute | solution.py:568
  186.7 3.0 %collective-permute-start.9 = (f32[8,768]{1,0:T(8,128)S(1)}, f32[8,768]{1,0:T(8,128)S(1)}, u32[]{:S(2)}, u32[]{:S(2)}) collective-permute-start(f32[8,768]{1,0:T(8,128)S(1)} %fusion.7), channel_id=1, source_target_pairs={{0,8},{8,0},{16,24},{24,16},{32,40},{40,32},{48,56},{56,48},{64,72... | collective-permute-start | bytes 73736 | tf_op jit(solution)/shard_map/ppermute | solution.py:568
  189.7 4.3 %collective-permute-start.13 = (f32[8,768]{1,0:T(8,128)S(1)}, f32[8,768]{1,0:T(8,128)S(1)}, u32[]{:S(2)}, u32[]{:S(2)}) collective-permute-start(f32[8,768]{1,0:T(8,128)S(1)} %add_add_fusion.1), channel_id=1, source_target_pairs={{0,64},{8,72},{16,80},{24,88},{32,96},{40,104},{48,112},{56,120},{... | collective-permute-start | bytes 73736 | tf_op jit(solution)/shard_map/ppermute | solution.py:568
  192.5 3.9 %collective-permute-start.14 = (f32[8,768]{1,0:T(8,128)S(1)}, f32[8,768]{1,0:T(8,128)S(1)}, u32[]{:S(2)}, u32[]{:S(2)}) collective-permute-start(f32[8,768]{1,0:T(8,128)S(1)} %add_add_fusion.1), channel_id=1, source_target_pairs={{0,96},{8,104},{16,112},{24,120},{32,64},{40,72},{48,80},{56,88},{... | collective-permute-start | bytes 73736 | tf_op jit(solution)/shard_map/ppermute | solution.py:568
  193.4 3.0 %collective-permute-start.12 = (f32[8,768]{1,0:T(8,128)S(1)}, f32[8,768]{1,0:T(8,128)S(1)}, u32[]{:S(2)}, u32[]{:S(2)}) collective-permute-start(f32[8,768]{1,0:T(8,128)S(1)} %add_add_fusion.1), channel_id=1, source_target_pairs={{0,32},{8,40},{16,48},{24,56},{32,0},{40,8},{48,16},{56,24},{64,96... | collective-permute-start | bytes 73736 | tf_op jit(solution)/shard_map/ppermute | solution.py:568
  193.4 11.9 %copy-start.15 = (f32[512,1]{1,0:T(8,128)S(1)}, f32[512,1]{1,0:T(8,128)}, u32[]{:S(2)}) copy-start(f32[512,1]{1,0:T(8,128)} %copy-done.14) | copy-start | bytes 6148
  197.3 19.3 %all-to-all-start.3 = ((f32[8,20,768]{2,1,0:T(8,128)}), f32[8,20,768]{2,1,0:T(8,128)S(1)}, u32[]{:S(2)}, u32[]{:S(2)}) async-start(f32[8,20,768]{2,1,0:T(8,128)} %pad_maximum_fusion), calls=%async_computation.3 | async-start | bytes 1179648 | tf_op jit(solution)/shard_map/all_to_all | solution.py:594
Sparse Core Ops, SparseCore 0:
  9.7 57.7 all-gather.2
  69.1 34.5 all-gather.4

commit v3 on v2

--- a/solution.py
+++ b/solution.py
@@ -144,12 +144,12 @@
         project_kernel,
         out_shape=[
             pltpu.HBM((rows, width), BF16),
-            jax.ShapeDtypeStruct((rows, 1), F32),
+            pltpu.HBM((rows, 1), F32),
             pltpu.HBM((rows, width), F32),
             pltpu.HBM((rows, width), F32),
             jax.ShapeDtypeStruct((rows, width), BF16),
-            jax.ShapeDtypeStruct((HALF, width), BF16),
-            jax.ShapeDtypeStruct((HALF, width), BF16),
+            pltpu.HBM((HALF, width), BF16),
+            pltpu.HBM((HALF, width), BF16),
         ],
         grid_spec=pltpu.PrefetchScalarGridSpec(
             num_scalar_prefetch=1,
@@ -212,12 +212,22 @@
 
 
 def depthwise(pad, taps, lanes, first, tap_of):
-    total = jnp.zeros((BLOCK // 8, 8, LANES), F32)
-    for slab, offsets in slabs(pad, lanes, first):
+    count = BLOCK // 8 + 1
+    padded = pad[:, lanes].reshape(pad.shape[0] // 8, 8, LANES)
+    total = None
+    for p in range(8):
+        offsets = [o for o in range(first, first + TAPS) if o % 8 == p]
+        part = None
         for o in offsets:
             i = tap_of(o)
-            total = total + slab[o // 8 : o // 8 + BLOCK // 8] * taps[i : i + 1, lanes][None]
-    return total.reshape(BLOCK, LANES)
+            rows = count if p else count - 1
+            term = padded[o // 8 : o // 8 + rows] * taps[i : i + 1, lanes][None]
+            part = term if part is None else part + term
+        part = part.reshape(-1, LANES)
+        if p:
+            part = pltpu.roll(part, part.shape[0] - p, 0)[:BLOCK]
+        total = part if total is None else total + part
+    return total
 
 
 def lane_tiles(width):
@@ -287,7 +297,7 @@
     args = list(operands)
     aliases = {}
     if not inner:
-        args += list(edges)
+        args += map(in_hbm, edges)
         in_specs += [whole(e.shape) for e in edges]
         for n, h in enumerate(held):
             aliases[1 + len(args)] = n
@@ -385,9 +395,9 @@
     return pl.pallas_call(
         grad_conv_kernel,
         out_shape=[
-            jax.ShapeDtypeStruct((rows, width), BF16),
-            jax.ShapeDtypeStruct((HALF, width), BF16),
-            jax.ShapeDtypeStruct((HALF, width), BF16),
+            pltpu.HBM((rows, width), BF16),
+            pltpu.HBM((HALF, width), BF16),
+            pltpu.HBM((HALF, width), BF16),
         ],
         grid_spec=pltpu.PrefetchScalarGridSpec(
             num_scalar_prefetch=1,
@@ -470,7 +480,7 @@
         compiler_params=params(),
         cost_estimate=cost(),
         name="taps_gradient",
-    )(meta, glu, grad_conv, *edges)
+    )(meta, glu, in_hbm(grad_conv), *map(in_hbm, edges))
 
 
 def back_kernel(meta, src, taps, gate_ref, slope_ref, low, high, out_ref, pad):
@@ -513,7 +523,7 @@
         compiler_params=params(),
         cost_estimate=cost(),
         name="conv_backward",
-    )(meta, grad_conv, taps, in_hbm(gate), in_hbm(slope), *edges)
+    )(meta, in_hbm(grad_conv), taps, in_hbm(gate), in_hbm(slope), *map(in_hbm, edges))
 
 
 def input_kernel(gain_ref, grad_ref, w_ref, normed_ref, inverse_ref, out_ref, hidden):
@@ -554,7 +564,7 @@
         compiler_params=params(),
         cost_estimate=cost(),
         name="input_gradient",
-    )(gain, in_hbm(grad_proj), in_hbm(weight), in_hbm(normed), inverse)
+    )(gain, in_hbm(grad_proj), in_hbm(weight), in_hbm(normed), in_hbm(inverse))
 
 
 def halves_of_neighbours(low, high):

time: 226 us -> 221 us (0.978)
  local copies, waits for them, and re-layouts: 9.92 us -> 2.09 us
  Pallas kernels: 72.2 us -> 75 us
    unnamed x60 -> x38, local copies, waits for them, and re-layouts: 9.69 us -> 1.86 us
  transfers between devices with their start and end apart: 21 -> 21, of which waited for: 7 -> 7; matrix products, arithmetic and copies ran while one was open for 5% -> 5% of each run, Pallas kernels for 31% -> 32%
where the time goes in v3:
time: 221 us; the launch traced here: 220 us
  Pallas kernels  75 us (34%)
  starting transfers between devices  57.6 us (26%)
  waiting for transfers between devices  53.1 us (24%)
  between operations  14.6 us (7%)
  matrix products  12.7 us (6%)
  other arithmetic  5.03 us (2%)
    all_to_all x4, waiting for transfers between devices, spread(): return lax.all_to_all(values, axis, split_axis=0, concat_axis=0, tiled=True)  43 us
    all_to_all x4, starting transfers between devices, spread(): return lax.all_to_all(values, axis, split_axis=0, concat_axis=0, tiled=True)  31.5 us
    ppermute x11, starting transfers between devices, swap(): lax.ppermute(values, axis, [(i, i ^ bits) for i in range(lax.axis_size(ax...  16.5 us
    pallas_call x2, Pallas kernels, split_call(): pl.pallas_call(functools.partial(kernel, inner), out_shape=[jax.ShapeDtyp...  14.5 us
    pallas_call x1, Pallas kernels, conv_backward(): pl.pallas_call(back_kernel, out_shape=pltpu.HBM((rows, 2 * width), BF16),...  14.4 us
    pallas_call x1, Pallas kernels, project(): pl.pallas_call(project_kernel, out_shape=[pltpu.HBM((rows, width), BF16),...  12.5 us
    pallas_call x1, Pallas kernels, input_gradient(): pl.pallas_call(input_kernel, out_shape=jax.ShapeDtypeStruct((rows, width)...  11.3 us
    pallas_call x1, Pallas kernels, taps_gradient(): pl.pallas_call(functools.partial(taps_kernel, scale), out_shape=jax.Shape...  11.3 us
  transfers between devices with their start and end apart: 21, of which 7 were waited for; matrix products, arithmetic and copies ran while one was open for 5% of the time, Pallas kernels for 32%

profile of v3, /device:TPU:1, one launch (start us, length us, event | category | flops | bytes accessed | tf_op | source)
XLA Modules:
  0.0 220.1 jit_solution(10888016249575836579)
XLA Ops:
  7.2 0.0 copy-start
  7.2 0.0 all-gather.3.cloned.1.call-start
  7.2 0.7 all-gather.3.cloned.1.call-update
  7.9 0.0 all-gather.5.cloned.1.call-start
  8.0 0.7 all-gather.5.cloned.1.call-update
  8.7 8.7 %all-to-all-start = ((bf16[16,32,1536]{2,1,0:T(8,128)(2,1)}), bf16[16,32,1536]{2,1,0:T(8,128)(2,1)S(1)}, u32[]{:S(2)}, u32[]{:S(2)}) async-start(bf16[16,32,1536]{2,1,0:T(8,128)(2,1)} %bitcast.54), calls=%async_computation | async-start | bytes 3145728 | tf_op jit(solution)/shard_map/all_to_all | solution.py:604
  17.5 0.1 select_reduce_fusion.1.order
  17.6 0.1 select_reduce_fusion
  17.7 22.6 %all-to-all-done.x_ref = bf16[16,32,1536]{2,1,0:T(8,128)(2,1)S(1)} async-done(((bf16[16,32,1536]{2,1,0:T(8,128)(2,1)}), bf16[16,32,1536]{2,1,0:T(8,128)(2,1)S(1)}, u32[]{:S(2)}, u32[]{:S(2)}) %all-to-all-start) | async-done | bytes 1572896 | tf_op jit(solution)/shard_map/all_to_all | solution.py:604
  40.3 1.8 reorder.1
  42.1 4.8 %all-to-all-start.1 = ((bf16[16,32,1536]{2,1,0:T(8,128)(2,1)}), bf16[16,32,1536]{2,1,0:T(8,128)(2,1)S(1)}, u32[]{:S(2)}, u32[]{:S(2)}) async-start(bf16[16,32,1536]{2,1,0:T(8,128)(2,1)} %reorder.1), calls=%async_computation.1 | async-start | bytes 3145728 | tf_op jit(solution)/shard_map/all_to_all | solution.py:604
  47.0 0.2 select_reduce_fusion.2
  47.2 0.2 fusion.9
  47.4 0.1 pad_add_fusion.meta
  47.5 20.4 %all-to-all-done.1.x_ref = bf16[16,32,1536]{2,1,0:T(8,128)(2,1)S(1)} async-done(((bf16[16,32,1536]{2,1,0:T(8,128)(2,1)}), bf16[16,32,1536]{2,1,0:T(8,128)(2,1)S(1)}, u32[]{:S(2)}, u32[]{:S(2)}) %all-to-all-start.1) | async-done | bytes 1572896 | tf_op jit(solution)/shard_map/all_to_all | solution.py:604
  67.9 1.1 copy-done.11
  69.1 12.5 %project.1 = (bf16[512,1536]{1,0:T(8,128)(2,1)}, f32[512,1]{1,0:T(8,128)}, f32[512,1536]{1,0:T(8,128)}, f32[512,1536]{1,0:T(8,128)}, bf16[512,1536]{1,0:T(8,128)...) custom-call(s32[16]{0:T(128)S(1)} %pad_add_fusion.meta, bf16[16,32,1536]{2,1,0:T(8,128)(2,1)} %copy-done.11, ...), custom_call_target="tpu_custom_call" | custom-call | flops 1000 | bytes 1000 | tf_op jit(solution)/shard_map/project/pallas_call | solution.py:143
  81.5 2.1 collective-permute-start
  83.7 1.3 collective-permute-start.1
  85.0 6.8 %conv_kernel_inner.1 = (bf16[512,1536]{1,0:T(8,128)(2,1)S(1)}, f32[512,1]{1,0:T(8,128)S(1)}, f32[512,1536]{1,0:T(8,128)S(1)}, bf16[512,1536]{1,0:T(8,128)(2,1)S(1)}) custom-call(s32[16]{0:T(128)S(1)} %pad_add_fusion.meta, bf16[512,1536]{1,0:T(8,128)(2,1)S(1)} %get-tuple-element.39.refs_0_.src, f32[32,1536]{1,0:T(8,128)S(1)} %copy-done.8, ...), custom_call_target="tpu_custom_call" | custom-call | flops 1000 | bytes 1000 | tf_op jit(solution)/shard_map/conv_kernel_inner/pallas_call | solution.py:306
  91.8 0.0 collective-permute-done.refs_3_.low
  91.8 0.0 copy-start.12
  91.9 0.0 copy-start.13
  91.9 0.6 copy-done.12
  92.5 0.0 copy-done.13
  92.5 7.7 %conv_kernel_edges.1 = (bf16[512,1536]{1,0:T(8,128)(2,1)S(1)}, f32[512,1]{1,0:T(8,128)S(1)}, f32[512,1536]{1,0:T(8,128)S(1)}, bf16[512,1536]{1,0:T(8,128)(2,1)S(1)}) custom-call(s32[16]{0:T(128)S(1)} %pad_add_fusion.meta, ...), custom_call_target="tpu_custom_call", output_to_operand_aliasing={{0}: (6, {}), {1}: (7, {}), {2}: (8, {}), {3}: (9, {})} | custom-call | flops 1000 | bytes 1000 | tf_op jit(solution)/shard_map/conv_kernel_edges/pallas_call | solution.py:306
  100.2 0.0 copy-start.3
  100.2 0.0 copy-start.5
  100.2 3.3 %convolution_convert_fusion = bf16[1536,768]{1,0:T(8,128)(2,1)} fusion(bf16[512,1536]{1,0:T(8,128)(2,1)S(1)} %get-tuple-element.64.x_ref, bf16[1,1,512,1536]{3,2,1,0:T(8,128)(2,1)S(1)} %copy-done, s32[]{:T(128)S(6)} %select_n.99), kind=kOutput, calls=%fused_computation.2 | convolution fusion | flops 1209139200 | bytes 4718596 | tf_op jit(solution)/shard_map/dot_general | solution.py:608
  103.6 0.0 copy-done.5
  103.6 0.0 copy-done.9
  103.6 3.4 %collective-permute-start.2 = (bf16[1536,768]{1,0:T(8,128)(2,1)}, bf16[1536,768]{1,0:T(8,128)(2,1)}, u32[]{:S(2)}, u32[]{:S(2)}) collective-permute-start(bf16[1536,768]{1,0:T(8,128)(2,1)} %convolution_convert_fusion), channel_id=1, source_target_pairs={{0,1},{1,0},{2,3},{3,2},{4,5},{5,4},{6,7},{7,6},{8,9},{9,8},{10,11... | collective-permute-start | bytes 7077896 | tf_op jit(solution)/shard_map/ppermute | solution.py:578
  107.0 4.6 %fusion.grad_ref = f32[512,1536]{1,0:T(8,128)S(1)} fusion(bf16[1536,1536]{1,0:T(8,128)(2,1)} %all-gather.5.cloned.1.call-done.w_ref, bf16[1,1,512,1536]{3,2,1,0:T(8,128)(2,1)S(1)} %copy-done), kind=kOutput, calls=%fused_computation.3 | convolution fusion | flops 2415919104 | bytes 9437184 | tf_op jit(solution)/shard_map/dot_general | solution.py:710
  111.6 0.0 copy-start.4
  111.7 4.7 %add_convert_fusion = bf16[1536,768]{1,0:T(8,128)(2,1)} fusion(bf16[1536,768]{1,0:T(8,128)(2,1)} %collective-permute-done.2, bf16[512,1536]{1,0:T(8,128)(2,1)S(1)} %copy-done.6, bf16[1,1,512,1536]{3,2,1,0:T(8,128)(2,1)S(1)} %copy-done, s32[]{:T(128)S(6)} %select_n.98), kind=kOutput, calls=%fused_computation.1 | convolution fusion | flops 1211498496 | bytes 7077892 | tf_op jit(solution)/shard_map/dot_general | solution.py:608
  116.4 3.5 %grad_conv.1 = (bf16[512,1536]{1,0:T(8,128)(2,1)}, bf16[16,1536]{1,0:T(8,128)(2,1)}, bf16[16,1536]{1,0:T(8,128)(2,1)}) custom-call(s32[16]{0:T(128)S(1)} %pad_add_fusion.meta, bf16[512,1536]{1,0:T(8,128)(2,1)S(1)} %copy-done.4, f32[512,1]{1,0:T(8,128)S(1)} %copy-done.10, f32[512,1536]{1,0:T(8,128)S(1)} %copy-done.2, f32[512,1536]{1,0:T(8,128)S(1)} %fusion.grad_ref), custom_call_target="tpu_custom_call" | custom-call | flops 1000 | bytes 1000 | tf_op jit(solution)/shard_map/grad_conv/pallas_call | solution.py:395
  119.9 4.9 %collective-permute-start.3 = (bf16[16,1536]{1,0:T(8,128)(2,1)}, bf16[16,1536]{1,0:T(8,128)(2,1)}, u32[]{:S(2)}, u32[]{:S(2)}) collective-permute-start(bf16[16,1536]{1,0:T(8,128)(2,1)} %get-tuple-element.53), channel_id=1, source_target_pairs={{0,8},{8,16},{16,24},{24,32},{32,40},{40,48},{48,56},{56,64},{64,7... | collective-permute-start | bytes 147464 | tf_op jit(solution)/shard_map/ppermute | solution.py:574
  124.8 1.3 collective-permute-start.4
  126.1 0.0 collective-permute-done.3.low
  126.1 3.8 %collective-permute-done.4.high = bf16[16,1536]{1,0:T(8,128)(2,1)} collective-permute-done((bf16[16,1536]{1,0:T(8,128)(2,1)}, bf16[16,1536]{1,0:T(8,128)(2,1)}, u32[]{:S(2)}, u32[]{:S(2)}) %collective-permute-start.4) | collective-permute-done | bytes 49184 | tf_op jit(solution)/shard_map/ppermute | solution.py:574
  129.9 9.9 %all-to-all-start.2 = ((bf16[16,96,768]{2,1,0:T(8,128)(2,1)}), bf16[16,96,768]{2,1,0:T(8,128)(2,1)}, u32[]{:S(2)}, u32[]{:S(2)}) async-start(bf16[16,96,768]{2,1,0:T(8,128)(2,1)} %bitcast.52), calls=%async_computation.2 | async-start | bytes 4718592 | tf_op jit(solution)/shard_map/all_to_all | solution.py:604
  139.8 11.3 %taps_gradient.1 = f32[8,8,768]{2,1,0:T(8,128)S(1)} custom-call(s32[16]{0:T(128)S(1)} %pad_add_fusion.meta, bf16[512,1536]{1,0:T(8,128)(2,1)S(1)} %get-tuple-element.39.refs_0_.src, bf16[512,1536]{1,0:T(8,128)(2,1)} %get-tuple-element.57.grad_ref.src, bf16[16,1536]{1,0:T(8,128)(2,1)} %copy-done.12, bf16[16,1536]{1,0:T(8,128)(2,1)} %copy-done.13), custom_call_target="tpu_custom_call" | custom-call | flops 1000 | bytes 1000 | tf_op jit(solution)/shard_map/taps_gradient/pallas_call | solution.py:462
  151.2 2.0 collective-permute-start.5
  153.1 0.9 collective-permute-done.5
  154.1 2.7 %collective-permute-start.8 = (f32[8,768]{1,0:T(8,128)S(1)}, f32[8,768]{1,0:T(8,128)S(1)}, u32[]{:S(2)}, u32[]{:S(2)}) collective-permute-start(f32[8,768]{1,0:T(8,128)S(1)} %get-tuple-element.82), channel_id=1, source_target_pairs={{0,6},{1,7},{2,4},{3,5},{4,2},{5,3},{6,0},{7,1},{8,14},{9,15},{10,... | collective-permute-start | bytes 73736 | tf_op jit(solution)/shard_map/ppermute | solution.py:578
  156.8 0.2 collective-permute-start.7
  157.0 0.6 collective-permute-start.6
  157.6 14.4 %conv_backward.1.grad_ref = bf16[512,3072]{1,0:T(8,128)(2,1)} custom-call(s32[16]{0:T(128)S(1)} %pad_add_fusion.meta, bf16[512,1536]{1,0:T(8,128)(2,1)} %get-tuple-element.57.grad_ref.src, f32[32,1536]{1,0:T(8,128)S(1)} %copy-done.8, f32[512,1536]{1,0:T(8,128)} %get-tuple-element.58.gate_ref, f32[512,1536]{1,0:T(8,128)} %get-tuple-element.59.slope_ref, ...), custom_call_target="tpu_custom_call" | custom-call | flops 1000 | bytes 1000 | tf_op jit(solution)/shard_map/conv_backward/pallas_call | solution.py:506
  172.0 0.0 collective-permute-done.8
  172.0 0.0 collective-permute-done.7
  172.1 5.8 %multiply.1 = bf16[512,1536]{1,0:T(8,128)(2,1)} custom-call(bf16[512,1536]{1,0:T(8,128)(2,1)S(1)} %copy-done.7, bf16[1536,1536]{1,0:T(8,128)(2,1)} %all-gather.5.cloned.1.call-done.w_ref), custom_call_target="tpu_custom_call" | custom-call | flops 1000 | bytes 1000 | tf_op jit(solution)/shard_map/multiply/pallas_call | solution.py:348
  177.8 3.1 %collective-permute-start.10 = (f32[8,768]{1,0:T(8,128)S(1)}, f32[8,768]{1,0:T(8,128)S(1)}, u32[]{:S(2)}, u32[]{:S(2)}) collective-permute-start(f32[8,768]{1,0:T(8,128)S(1)} %fusion.7), channel_id=1, source_target_pairs={{0,16},{8,24},{16,0},{24,8},{32,48},{40,56},{48,32},{56,40},{64,80... | collective-permute-start | bytes 73736 | tf_op jit(solution)/shard_map/ppermute | solution.py:578
  180.9 0.9 collective-permute-start.11
  181.8 2.0 convert_reduce_fusion
  183.9 1.0 collective-permute-done.11
  184.8 2.8 %collective-permute-start.13 = (f32[8,768]{1,0:T(8,128)S(1)}, f32[8,768]{1,0:T(8,128)S(1)}, u32[]{:S(2)}, u32[]{:S(2)}) collective-permute-start(f32[8,768]{1,0:T(8,128)S(1)} %add_add_fusion.1), channel_id=1, source_target_pairs={{0,64},{8,72},{16,80},{24,88},{32,96},{40,104},{48,112},{56,120},{... | collective-permute-start | bytes 73736 | tf_op jit(solution)/shard_map/ppermute | solution.py:578
  187.6 0.9 collective-permute-start.14
  188.6 0.5 collective-permute-done.13
  189.1 2.4 %collective-permute-done.14 = f32[8,768]{1,0:T(8,128)S(1)} collective-permute-done((f32[8,768]{1,0:T(8,128)S(1)}, f32[8,768]{1,0:T(8,128)S(1)}, u32[]{:S(2)}, u32[]{:S(2)}) %collective-permute-start.14) | collective-permute-done | bytes 24608 | tf_op jit(solution)/shard_map/ppermute | solution.py:578
  191.5 0.8 pad_maximum_fusion
  192.4 8.1 %all-to-all-start.3 = ((f32[8,20,768]{2,1,0:T(8,128)}), f32[8,20,768]{2,1,0:T(8,128)S(1)}, u32[]{:S(2)}, u32[]{:S(2)}) async-start(f32[8,20,768]{2,1,0:T(8,128)} %pad_maximum_fusion), calls=%async_computation.3 | async-start | bytes 1179648 | tf_op jit(solution)/shard_map/all_to_all | solution.py:604
  200.4 11.3 %input_gradient.1 = bf16[512,1536]{1,0:T(8,128)(2,1)} custom-call(f32[1,1536]{1,0:T(1,128)S(1)} %reshape.86.gain_ref, bf16[512,3072]{1,0:T(8,128)(2,1)} %conv_backward.1.grad_ref, bf16[1536,3072]{1,0:T(8,128)(2,1)} %all-gather.3.cloned.1.call-done.wl_ref.wg_ref.w_ref, bf16[512,1536]{1,0:T(8,128)(2,1)} %get-tuple-element.70.normed_ref, ...), custom_call_target="tpu_custom_call" | custom-call | flops 1000 | bytes 1000 | tf_op jit(solution)/shard_map/input_gradient/pallas_call | solution.py:551
  212.0 0.6 pad_maximum_fusion.2
  212.6 0.7 pad_maximum_fusion.1
  (66 shorter events, 0.5 us)
Async XLA Ops:
  7.2 93.0 %copy-start = (bf16[1,1,512,1536]{3,2,1,0:T(8,128)(2,1)S(1)}, bf16[1,1,512,1536]{3,2,1,0:T(8,128)(2,1)}, u32[]{:S(2)}) copy-start(bf16[1,1,512,1536]{3,2,1,0:T(8,128)(2,1)} %param.16) | copy-start | bytes 4718596
  7.2 61.9 %all-gather.3.cloned.1.call-start = ((), (), s32[]{:S(2)}) async-start(), calls=%async_computation.4 | async-start | bytes 10616832 | tf_op jit(solution)/shard_map/all_gather | solution.py:690
  7.9 99.1 %all-gather.5.cloned.1.call-start = ((), (), s32[]{:S(2)}) async-start(), calls=%async_computation.5 | async-start | bytes 5308416 | tf_op jit(solution)/shard_map/all_gather | solution.py:691
  8.7 8.8 %copy-start.16 = (s32[1,64]{1,0:T(1,128)S(1)}, s32[1,64]{1,0:T(1,128)}, u32[]{:S(2)}) copy-start(s32[1,64]{1,0:T(1,128)} %param.17) | copy-start | bytes 772
  8.7 9.0 %copy-start.18 = (s32[1,32]{1,0:T(1,128)S(1)}, s32[1,32]{1,0:T(1,128)}, u32[]{:S(2)}) copy-start(s32[1,32]{1,0:T(1,128)} %param.18) | copy-start | bytes 388
  8.7 31.6 %all-to-all-start = ((bf16[16,32,1536]{2,1,0:T(8,128)(2,1)}), bf16[16,32,1536]{2,1,0:T(8,128)(2,1)S(1)}, u32[]{:S(2)}, u32[]{:S(2)}) async-start(bf16[16,32,1536]{2,1,0:T(8,128)(2,1)} %bitcast.54), calls=%async_computation | async-start | bytes 3145728 | tf_op jit(solution)/shard_map/all_to_all | solution.py:604
  42.1 4.8 %copy-start.14 = (f32[1536]{0:T(1024)S(1)}, f32[1536]{0:T(1024)}, u32[]{:S(2)}) copy-start(f32[1536]{0:T(1024)} %param.11) | copy-start | bytes 18436
  42.1 5.0 %copy-start.17 = (s32[1,32]{1,0:T(1,128)S(1)}, s32[1,32]{1,0:T(1,128)}, u32[]{:S(2)}) copy-start(s32[1,32]{1,0:T(1,128)} %param.19) | copy-start | bytes 388
  42.1 25.8 %all-to-all-start.1 = ((bf16[16,32,1536]{2,1,0:T(8,128)(2,1)}), bf16[16,32,1536]{2,1,0:T(8,128)(2,1)S(1)}, u32[]{:S(2)}, u32[]{:S(2)}) async-start(bf16[16,32,1536]{2,1,0:T(8,128)(2,1)} %reorder.1), calls=%async_computation.1 | async-start | bytes 3145728 | tf_op jit(solution)/shard_map/all_to_all | solution.py:604
  47.5 37.5 %copy-start.15 = (f32[1536]{0:T(1024)S(1)}, f32[1536]{0:T(1024)}, u32[]{:S(2)}) copy-start(f32[1536]{0:T(1024)} %param.14) | copy-start | bytes 18436
  47.5 37.5 %copy-start.8 = (f32[32,1536]{1,0:T(8,128)S(1)}, f32[32,1536]{1,0:T(8,128)}, u32[]{:S(2)}) copy-start(f32[32,1536]{1,0:T(8,128)} %taps.1) | copy-start | bytes 589828
  67.9 1.1 copy-start.11
  81.5 10.3 %collective-permute-start = (bf16[16,1536]{1,0:T(8,128)(2,1)}, bf16[16,1536]{1,0:T(8,128)(2,1)S(1)}, u32[]{:S(2)}, u32[]{:S(2)}) collective-permute-start(bf16[16,1536]{1,0:T(8,128)(2,1)} %get-tuple-element.40), channel_id=1, source_target_pairs={{0,8},{8,16},{16,24},{24,32},{32,40},{40,48},{48,56},{56,64},{64,7... | collective-permute-start | bytes 147464 | tf_op jit(solution)/shard_map/ppermute | solution.py:574
  83.7 8.2 %collective-permute-start.1 = (bf16[16,1536]{1,0:T(8,128)(2,1)}, bf16[16,1536]{1,0:T(8,128)(2,1)S(1)}, u32[]{:S(2)}, u32[]{:S(2)}) collective-permute-start(bf16[16,1536]{1,0:T(8,128)(2,1)} %get-tuple-element.41), channel_id=1, source_target_pairs={{8,0},{16,8},{24,16},{32,24},{40,32},{48,40},{56,48},{64,56},{72,6... | collective-permute-start | bytes 147464 | tf_op jit(solution)/shard_map/ppermute | solution.py:574
  91.8 0.6 copy-start.12
  91.9 0.6 copy-start.13
  100.2 3.4 %copy-start.1 = (f32[512,1536]{1,0:T(8,128)}, f32[512,1536]{1,0:T(8,128)S(1)}, u32[]{:S(2)}) copy-start(f32[512,1536]{1,0:T(8,128)S(1)} %get-tuple-element.50.slope_ref) | copy-start | bytes 9437188
  100.2 3.4 %copy-start.3 = (bf16[512,1536]{1,0:T(8,128)(2,1)}, bf16[512,1536]{1,0:T(8,128)(2,1)S(1)}, u32[]{:S(2)}) copy-start(bf16[512,1536]{1,0:T(8,128)(2,1)S(1)} %get-tuple-element.48.normed_ref) | copy-start | bytes 4718596
  100.2 3.4 %copy-start.5 = (bf16[512,1536]{1,0:T(8,128)(2,1)}, bf16[512,1536]{1,0:T(8,128)(2,1)S(1)}, u32[]{:S(2)}) copy-start(bf16[512,1536]{1,0:T(8,128)(2,1)S(1)} %get-tuple-element.64.x_ref) | copy-start | bytes 4718596
  100.2 3.4 %copy-start.9 = (f32[512,1]{1,0:T(8,128)}, f32[512,1]{1,0:T(8,128)S(1)}, u32[]{:S(2)}) copy-start(f32[512,1]{1,0:T(8,128)S(1)} %get-tuple-element.49.inverse_ref) | copy-start | bytes 6148
  103.6 8.1 %collective-permute-start.2 = (bf16[1536,768]{1,0:T(8,128)(2,1)}, bf16[1536,768]{1,0:T(8,128)(2,1)}, u32[]{:S(2)}, u32[]{:S(2)}) collective-permute-start(bf16[1536,768]{1,0:T(8,128)(2,1)} %convolution_convert_fusion), channel_id=1, source_target_pairs={{0,1},{1,0},{2,3},{3,2},{4,5},{5,4},{6,7},{7,6},{8,9},{9,8},{10,11... | collective-permute-start | bytes 7077896 | tf_op jit(solution)/shard_map/ppermute | solution.py:578
  107.0 4.7 %copy-start.6 = (bf16[512,1536]{1,0:T(8,128)(2,1)S(1)}, bf16[512,1536]{1,0:T(8,128)(2,1)}, u32[]{:S(2)}) copy-start(bf16[512,1536]{1,0:T(8,128)(2,1)} %copy-done.5) | copy-start | bytes 4718596
  111.6 4.8 %copy-start.4 = (bf16[512,1536]{1,0:T(8,128)(2,1)S(1)}, bf16[512,1536]{1,0:T(8,128)(2,1)}, u32[]{:S(2)}) copy-start(bf16[512,1536]{1,0:T(8,128)(2,1)} %copy-done.3) | copy-start | bytes 4718596
  111.6 4.8 %copy-start.10 = (f32[512,1]{1,0:T(8,128)S(1)}, f32[512,1]{1,0:T(8,128)}, u32[]{:S(2)}) copy-start(f32[512,1]{1,0:T(8,128)} %copy-done.9) | copy-start | bytes 6148
  111.7 4.8 %copy-start.2 = (f32[512,1536]{1,0:T(8,128)S(1)}, f32[512,1536]{1,0:T(8,128)}, u32[]{:S(2)}) copy-start(f32[512,1536]{1,0:T(8,128)} %copy-done.1) | copy-start | bytes 9437188
  119.9 6.2 %collective-permute-start.3 = (bf16[16,1536]{1,0:T(8,128)(2,1)}, bf16[16,1536]{1,0:T(8,128)(2,1)}, u32[]{:S(2)}, u32[]{:S(2)}) collective-permute-start(bf16[16,1536]{1,0:T(8,128)(2,1)} %get-tuple-element.53), channel_id=1, source_target_pairs={{0,8},{8,16},{16,24},{24,32},{32,40},{40,48},{48,56},{56,64},{64,7... | collective-permute-start | bytes 147464 | tf_op jit(solution)/shard_map/ppermute | solution.py:574
  124.8 5.1 %collective-permute-start.4 = (bf16[16,1536]{1,0:T(8,128)(2,1)}, bf16[16,1536]{1,0:T(8,128)(2,1)}, u32[]{:S(2)}, u32[]{:S(2)}) collective-permute-start(bf16[16,1536]{1,0:T(8,128)(2,1)} %get-tuple-element.54), channel_id=1, source_target_pairs={{8,0},{16,8},{24,16},{32,24},{40,32},{48,40},{56,48},{64,56},{72,6... | collective-permute-start | bytes 147464 | tf_op jit(solution)/shard_map/ppermute | solution.py:574
  129.9 47.9 %all-to-all-start.2 = ((bf16[16,96,768]{2,1,0:T(8,128)(2,1)}), bf16[16,96,768]{2,1,0:T(8,128)(2,1)}, u32[]{:S(2)}, u32[]{:S(2)}) async-start(bf16[16,96,768]{2,1,0:T(8,128)(2,1)} %bitcast.52), calls=%async_computation.2 | async-start | bytes 4718592 | tf_op jit(solution)/shard_map/all_to_all | solution.py:604
  151.2 2.9 %collective-permute-start.5 = (f32[4,8,768]{2,1,0:T(8,128)S(1)}, f32[4,8,768]{2,1,0:T(8,128)S(1)}, u32[]{:S(2)}, u32[]{:S(2)}) collective-permute-start(f32[4,8,768]{2,1,0:T(8,128)S(1)} %dynamic-slice_bitcast_fusion), channel_id=1, source_target_pairs={{0,1},{1,0},{2,3},{3,2},{4,5},{5,4},{6,7},{7,6},{8,9},{9,8},{10,11... | collective-permute-start | bytes 294920 | tf_op jit(solution)/shard_map/ppermute | solution.py:578
  154.1 17.9 %collective-permute-start.8 = (f32[8,768]{1,0:T(8,128)S(1)}, f32[8,768]{1,0:T(8,128)S(1)}, u32[]{:S(2)}, u32[]{:S(2)}) collective-permute-start(f32[8,768]{1,0:T(8,128)S(1)} %get-tuple-element.82), channel_id=1, source_target_pairs={{0,6},{1,7},{2,4},{3,5},{4,2},{5,3},{6,0},{7,1},{8,14},{9,15},{10,... | collective-permute-start | bytes 73736 | tf_op jit(solution)/shard_map/ppermute | solution.py:578
  156.8 15.2 %collective-permute-start.7 = (f32[8,768]{1,0:T(8,128)S(1)}, f32[8,768]{1,0:T(8,128)S(1)}, u32[]{:S(2)}, u32[]{:S(2)}) collective-permute-start(f32[8,768]{1,0:T(8,128)S(1)} %get-tuple-element.83), channel_id=1, source_target_pairs={{0,4},{1,5},{2,6},{3,7},{4,0},{5,1},{6,2},{7,3},{8,12},{9,13},{10,... | collective-permute-start | bytes 73736 | tf_op jit(solution)/shard_map/ppermute | solution.py:578
  157.0 15.0 %collective-permute-start.6 = (f32[8,768]{1,0:T(8,128)S(1)}, f32[8,768]{1,0:T(8,128)S(1)}, u32[]{:S(2)}, u32[]{:S(2)}) collective-permute-start(f32[8,768]{1,0:T(8,128)S(1)} %get-tuple-element.81), channel_id=1, source_target_pairs={{0,2},{1,3},{2,0},{3,1},{4,6},{5,7},{6,4},{7,5},{8,10},{9,11},{10,... | collective-permute-start | bytes 73736 | tf_op jit(solution)/shard_map/ppermute | solution.py:578
  157.6 14.4 %copy-start.7 = (bf16[512,1536]{1,0:T(8,128)(2,1)S(1)}, bf16[512,1536]{1,0:T(8,128)(2,1)}, u32[]{:S(2)}) copy-start(bf16[512,1536]{1,0:T(8,128)(2,1)} %copy-done.5) | copy-start | bytes 4718596
  177.8 6.0 %collective-permute-start.10 = (f32[8,768]{1,0:T(8,128)S(1)}, f32[8,768]{1,0:T(8,128)S(1)}, u32[]{:S(2)}, u32[]{:S(2)}) collective-permute-start(f32[8,768]{1,0:T(8,128)S(1)} %fusion.7), channel_id=1, source_target_pairs={{0,16},{8,24},{16,0},{24,8},{32,48},{40,56},{48,32},{56,40},{64,80... | collective-permute-start | bytes 73736 | tf_op jit(solution)/shard_map/ppermute | solution.py:578
  180.9 3.9 %collective-permute-start.11 = (f32[8,768]{1,0:T(8,128)S(1)}, f32[8,768]{1,0:T(8,128)S(1)}, u32[]{:S(2)}, u32[]{:S(2)}) collective-permute-start(f32[8,768]{1,0:T(8,128)S(1)} %fusion.7), channel_id=1, source_target_pairs={{0,24},{8,16},{16,8},{24,0},{32,56},{40,48},{48,40},{56,32},{64,88... | collective-permute-start | bytes 73736 | tf_op jit(solution)/shard_map/ppermute | solution.py:578
  181.8 3.0 %collective-permute-start.9 = (f32[8,768]{1,0:T(8,128)S(1)}, f32[8,768]{1,0:T(8,128)S(1)}, u32[]{:S(2)}, u32[]{:S(2)}) collective-permute-start(f32[8,768]{1,0:T(8,128)S(1)} %fusion.7), channel_id=1, source_target_pairs={{0,8},{8,0},{16,24},{24,16},{32,40},{40,32},{48,56},{56,48},{64,72... | collective-permute-start | bytes 73736 | tf_op jit(solution)/shard_map/ppermute | solution.py:578
  184.8 4.3 %collective-permute-start.13 = (f32[8,768]{1,0:T(8,128)S(1)}, f32[8,768]{1,0:T(8,128)S(1)}, u32[]{:S(2)}, u32[]{:S(2)}) collective-permute-start(f32[8,768]{1,0:T(8,128)S(1)} %add_add_fusion.1), channel_id=1, source_target_pairs={{0,64},{8,72},{16,80},{24,88},{32,96},{40,104},{48,112},{56,120},{... | collective-permute-start | bytes 73736 | tf_op jit(solution)/shard_map/ppermute | solution.py:578
  187.6 3.9 %collective-permute-start.14 = (f32[8,768]{1,0:T(8,128)S(1)}, f32[8,768]{1,0:T(8,128)S(1)}, u32[]{:S(2)}, u32[]{:S(2)}) collective-permute-start(f32[8,768]{1,0:T(8,128)S(1)} %add_add_fusion.1), channel_id=1, source_target_pairs={{0,96},{8,104},{16,112},{24,120},{32,64},{40,72},{48,80},{56,88},{... | collective-permute-start | bytes 73736 | tf_op jit(solution)/shard_map/ppermute | solution.py:578
  188.5 3.0 %collective-permute-start.12 = (f32[8,768]{1,0:T(8,128)S(1)}, f32[8,768]{1,0:T(8,128)S(1)}, u32[]{:S(2)}, u32[]{:S(2)}) collective-permute-start(f32[8,768]{1,0:T(8,128)S(1)} %add_add_fusion.1), channel_id=1, source_target_pairs={{0,32},{8,40},{16,48},{24,56},{32,0},{40,8},{48,16},{56,24},{64,96... | collective-permute-start | bytes 73736 | tf_op jit(solution)/shard_map/ppermute | solution.py:578
  192.4 19.4 %all-to-all-start.3 = ((f32[8,20,768]{2,1,0:T(8,128)}), f32[8,20,768]{2,1,0:T(8,128)S(1)}, u32[]{:S(2)}, u32[]{:S(2)}) async-start(f32[8,20,768]{2,1,0:T(8,128)} %pad_maximum_fusion), calls=%async_computation.3 | async-start | bytes 1179648 | tf_op jit(solution)/shard_map/all_to_all | solution.py:604
Sparse Core Ops, SparseCore 0:
  9.7 57.7 all-gather.2
  69.1 34.5 all-gather.4

commit v4 on v3

--- a/solution.py
+++ b/solution.py
@@ -13,11 +13,10 @@
 HALF = 16
 TAPS = 32
 EPS = 1e-05
-VMEM = 28 * 2**20
 F32 = jnp.float32
 BF16 = jnp.bfloat16
 
-LEFT, RIGHT, COUNT, SLOT = 0, 4, 8, 12
+LEFT, RIGHT, COUNT, SLOT, NEXT = 0, 4, 8, 12, 16
 
 
 def row_mean(values):
@@ -42,8 +41,8 @@
     return pltpu.with_memory_space_constraint(x, pltpu.VMEM)
 
 
-def params():
-    return pltpu.CompilerParams(vmem_limit_bytes=VMEM)
+def params(mib):
+    return pltpu.CompilerParams(vmem_limit_bytes=mib * 2**20)
 
 
 def cost():
@@ -69,7 +68,7 @@
             in_specs=[whole(x.shape)],
             out_specs=whole(x.shape),
         ),
-        compiler_params=params(),
+        compiler_params=params(8),
         cost_estimate=cost(),
         name="reorder",
     )(order, in_vmem(x))
@@ -129,9 +128,9 @@
         glu = jnp.where(below(meta[COUNT + j], BLOCK), product[rows], 0.0).astype(BF16)
         glu_ref[rows] = glu
         if j == 0:
-            low_ref[...] = glu[:HALF]
+            low_ref[...] = glu[: 2 * HALF]
         if j == blocks - 1:
-            high_ref[...] = glu[BLOCK - HALF :]
+            high_ref[...] = glu[BLOCK - 2 * HALF :]
 
 
 def project(meta, x, gain, weight, tile=512):
@@ -139,7 +138,7 @@
     rows = count * quarter
     steps = width // tile
     column = pl.BlockSpec((rows, tile), lambda n, _: (0, n))
-    edge = pl.BlockSpec((HALF, tile), lambda n, _: (0, n))
+    edge = pl.BlockSpec((2 * HALF, tile), lambda n, _: (0, n))
     return pl.pallas_call(
         project_kernel,
         out_shape=[
@@ -148,8 +147,8 @@
             pltpu.HBM((rows, width), F32),
             pltpu.HBM((rows, width), F32),
             jax.ShapeDtypeStruct((rows, width), BF16),
-            pltpu.HBM((HALF, width), BF16),
-            pltpu.HBM((HALF, width), BF16),
+            pltpu.HBM((2 * HALF, width), BF16),
+            pltpu.HBM((2 * HALF, width), BF16),
         ],
         grid_spec=pltpu.PrefetchScalarGridSpec(
             num_scalar_prefetch=1,
@@ -163,7 +162,7 @@
             out_specs=[whole((rows, width)), whole((rows, 1)), column, column, column, edge, edge],
             scratch_shapes=[pltpu.VMEM((rows, width), BF16)],
         ),
-        compiler_params=params(),
+        compiler_params=params(28),
         cost_estimate=cost(),
         name="project",
     )(meta, in_hbm(x), gain, in_hbm(weight), in_hbm(weight))
@@ -188,7 +187,7 @@
 
 
 def fill_first(pad, meta, src, low):
-    fill(pad, low[...], src[0:BLOCK], src[BLOCK : BLOCK + HALF], meta[LEFT], meta[RIGHT])
+    fill(pad, low, src[0:BLOCK], src[BLOCK : BLOCK + HALF], meta[LEFT], meta[RIGHT])
 
 
 def fill_last(pad, meta, src, high):
@@ -198,7 +197,7 @@
         pad,
         src[rows - BLOCK - HALF : rows - BLOCK],
         src[rows - BLOCK :],
-        high[...],
+        high,
         meta[LEFT + last],
         meta[RIGHT + last],
     )
@@ -211,8 +210,8 @@
         yield pad[pl.ds(p, count), lanes].reshape(count // 8, 8, LANES), offsets
 
 
-def depthwise(pad, taps, lanes, first, tap_of):
-    count = BLOCK // 8 + 1
+def depthwise(pad, taps, lanes, first, tap_of, block=BLOCK):
+    count = block // 8 + 1
     padded = pad[:, lanes].reshape(pad.shape[0] // 8, 8, LANES)
     total = None
     for p in range(8):
@@ -225,7 +224,7 @@
             part = term if part is None else part + term
         part = part.reshape(-1, LANES)
         if p:
-            part = pltpu.roll(part, part.shape[0] - p, 0)[:BLOCK]
+            part = pltpu.roll(part, part.shape[0] - p, 0)[:block]
         total = part if total is None else total + part
     return total
 
@@ -236,39 +235,31 @@
     )
 
 
-def pad_by_step(inner, meta, src, low, high, pad):
+def pad_by_step(inner, meta, src, low, high, pad, beyond):
     step = pl.program_id(0)
     if inner:
         b = step + 1
         fill_inner(pad, meta, b, src)
         return b
+    rows = src.shape[0]
 
     @pl.when(step == 0)
     def _():
-        fill_first(pad, meta, src, low)
+        fill_first(pad, meta, src, low[HALF:])
+        beyond[: 2 * HALF] = low[...].astype(F32)
+        beyond[2 * HALF :] = src[:HALF].astype(F32)
 
     @pl.when(step == 1)
     def _():
-        fill_last(pad, meta, src, high)
-
-    return step * (src.shape[0] // BLOCK - 1)
-
-
-def conv_kernel(inner, meta, *refs):
-    if inner:
-        src, taps, gain, normed_ref, inverse_ref, slope_ref, swished_ref, pad, conv = refs
-        low = high = None
-    else:
-        src, taps, gain, low, high, _, _, _, _, *refs = refs
-        normed_ref, inverse_ref, slope_ref, swished_ref, pad, conv = refs
-    width = src.shape[1]
-    b = pad_by_step(inner, meta, src, low, high, pad)
-    valid = below(meta[COUNT + b], BLOCK)
-
-    @lane_tiles(width)
-    def _(lanes):
-        conv[:, lanes] = jnp.where(valid, depthwise(pad, taps, lanes, 0, lambda o: o), 0.0)
-
+        fill_last(pad, meta, src, high[:HALF])
+        beyond[:HALF] = src[rows - HALF :].astype(F32)
+        beyond[HALF:] = high[...].astype(F32)
+
+    return step * (rows // BLOCK - 1)
+
+
+def activate(conv, gain, normed_ref, inverse_ref, slope_ref, swished_ref=None):
+    width = conv.shape[1]
     mean, inverse = row_stats(lambda t: conv[:, t], width)
     inverse_ref[...] = inverse
     for t in tiles(width):
@@ -277,8 +268,32 @@
         sig = jax.nn.sigmoid(scaled)
         swished = scaled * sig
         normed_ref[:, t] = normed.astype(BF16)
-        swished_ref[:, t] = swished.astype(BF16)
         slope_ref[:, t] = (sig + swished * (1.0 - sig)) * gain[:, t]
+        if swished_ref is not None:
+            swished_ref[:, t] = swished.astype(BF16)
+
+
+def conv_kernel(inner, meta, *refs):
+    if inner:
+        src, taps, gain, *outs, pad, conv, beyond, far = refs
+        low = high = None
+    else:
+        src, taps, gain, low, high, _, _, _, _, *outs, pad, conv, beyond, far = refs
+    width = src.shape[1]
+    b = pad_by_step(inner, meta, src, low, high, pad, beyond)
+    valid = below(meta[COUNT + b], BLOCK)
+    far_valid = below(jnp.where(pl.program_id(0) == 0, HALF, meta[NEXT]), HALF)
+
+    @lane_tiles(width)
+    def _(lanes):
+        conv[:, lanes] = jnp.where(valid, depthwise(pad, taps, lanes, 0, lambda o: o), 0.0)
+        if not inner:
+            found = depthwise(beyond, taps, lanes, 0, lambda o: o, HALF)
+            far[:, lanes] = jnp.where(far_valid, found, 0.0)
+
+    activate(conv, gain, *outs[:4])
+    if not inner:
+        activate(far, gain, *outs[4:])
 
 
 def split_call(kernel, inner, meta, operands, edges, held, outs, width, flops):
@@ -301,23 +316,30 @@
         in_specs += [whole(e.shape) for e in edges]
         for n, h in enumerate(held):
             aliases[1 + len(args)] = n
-            args.append(h)
+            args.append(in_hbm(h) if outs[n][2] is pltpu.HBM else h)
             in_specs.append(pl.BlockSpec(memory_space=pl.ANY))
     return pl.pallas_call(
         functools.partial(kernel, inner),
-        out_shape=[jax.ShapeDtypeStruct(*o) for o in outs],
+        out_shape=[o[2](*o[:2]) for o in outs],
         grid_spec=pltpu.PrefetchScalarGridSpec(
             num_scalar_prefetch=1,
             grid=(2,),
             in_specs=in_specs,
-            out_specs=[pl.BlockSpec((BLOCK, o[0][1]), place) for o in outs],
+            out_specs=[
+                pl.BlockSpec((BLOCK, o[0][1]), place)
+                if o[0][0] == rows
+                else pl.BlockSpec((HALF, o[0][1]), lambda n, _: (n, 0))
+                for o in outs
+            ],
             scratch_shapes=[
                 pltpu.VMEM((BLOCK + 2 * HALF, width), F32),
                 pltpu.VMEM((BLOCK, width), F32),
+                pltpu.VMEM((3 * HALF, width), F32),
+                pltpu.VMEM((HALF, width), F32),
             ],
         ),
         input_output_aliases=aliases,
-        compiler_params=params(),
+        compiler_params=params(16),
         cost_estimate=cost(),
         name=kernel.__name__ + ("_inner" if inner else "_edges"),
     )(meta, *args)
@@ -325,6 +347,14 @@
 
 def conv_forward(inner, meta, glu, taps, gain, edges=(), held=()):
     rows, width = glu.shape
+    outs = [
+        ((rows, width), BF16, pltpu.HBM),
+        ((rows, 1), F32, pltpu.HBM),
+        ((rows, width), F32, pltpu.HBM),
+        ((rows, width), BF16, jax.ShapeDtypeStruct),
+    ]
+    if not inner:
+        outs += [((2 * HALF, o[0][1]), *o[1:]) for o in outs[:3]]
     return split_call(
         conv_kernel,
         inner,
@@ -332,7 +362,7 @@
         (glu, taps, gain),
         edges,
         held,
-        [((rows, width), BF16), ((rows, 1), F32), ((rows, width), F32), ((rows, width), BF16)],
+        outs,
         width,
         4 * 10**9,
     )
@@ -351,64 +381,91 @@
         grid=(width // tile,),
         in_specs=[whole((rows, depth)), pl.BlockSpec((depth, tile), lambda n: (0, n))],
         out_specs=pl.BlockSpec((rows, tile), lambda n: (0, n)),
-        compiler_params=params(),
+        compiler_params=params(12),
         cost_estimate=cost(),
         name="multiply",
     )(x, in_hbm(weight))
 
 
-def norm_back(load, normed_ref, inverse_ref, rows, width):
+def norm_back(load, normed_ref, inverse_ref, rows, width, first=None):
     normed = {t.start: normed_ref[rows, t].astype(F32) for t in tiles(width)}
-    first = row_total(load(t) for t in tiles(width)) * (1.0 / width)
+    mean = row_total(load(t) for t in tiles(width)) * (1.0 / width)
     second = row_total(load(t) * normed[t.start] for t in tiles(width)) * (1.0 / width)
+    if first is not None:
+        rows = slice(first, first + rows.stop - rows.start)
     inverse = inverse_ref[rows]
     for t in tiles(width):
-        yield t, (load(t) - first - normed[t.start] * second) * inverse
+        yield t, (load(t) - mean - normed[t.start] * second) * inverse
 
 
 def grad_conv_kernel(
-    meta, normed_ref, inverse_ref, slope_ref, grad_ref, out_ref, low_ref, high_ref
+    meta, grad_ref, w_ref, normed_ref, slope_ref, far_normed, far_slope, inverse_ref, far_inverse,
+    out_ref, far_ref, incoming, normed,
 ):
-    b = pl.program_id(0)
-    valid = below(meta[COUNT + b], BLOCK)
-    for t, back in norm_back(
-        lambda t: grad_ref[:, t] * slope_ref[:, t],
-        normed_ref,
-        inverse_ref,
-        slice(None),
-        normed_ref.shape[1],
-    ):
-        out_ref[:, t] = jnp.where(valid, back, 0.0).astype(BF16)
-
-    @pl.when(b == 0)
-    def _():
-        low_ref[...] = out_ref[0:HALF]
-
-    @pl.when(b == pl.num_programs(0) - 1)
-    def _():
-        high_ref[...] = out_ref[BLOCK - HALF :]
-
-
-def grad_conv_call(meta, normed, inverse, slope, grad_s):
+    n = pl.program_id(0)
+    rows, width = out_ref.shape
+    tile = w_ref.shape[0]
+    at = pl.ds(pl.multiple_of(n * tile, tile), tile)
+    grad_s = lax.dot_general(
+        grad_ref[...], w_ref[...], (((1,), (1,)), ((), ())), preferred_element_type=F32
+    )
+    incoming[:rows, at] = grad_s[:rows] * slope_ref[...]
+    incoming[rows:, at] = grad_s[rows:] * far_slope[...]
+    normed[:rows, at] = normed_ref[...]
+    normed[rows:, at] = far_normed[...]
+
+    def finish(ref, part, first, inverse, valid):
+        count = part.stop - part.start
+        for t, back in norm_back(
+            lambda t: incoming[part, t], normed, inverse, part, width, first
+        ):
+            ref[first : first + count, t] = jnp.where(valid, back, 0.0).astype(BF16)
+
+    @pl.when(n == pl.num_programs(0) - 1)
+    def _():
+        for b in range(rows // BLOCK):
+            part = slice(b * BLOCK, (b + 1) * BLOCK)
+            finish(out_ref, part, b * BLOCK, inverse_ref, below(meta[COUNT + b], BLOCK))
+        part = slice(rows, rows + 2 * HALF)
+        finish(far_ref, part, 0, far_inverse, below(HALF + meta[NEXT], 2 * HALF))
+
+
+def grad_conv_call(meta, around, weight, normed, inverse, slope, far, tile=512):
     rows, width = normed.shape
-    block = pl.BlockSpec((BLOCK, width), lambda n, _: (n, 0))
+    far_normed, far_inverse, far_slope = far
+    column = pl.BlockSpec((rows, tile), lambda n, _: (0, n))
+    beyond = pl.BlockSpec((2 * HALF, tile), lambda n, _: (0, n))
     return pl.pallas_call(
         grad_conv_kernel,
-        out_shape=[
-            pltpu.HBM((rows, width), BF16),
-            pltpu.HBM((HALF, width), BF16),
-            pltpu.HBM((HALF, width), BF16),
-        ],
+        out_shape=[pltpu.HBM((rows, width), BF16), pltpu.HBM((2 * HALF, width), BF16)],
         grid_spec=pltpu.PrefetchScalarGridSpec(
             num_scalar_prefetch=1,
-            grid=(rows // BLOCK,),
-            in_specs=[block, pl.BlockSpec((BLOCK, 1), lambda n, _: (n, 0)), block, block],
-            out_specs=[block, whole((HALF, width)), whole((HALF, width))],
+            grid=(width // tile,),
+            in_specs=[
+                whole(around.shape),
+                pl.BlockSpec((tile, width), lambda n, _: (n, 0)),
+                column,
+                column,
+                beyond,
+                beyond,
+                whole(inverse.shape),
+                whole(far_inverse.shape),
+            ],
+            out_specs=[whole((rows, width)), whole((2 * HALF, width))],
+            scratch_shapes=[
+                pltpu.VMEM((rows + 2 * HALF, width), F32),
+                pltpu.VMEM((rows + 2 * HALF, width), BF16),
+            ],
         ),
-        compiler_params=params(),
+        compiler_params=params(28),
         cost_estimate=cost(),
         name="grad_conv",
-    )(meta, normed, inverse, slope, grad_s)
+    )(
+        meta,
+        around,
+        in_hbm(weight),
+        *map(in_hbm, (normed, slope, far_normed, far_slope, inverse, far_inverse)),
+    )
 
 
 def pad_by_block(meta, src, low, high, pad):
@@ -417,11 +474,11 @@
 
     @pl.when(b == 0)
     def _():
-        fill_first(pad, meta, src, low)
+        fill_first(pad, meta, src, low())
 
     @pl.when(b == last)
     def _():
-        fill_last(pad, meta, src, high)
+        fill_last(pad, meta, src, high())
 
     @pl.when((b > 0) & (b < last))
     def _():
@@ -432,7 +489,7 @@
     b = pl.program_id(0)
     last = pl.num_programs(0) - 1
     width = src.shape[1]
-    pad_by_block(meta, src, low, high, pad)
+    pad_by_block(meta, src, lambda: low[HALF:], lambda: high[:HALF], pad)
 
     @pl.when(b == 0)
     def _():
@@ -468,8 +525,8 @@
             in_specs=[
                 whole(glu.shape),
                 pl.BlockSpec((BLOCK, width), lambda n, _: (n, 0)),
-                whole((HALF, width)),
-                whole((HALF, width)),
+                whole((2 * HALF, width)),
+                whole((2 * HALF, width)),
             ],
             out_specs=whole((groups, 2 * TAPS // groups, width // 2)),
             scratch_shapes=[
@@ -477,16 +534,16 @@
                 pltpu.VMEM((TAPS, 8, width), F32),
             ],
         ),
-        compiler_params=params(),
+        compiler_params=params(16),
         cost_estimate=cost(),
         name="taps_gradient",
     )(meta, glu, in_hbm(grad_conv), *map(in_hbm, edges))
 
 
-def back_kernel(meta, src, taps, gate_ref, slope_ref, low, high, out_ref, pad):
+def back_kernel(meta, src, taps, gate_ref, slope_ref, far, out_ref, pad):
     b = pl.program_id(0)
     width = src.shape[1]
-    pad_by_block(meta, src, low, high, pad)
+    pad_by_block(meta, src, lambda: far[:HALF], lambda: far[HALF:], pad)
     valid = below(meta[COUNT + b], BLOCK)
 
     @pl.loop(0, width // LANES)
@@ -500,7 +557,7 @@
         ).astype(BF16)
 
 
-def conv_backward(meta, grad_conv, taps, gate, slope, edges):
+def conv_backward(meta, grad_conv, far, taps, gate, slope):
     rows, width = grad_conv.shape
     block = pl.BlockSpec((BLOCK, width), lambda n, _: (n, 0))
     return pl.pallas_call(
@@ -514,16 +571,15 @@
                 whole(taps.shape),
                 block,
                 block,
-                whole((HALF, width)),
-                whole((HALF, width)),
+                whole(far.shape),
             ],
             out_specs=pl.BlockSpec((BLOCK, 2 * width), lambda n, _: (n, 0)),
             scratch_shapes=[pltpu.VMEM((BLOCK + 2 * HALF, width), F32)],
         ),
-        compiler_params=params(),
+        compiler_params=params(16),
         cost_estimate=cost(),
         name="conv_backward",
-    )(meta, in_hbm(grad_conv), taps, in_hbm(gate), in_hbm(slope), *map(in_hbm, edges))
+    )(meta, in_hbm(grad_conv), taps, in_hbm(gate), in_hbm(slope), in_hbm(far))
 
 
 def input_kernel(gain_ref, grad_ref, w_ref, normed_ref, inverse_ref, out_ref, hidden):
@@ -561,7 +617,7 @@
         ],
         out_specs=whole((rows, width)),
         scratch_shapes=[pltpu.VMEM((rows, width), F32)],
-        compiler_params=params(),
+        compiler_params=params(28),
         cost_estimate=cost(),
         name="input_gradient",
     )(gain, in_hbm(grad_proj), in_hbm(weight), in_hbm(normed), in_hbm(inverse))
@@ -608,12 +664,17 @@
     return lax.dot_general(left, right, (((0,), (0,)), ((), ())), preferred_element_type=F32)
 
 
-def outer_of_chip(left, right, core):
-    half = right.shape[1] // 2
-    ours = lax.dynamic_slice_in_dim(right, core * half, half, axis=1)
-    theirs = lax.dynamic_slice_in_dim(right, (1 - core) * half, half, axis=1)
-    arrived = swap(outer(left, theirs).astype(BF16), "fsdp", 1)
-    return (outer(left, ours) + arrived.astype(F32)).astype(BF16)
+def half_of(values, which):
+    half = values.shape[1] // 2
+    return lax.dynamic_slice_in_dim(values, which * half, half, axis=1)
+
+
+def half_for_other(left, right, core):
+    return swap(outer(left, half_of(right, 1 - core)).astype(BF16), "fsdp", 1)
+
+
+def with_own_half(left, right, core, arrived):
+    return (outer(left, half_of(right, core)) + arrived.astype(F32)).astype(BF16)
 
 
 def send_over_dp(both):
@@ -657,7 +718,9 @@
     slot = jnp.sum(
         jnp.where(packing[None, :] == mine[:, None], number[None, :] % blocks, 0), axis=1
     )
-    return jnp.concatenate([left, right, valid, slot]).astype(jnp.int32)
+    closes = ends - 1 == (place + 1) * blocks
+    after = BLOCK + jnp.sum(jnp.where(closes, tails - BLOCK, 0), keepdims=True)
+    return jnp.concatenate([left, right, valid, slot, after]).astype(jnp.int32)
 
 
 def target_order(packing, place, blocks):
@@ -695,6 +758,10 @@
     gain_conv = conv_gain.reshape(1, width)
 
     quarters = spread(inputs.reshape(dp_count, rows // dp_count, width), "dp")
+    upstream = out_grad[0, 0]
+    beyond = halves_of_neighbours(upstream[:HALF], upstream[rows - HALF :])
+    order, beyond = lax.optimization_barrier((order, beyond))
+    around = jnp.concatenate([upstream, *beyond])
     arrived = spread(reorder(order, quarters), "dp")
 
     normed_in, inverse_in, gate, gate_slope, glu, low, high = project(
@@ -702,25 +769,20 @@
     )
     glu_edges = halves_of_neighbours(low, high)
     held = conv_forward(True, meta, glu, kernel, gain_conv)
-    normed, inverse, slope, swished = conv_forward(
+    normed, inverse, slope, swished, *far = conv_forward(
         False, meta, glu, kernel, gain_conv, glu_edges, held
     )
 
-    upstream = out_grad[0, 0]
-    grad_s = lax.dot_general(
-        upstream, full_out, (((1,), (1,)), ((), ())), preferred_element_type=F32
-    )
-    both = outer_of_chip(swished, upstream, core)
-    both, grad_s = lax.optimization_barrier((both, grad_s))
-    grad_conv, low, high = grad_conv_call(meta, normed, inverse, slope, grad_s)
-    edges = halves_of_neighbours(low, high)
-    both, grad_conv, edges = lax.optimization_barrier((both, grad_conv, edges))
+    arrived = half_for_other(swished, upstream, core)
+    grad_conv, far = grad_conv_call(meta, around, full_out, normed, inverse, slope, far)
+    arrived, grad_conv = lax.optimization_barrier((arrived, grad_conv))
+    both = with_own_half(swished, upstream, core, arrived)
     sent = send_over_dp(both)
     fsdp_count = lax.axis_size("fsdp")
     taps_rows = taps_gradient(meta, glu, grad_conv, glu_edges, fsdp_count, scale)
     taps_rows = sum_of_chip(taps_rows, core)
     taps_rows, grad_conv = lax.optimization_barrier((taps_rows, grad_conv))
-    grad_proj = conv_backward(meta, grad_conv, kernel, gate, gate_slope, edges)
+    grad_proj = conv_backward(meta, grad_conv, far, kernel, gate, gate_slope)
     taps_rows = sum_along_x(taps_rows)
     taps_rows, grad_proj, swished = lax.optimization_barrier((taps_rows, grad_proj, swished))
     module_out = multiply(swished, full_out)

time: 221 us -> 215 us (0.973)
  Pallas kernels: 75 us -> 83.9 us
  starting transfers between devices: 57.6 us -> 51.2 us
  waiting for transfers between devices: 53.1 us -> 46.8 us
  matrix products: 12.7 us -> 7.32 us
    all_to_all x4, waiting for transfers between devices: 43 us -> 25.9 us  [spread(): return lax.all_to_all(values, axis, split_axis=0, concat_axis=0, tiled=True)]
    ppermute x2, waiting for transfers between devices: 0.01 us -> 13.4 us  [halves_of_neighbours(): lax.ppermute(high, 'dp', forward)]
    pallas_call x1, Pallas kernels: 3.49 us -> 9.6 us  [grad_conv_call(): pl.pallas_call(grad_conv_kernel, out_shape=[pltpu.HBM((rows, width), BF16...]
    dot_general x1 -> x0, matrix products: 4.64 us -> none  [local(): lax.dot_general(upstream, full_out, (((1,), (1,)), ((), ())), preferred_e...]
    ppermute x11, starting transfers between devices: 16.5 us -> 13.1 us  [swap(): lax.ppermute(values, axis, [(i, i ^ bits) for i in range(lax.axis_size(ax...]
    ppermute x2, waiting for transfers between devices: 3.84 us -> 0.61 us  [halves_of_neighbours(): lax.ppermute(low, 'dp', backward)]
    pallas_call x2, Pallas kernels: 14.5 us -> 17.3 us  [split_call(): pl.pallas_call(functools.partial(kernel, inner), out_shape=[o[2](*o[:2])...]
    ppermute x2, starting transfers between devices: 6.99 us -> 4.55 us  [halves_of_neighbours(): lax.ppermute(high, 'dp', forward)]
  transfers between devices with their start and end apart: 21 -> 21, of which waited for: 7 -> 9; matrix products, arithmetic and copies ran while one was open for 5% -> 4% of each run, Pallas kernels for 32% -> 39%
where the time goes in v4:
time: 215 us
  Pallas kernels  83.9 us (39%)
  starting transfers between devices  51.2 us (24%)
  waiting for transfers between devices  46.8 us (22%)
  between operations  15.2 us (7%)
  matrix products  7.32 us (3%)
  other arithmetic  7.08 us (3%)
  local copies, waits for them, and re-layouts  3.01 us (1%)
    all_to_all x4, starting transfers between devices, spread(): return lax.all_to_all(values, axis, split_axis=0, concat_axis=0, tiled=True)  30.9 us
    all_to_all x4, waiting for transfers between devices, spread(): return lax.all_to_all(values, axis, split_axis=0, concat_axis=0, tiled=True)  25.9 us
    pallas_call x2, Pallas kernels, split_call(): pl.pallas_call(functools.partial(kernel, inner), out_shape=[o[2](*o[:2])...  17.3 us
    pallas_call x1, Pallas kernels, conv_backward(): pl.pallas_call(back_kernel, out_shape=pltpu.HBM((rows, 2 * width), BF16),...  14.4 us
    ppermute x2, waiting for transfers between devices, halves_of_neighbours(): lax.ppermute(high, 'dp', forward)  13.4 us
    ppermute x11, starting transfers between devices, swap(): lax.ppermute(values, axis, [(i, i ^ bits) for i in range(lax.axis_size(ax...  13.1 us
    pallas_call x1, Pallas kernels, project(): pl.pallas_call(project_kernel, out_shape=[pltpu.HBM((rows, width), BF16),...  12.5 us
    pallas_call x1, Pallas kernels, taps_gradient(): pl.pallas_call(functools.partial(taps_kernel, scale), out_shape=jax.Shape...  11.3 us
  transfers between devices with their start and end apart: 21, of which 9 were waited for; matrix products, arithmetic and copies ran while one was open for 4% of the time, Pallas kernels for 39%

profile of v4, /device:TPU:1, one launch (start us, length us, event | category | flops | bytes accessed | tf_op | source)
XLA Modules:
  0.0 214.6 jit_solution(3721216955121864645)
XLA Ops:
  7.2 0.0 all-gather.3.cloned.1.call-start
  7.2 0.7 all-gather.3.cloned.1.call-update
  7.9 0.0 all-gather.5.cloned.1.call-start
  7.9 0.7 all-gather.5.cloned.1.call-update
  8.7 8.7 %all-to-all-start = ((bf16[16,32,1536]{2,1,0:T(8,128)(2,1)}), bf16[16,32,1536]{2,1,0:T(8,128)(2,1)S(1)}, u32[]{:S(2)}, u32[]{:S(2)}) async-start(bf16[16,32,1536]{2,1,0:T(8,128)(2,1)} %bitcast.9), calls=%async_computation | async-start | bytes 3145728 | tf_op jit(solution)/shard_map/all_to_all | solution.py:660
  17.4 0.8 slice_bitcast_fusion.2
  18.3 3.3 %collective-permute-start = (bf16[16,1536]{1,0:T(8,128)(2,1)S(1)}, bf16[16,1536]{1,0:T(8,128)(2,1)S(1)}, u32[]{:S(2)}, u32[]{:S(2)}) collective-permute-start(bf16[16,1536]{1,0:T(8,128)(2,1)S(1)} %get-tuple-element.80), channel_id=1, source_target_pairs={{0,8},{8,16},{16,24},{24,32},{32,40},{40,48},{48,56},{56,64},{64,7... | collective-permute-start | bytes 147464 | tf_op jit(solution)/shard_map/ppermute | solution.py:630
  21.5 1.3 collective-permute-start.1
  22.9 0.1 select_reduce_fusion
  23.0 0.1 select_reduce_fusion.1.order
  23.1 13.4 %collective-permute-done = bf16[16,1536]{1,0:T(8,128)(2,1)S(1)} collective-permute-done((bf16[16,1536]{1,0:T(8,128)(2,1)S(1)}, bf16[16,1536]{1,0:T(8,128)(2,1)S(1)}, u32[]{:S(2)}, u32[]{:S(2)}) %collective-permute-start) | collective-permute-done | bytes 49184 | tf_op jit(solution)/shard_map/ppermute | solution.py:630
  36.5 0.6 collective-permute-done.1
  37.1 3.2 %all-to-all-done.x_ref = bf16[16,32,1536]{2,1,0:T(8,128)(2,1)S(1)} async-done(((bf16[16,32,1536]{2,1,0:T(8,128)(2,1)}), bf16[16,32,1536]{2,1,0:T(8,128)(2,1)S(1)}, u32[]{:S(2)}, u32[]{:S(2)}) %all-to-all-start) | async-done | bytes 1572896 | tf_op jit(solution)/shard_map/all_to_all | solution.py:660
  40.3 1.8 reorder.1
  42.1 5.8 %all-to-all-start.1 = ((bf16[16,32,1536]{2,1,0:T(8,128)(2,1)}), bf16[16,32,1536]{2,1,0:T(8,128)(2,1)S(1)}, u32[]{:S(2)}, u32[]{:S(2)}) async-start(bf16[16,32,1536]{2,1,0:T(8,128)(2,1)} %reorder.1), calls=%async_computation.1 | async-start | bytes 3145728 | tf_op jit(solution)/shard_map/all_to_all | solution.py:660
  48.0 0.6 fusion.11
  49.3 0.2 select_reduce_fusion.2
  49.5 0.2 fusion.8
  49.7 0.1 concatenate.15.meta
  49.8 21.9 %all-to-all-done.1.x_ref = bf16[16,32,1536]{2,1,0:T(8,128)(2,1)S(1)} async-done(((bf16[16,32,1536]{2,1,0:T(8,128)(2,1)}), bf16[16,32,1536]{2,1,0:T(8,128)(2,1)S(1)}, u32[]{:S(2)}, u32[]{:S(2)}) %all-to-all-start.1) | async-done | bytes 1572896 | tf_op jit(solution)/shard_map/all_to_all | solution.py:660
  71.7 1.1 copy-done.4
  72.8 12.5 %project.1 = (bf16[512,1536]{1,0:T(8,128)(2,1)}, f32[512,1]{1,0:T(8,128)}, f32[512,1536]{1,0:T(8,128)}, f32[512,1536]{1,0:T(8,128)}, bf16[512,1536]{1,0:T(8,128)...) custom-call(s32[17]{0:T(128)S(1)} %concatenate.15.meta, bf16[16,32,1536]{2,1,0:T(8,128)(2,1)} %copy-done.4, ...), custom_call_target="tpu_custom_call" | custom-call | flops 1000 | bytes 1000 | tf_op jit(solution)/shard_map/project/pallas_call | solution.py:142
  85.3 1.3 collective-permute-start.2
  86.6 1.3 collective-permute-start.3
  88.0 7.7 %conv_kernel_inner.1 = (bf16[512,1536]{1,0:T(8,128)(2,1)}, f32[512,1]{1,0:T(8,128)}, f32[512,1536]{1,0:T(8,128)}, bf16[512,1536]{1,0:T(8,128)(2,1)S(1)}) custom-call(s32[17]{0:T(128)S(1)} %concatenate.15.meta, bf16[512,1536]{1,0:T(8,128)(2,1)S(1)} %get-tuple-element.41.refs_0_.src, f32[32,1536]{1,0:T(8,128)S(1)} %copy-done.3, f32[1,1536]{1,0:T(1,128)S(1)} %reshape.93.refs_2_), custom_call_target="tpu_custom_call" | custom-call | flops 1000 | bytes 1000 | tf_op jit(solution)/shard_map/conv_kernel_inner/pallas_call | solution.py:321
  95.7 0.0 collective-permute-done.2.refs_3_.low
  95.7 0.0 collective-permute-done.3.refs_4_.high
  95.7 0.0 copy-start.8
  95.7 0.7 copy-done.8
  96.4 9.6 %conv_kernel_edges.1 = (bf16[512,1536]{1,0:T(8,128)(2,1)}, f32[512,1]{1,0:T(8,128)}, f32[512,1536]{1,0:T(8,128)}, bf16[512,1536]{1,0:T(8,128)(2,1)S(1)}, bf16[32...) custom-call(s32[17]{0:T(128)S(1)} %concatenate.15.meta, ...), custom_call_target="tpu_custom_call", output_to_operand_aliasing={{0}: (6, {}), {1}: (7, {}), {2}: (8, {}), {3}: (9, {})} | custom-call | flops 1000 | bytes 1000 | tf_op jit(solution)/shard_map/conv_kernel_edges/pallas_call | solution.py:321
  106.0 2.8 %convolution_convert_fusion = bf16[1536,768]{1,0:T(8,128)(2,1)} fusion(bf16[512,1536]{1,0:T(8,128)(2,1)S(1)} %get-tuple-element.66.x_ref, bf16[1,1,512,1536]{3,2,1,0:T(8,128)(2,1)S(1)} %copy-done.5, s32[]{:T(128)S(6)} %select_n.103), kind=kOutput, calls=%fused_computation.2 | convolution fusion | flops 1209139200 | bytes 4718596 | tf_op jit(solution)/shard_map/dot_general | solution.py:664
  108.8 1.8 collective-permute-start.4
  110.6 1.5 pad_maximum_fusion.grad_ref
  112.1 0.0 all-gather.5.cloned.1.call-done.w_ref
  112.1 0.0 copy-start.1
  112.2 0.0 copy-start.6
  112.2 9.6 %grad_conv.1 = (bf16[512,1536]{1,0:T(8,128)(2,1)}, bf16[32,1536]{1,0:T(8,128)(2,1)}) custom-call(s32[17]{0:T(128)S(1)} %concatenate.15.meta, bf16[544,1536]{1,0:T(8,128)(2,1)S(1)} %pad_maximum_fusion.grad_ref, bf16[1536,1536]{1,0:T(8,128)(2,1)} %all-gather.5.cloned.1.call-done.w_ref, bf16[512,1536]{1,0:T(8,128)(2,1)} %get-tuple-element.51.normed_ref, ...), custom_call_target="tpu_custom_call" | custom-call | flops 1000 | bytes 1000 | tf_op jit(solution)/shard_map/grad_conv/pallas_call | solution.py:438
  121.8 0.0 collective-permute-done.4
  121.8 4.5 %add_convert_fusion = bf16[1536,768]{1,0:T(8,128)(2,1)} fusion(bf16[1536,768]{1,0:T(8,128)(2,1)} %collective-permute-done.4, bf16[512,1536]{1,0:T(8,128)(2,1)S(1)} %copy-done.1, bf16[1,1,512,1536]{3,2,1,0:T(8,128)(2,1)S(1)} %copy-done.6, s32[]{:T(128)S(6)} %select_n.111), kind=kOutput, calls=%fused_computation.1 | convolution fusion | flops 1211498496 | bytes 7077892 | tf_op jit(solution)/shard_map/dot_general | solution.py:664
  126.3 8.0 %all-to-all-start.2 = ((bf16[16,96,768]{2,1,0:T(8,128)(2,1)}), bf16[16,96,768]{2,1,0:T(8,128)(2,1)}, u32[]{:S(2)}, u32[]{:S(2)}) async-start(bf16[16,96,768]{2,1,0:T(8,128)(2,1)} %bitcast.56), calls=%async_computation.2 | async-start | bytes 4718592 | tf_op jit(solution)/shard_map/all_to_all | solution.py:660
  134.3 11.3 %taps_gradient.1 = f32[8,8,768]{2,1,0:T(8,128)S(1)} custom-call(s32[17]{0:T(128)S(1)} %concatenate.15.meta, bf16[512,1536]{1,0:T(8,128)(2,1)S(1)} %get-tuple-element.41.refs_0_.src, bf16[512,1536]{1,0:T(8,128)(2,1)} %get-tuple-element.60.grad_ref.src, bf16[32,1536]{1,0:T(8,128)(2,1)} %copy-done.7, bf16[32,1536]{1,0:T(8,128)(2,1)} %copy-done.8), custom_call_target="tpu_custom_call" | custom-call | flops 1000 | bytes 1000 | tf_op jit(solution)/shard_map/taps_gradient/pallas_call | solution.py:519
  145.7 0.4 collective-permute-start.5
  146.1 1.0 collective-permute-done.5
  147.1 1.3 collective-permute-start.6
  148.4 2.3 %collective-permute-start.7 = (f32[8,768]{1,0:T(8,128)S(1)}, f32[8,768]{1,0:T(8,128)S(1)}, u32[]{:S(2)}, u32[]{:S(2)}) collective-permute-start(f32[8,768]{1,0:T(8,128)S(1)} %get-tuple-element.87), channel_id=1, source_target_pairs={{0,4},{1,5},{2,6},{3,7},{4,0},{5,1},{6,2},{7,3},{8,12},{9,13},{10,... | collective-permute-start | bytes 73736 | tf_op jit(solution)/shard_map/ppermute | solution.py:634
  150.8 0.3 collective-permute-start.8
  151.1 14.4 %conv_backward.1.grad_ref = bf16[512,3072]{1,0:T(8,128)(2,1)} custom-call(s32[17]{0:T(128)S(1)} %concatenate.15.meta, bf16[512,1536]{1,0:T(8,128)(2,1)} %get-tuple-element.60.grad_ref.src, f32[32,1536]{1,0:T(8,128)S(1)} %copy-done.3, f32[512,1536]{1,0:T(8,128)} %get-tuple-element.61.gate_ref, f32[512,1536]{1,0:T(8,128)} %get-tuple-element.62.slope_ref, ...), custom_call_target="tpu_custom_call" | custom-call | flops 1000 | bytes 1000 | tf_op jit(solution)/shard_map/conv_backward/pallas_call | solution.py:563
  165.4 0.0 collective-permute-done.8
  165.5 5.8 %multiply.1 = bf16[512,1536]{1,0:T(8,128)(2,1)} custom-call(bf16[512,1536]{1,0:T(8,128)(2,1)S(1)} %copy-done.2, bf16[1536,1536]{1,0:T(8,128)(2,1)} %all-gather.5.cloned.1.call-done.w_ref), custom_call_target="tpu_custom_call" | custom-call | flops 1000 | bytes 1000 | tf_op jit(solution)/shard_map/multiply/pallas_call | solution.py:378
  171.3 0.8 all-to-all-done.2
  172.0 2.2 %collective-permute-start.10 = (f32[8,768]{1,0:T(8,128)S(1)}, f32[8,768]{1,0:T(8,128)S(1)}, u32[]{:S(2)}, u32[]{:S(2)}) collective-permute-start(f32[8,768]{1,0:T(8,128)S(1)} %fusion.5), channel_id=1, source_target_pairs={{0,16},{8,24},{16,0},{24,8},{32,48},{40,56},{48,32},{56,40},{64,80... | collective-permute-start | bytes 73736 | tf_op jit(solution)/shard_map/ppermute | solution.py:634
  174.3 0.9 collective-permute-start.11
  175.2 2.0 convert_reduce_fusion
  177.2 1.0 collective-permute-done.11
  178.2 1.3 collective-permute-start.12
  179.4 2.4 %collective-permute-start.13 = (f32[8,768]{1,0:T(8,128)S(1)}, f32[8,768]{1,0:T(8,128)S(1)}, u32[]{:S(2)}, u32[]{:S(2)}) collective-permute-start(f32[8,768]{1,0:T(8,128)S(1)} %add_add_fusion.1), channel_id=1, source_target_pairs={{0,64},{8,72},{16,80},{24,88},{32,96},{40,104},{48,112},{56,120},{... | collective-permute-start | bytes 73736 | tf_op jit(solution)/shard_map/ppermute | solution.py:634
  181.8 0.3 collective-permute-start.14
  182.2 1.4 collective-permute-done.13
  183.6 2.1 collective-permute-done.14
  185.8 0.8 pad_maximum_fusion.1
  186.6 8.3 %all-to-all-start.3 = ((f32[8,20,768]{2,1,0:T(8,128)}), f32[8,20,768]{2,1,0:T(8,128)S(1)}, u32[]{:S(2)}, u32[]{:S(2)}) async-start(f32[8,20,768]{2,1,0:T(8,128)} %pad_maximum_fusion.1), calls=%async_computation.3 | async-start | bytes 1179648 | tf_op jit(solution)/shard_map/all_to_all | solution.py:660
  194.9 11.3 %input_gradient.1 = bf16[512,1536]{1,0:T(8,128)(2,1)} custom-call(f32[1,1536]{1,0:T(1,128)S(1)} %reshape.92.gain_ref, bf16[512,3072]{1,0:T(8,128)(2,1)} %conv_backward.1.grad_ref, bf16[1536,3072]{1,0:T(8,128)(2,1)} %all-gather.3.cloned.1.call-done.wl_ref.wg_ref.w_ref, bf16[512,1536]{1,0:T(8,128)(2,1)} %get-tuple-element.72.normed_ref, ...), custom_call_target="tpu_custom_call" | custom-call | flops 1000 | bytes 1000 | tf_op jit(solution)/shard_map/input_gradient/pallas_call | solution.py:607
  206.4 0.7 pad_maximum_fusion.2
  207.1 0.6 pad_maximum_fusion.3
  (65 shorter events, 0.5 us)
Async XLA Ops:
  7.2 64.5 %all-gather.3.cloned.1.call-start = ((), (), s32[]{:S(2)}) async-start(), calls=%async_computation.4 | async-start | bytes 10616832 | tf_op jit(solution)/shard_map/all_gather | solution.py:753
  7.9 104.2 %all-gather.5.cloned.1.call-start = ((), (), s32[]{:S(2)}) async-start(), calls=%async_computation.5 | async-start | bytes 5308416 | tf_op jit(solution)/shard_map/all_gather | solution.py:754
  8.6 14.2 %copy-start.17 = (s32[1,32]{1,0:T(1,128)S(1)}, s32[1,32]{1,0:T(1,128)}, u32[]{:S(2)}) copy-start(s32[1,32]{1,0:T(1,128)} %param.18) | copy-start | bytes 388
  8.7 14.3 %copy-start.16 = (s32[1,64]{1,0:T(1,128)S(1)}, s32[1,64]{1,0:T(1,128)}, u32[]{:S(2)}) copy-start(s32[1,64]{1,0:T(1,128)} %param.17) | copy-start | bytes 772
  8.7 14.4 %copy-start.13 = (f32[1536]{0:T(1024)S(1)}, f32[1536]{0:T(1024)}, u32[]{:S(2)}) copy-start(f32[1536]{0:T(1024)} %param.11) | copy-start | bytes 18436
  8.7 31.6 %all-to-all-start = ((bf16[16,32,1536]{2,1,0:T(8,128)(2,1)}), bf16[16,32,1536]{2,1,0:T(8,128)(2,1)S(1)}, u32[]{:S(2)}, u32[]{:S(2)}) async-start(bf16[16,32,1536]{2,1,0:T(8,128)(2,1)} %bitcast.9), calls=%async_computation | async-start | bytes 3145728 | tf_op jit(solution)/shard_map/all_to_all | solution.py:660
  18.3 18.2 %collective-permute-start = (bf16[16,1536]{1,0:T(8,128)(2,1)S(1)}, bf16[16,1536]{1,0:T(8,128)(2,1)S(1)}, u32[]{:S(2)}, u32[]{:S(2)}) collective-permute-start(bf16[16,1536]{1,0:T(8,128)(2,1)S(1)} %get-tuple-element.80), channel_id=1, source_target_pairs={{0,8},{8,16},{16,24},{24,32},{32,40},{40,48},{48,56},{56,64},{64,7... | collective-permute-start | bytes 147464 | tf_op jit(solution)/shard_map/ppermute | solution.py:630
  21.5 15.6 %collective-permute-start.1 = (bf16[16,1536]{1,0:T(8,128)(2,1)S(1)}, bf16[16,1536]{1,0:T(8,128)(2,1)S(1)}, u32[]{:S(2)}, u32[]{:S(2)}) collective-permute-start(bf16[16,1536]{1,0:T(8,128)(2,1)S(1)} %get-tuple-element.79), channel_id=1, source_target_pairs={{8,0},{16,8},{24,16},{32,24},{40,32},{48,40},{56,48},{64,56},{72,6... | collective-permute-start | bytes 147464 | tf_op jit(solution)/shard_map/ppermute | solution.py:630
  36.5 5.6 %copy-start.9 = (bf16[16,1536]{1,0:T(8,128)(2,1)}, bf16[16,1536]{1,0:T(8,128)(2,1)S(1)}, u32[]{:S(2)}) copy-start(bf16[16,1536]{1,0:T(8,128)(2,1)S(1)} %collective-permute-done) | copy-start | bytes 147460
  37.1 5.0 %copy-start.11 = (bf16[16,1536]{1,0:T(8,128)(2,1)}, bf16[16,1536]{1,0:T(8,128)(2,1)S(1)}, u32[]{:S(2)}) copy-start(bf16[16,1536]{1,0:T(8,128)(2,1)S(1)} %collective-permute-done.1) | copy-start | bytes 147460
  42.1 5.9 %copy-start.15 = (s32[1,32]{1,0:T(1,128)S(1)}, s32[1,32]{1,0:T(1,128)}, u32[]{:S(2)}) copy-start(s32[1,32]{1,0:T(1,128)} %param.19) | copy-start | bytes 388
  42.1 29.6 %all-to-all-start.1 = ((bf16[16,32,1536]{2,1,0:T(8,128)(2,1)}), bf16[16,32,1536]{2,1,0:T(8,128)(2,1)S(1)}, u32[]{:S(2)}, u32[]{:S(2)}) async-start(bf16[16,32,1536]{2,1,0:T(8,128)(2,1)} %reorder.1), calls=%async_computation.1 | async-start | bytes 3145728 | tf_op jit(solution)/shard_map/all_to_all | solution.py:660
  49.8 38.2 %copy-start.14 = (f32[1536]{0:T(1024)S(1)}, f32[1536]{0:T(1024)}, u32[]{:S(2)}) copy-start(f32[1536]{0:T(1024)} %param.14) | copy-start | bytes 18436
  49.8 38.2 %copy-start.3 = (f32[32,1536]{1,0:T(8,128)S(1)}, f32[32,1536]{1,0:T(8,128)}, u32[]{:S(2)}) copy-start(f32[32,1536]{1,0:T(8,128)} %taps.1) | copy-start | bytes 589828
  71.7 1.1 copy-start.4
  85.3 10.4 %collective-permute-start.2 = (bf16[32,1536]{1,0:T(8,128)(2,1)}, bf16[32,1536]{1,0:T(8,128)(2,1)S(1)}, u32[]{:S(2)}, u32[]{:S(2)}) collective-permute-start(bf16[32,1536]{1,0:T(8,128)(2,1)} %get-tuple-element.42), channel_id=1, source_target_pairs={{0,8},{8,16},{16,24},{24,32},{32,40},{40,48},{48,56},{56,64},{64,7... | collective-permute-start | bytes 294920 | tf_op jit(solution)/shard_map/ppermute | solution.py:630
  86.6 9.1 %collective-permute-start.3 = (bf16[32,1536]{1,0:T(8,128)(2,1)}, bf16[32,1536]{1,0:T(8,128)(2,1)S(1)}, u32[]{:S(2)}, u32[]{:S(2)}) collective-permute-start(bf16[32,1536]{1,0:T(8,128)(2,1)} %get-tuple-element.43), channel_id=1, source_target_pairs={{8,0},{16,8},{24,16},{32,24},{40,32},{48,40},{56,48},{64,56},{72,6... | collective-permute-start | bytes 294920 | tf_op jit(solution)/shard_map/ppermute | solution.py:630
  95.7 0.7 copy-start.7
  95.7 0.7 copy-start.8
  96.4 9.6 %copy-start.5 = (bf16[1,1,512,1536]{3,2,1,0:T(8,128)(2,1)S(1)}, bf16[1,1,512,1536]{3,2,1,0:T(8,128)(2,1)}, u32[]{:S(2)}) copy-start(bf16[1,1,512,1536]{3,2,1,0:T(8,128)(2,1)} %param.16) | copy-start | bytes 4718596
  106.0 2.9 %copy-start = (bf16[512,1536]{1,0:T(8,128)(2,1)}, bf16[512,1536]{1,0:T(8,128)(2,1)S(1)}, u32[]{:S(2)}) copy-start(bf16[512,1536]{1,0:T(8,128)(2,1)S(1)} %get-tuple-element.66.x_ref) | copy-start | bytes 4718596
  106.0 4.6 %copy-start.10 = (bf16[16,1536]{1,0:T(8,128)(2,1)S(1)}, bf16[16,1536]{1,0:T(8,128)(2,1)}, u32[]{:S(2)}) copy-start(bf16[16,1536]{1,0:T(8,128)(2,1)} %copy-done.9) | copy-start | bytes 147460
  106.0 4.6 %copy-start.12 = (bf16[16,1536]{1,0:T(8,128)(2,1)S(1)}, bf16[16,1536]{1,0:T(8,128)(2,1)}, u32[]{:S(2)}) copy-start(bf16[16,1536]{1,0:T(8,128)(2,1)} %copy-done.11) | copy-start | bytes 147460
  108.8 13.0 %collective-permute-start.4 = (bf16[1536,768]{1,0:T(8,128)(2,1)}, bf16[1536,768]{1,0:T(8,128)(2,1)}, u32[]{:S(2)}, u32[]{:S(2)}) collective-permute-start(bf16[1536,768]{1,0:T(8,128)(2,1)} %convolution_convert_fusion), channel_id=1, source_target_pairs={{0,1},{1,0},{2,3},{3,2},{4,5},{5,4},{6,7},{7,6},{8,9},{9,8},{10,11... | collective-permute-start | bytes 7077896 | tf_op jit(solution)/shard_map/ppermute | solution.py:634
  112.1 9.6 %copy-start.1 = (bf16[512,1536]{1,0:T(8,128)(2,1)S(1)}, bf16[512,1536]{1,0:T(8,128)(2,1)}, u32[]{:S(2)}) copy-start(bf16[512,1536]{1,0:T(8,128)(2,1)} %copy-done) | copy-start | bytes 4718596
  112.2 9.6 %copy-start.6 = (bf16[1,1,512,1536]{3,2,1,0:T(8,128)(2,1)S(1)}, bf16[1,1,512,1536]{3,2,1,0:T(8,128)(2,1)}, u32[]{:S(2)}) copy-start(bf16[1,1,512,1536]{3,2,1,0:T(8,128)(2,1)} %param.16) | copy-start | bytes 4718596
  126.3 45.8 %all-to-all-start.2 = ((bf16[16,96,768]{2,1,0:T(8,128)(2,1)}), bf16[16,96,768]{2,1,0:T(8,128)(2,1)}, u32[]{:S(2)}, u32[]{:S(2)}) async-start(bf16[16,96,768]{2,1,0:T(8,128)(2,1)} %bitcast.56), calls=%async_computation.2 | async-start | bytes 4718592 | tf_op jit(solution)/shard_map/all_to_all | solution.py:660
  145.7 1.4 collective-permute-start.5
  147.1 18.3 %collective-permute-start.6 = (f32[8,768]{1,0:T(8,128)S(1)}, f32[8,768]{1,0:T(8,128)S(1)}, u32[]{:S(2)}, u32[]{:S(2)}) collective-permute-start(f32[8,768]{1,0:T(8,128)S(1)} %get-tuple-element.85), channel_id=1, source_target_pairs={{0,2},{1,3},{2,0},{3,1},{4,6},{5,7},{6,4},{7,5},{8,10},{9,11},{10,... | collective-permute-start | bytes 73736 | tf_op jit(solution)/shard_map/ppermute | solution.py:634
  148.4 17.0 %collective-permute-start.7 = (f32[8,768]{1,0:T(8,128)S(1)}, f32[8,768]{1,0:T(8,128)S(1)}, u32[]{:S(2)}, u32[]{:S(2)}) collective-permute-start(f32[8,768]{1,0:T(8,128)S(1)} %get-tuple-element.87), channel_id=1, source_target_pairs={{0,4},{1,5},{2,6},{3,7},{4,0},{5,1},{6,2},{7,3},{8,12},{9,13},{10,... | collective-permute-start | bytes 73736 | tf_op jit(solution)/shard_map/ppermute | solution.py:634
  150.8 14.7 %collective-permute-start.8 = (f32[8,768]{1,0:T(8,128)S(1)}, f32[8,768]{1,0:T(8,128)S(1)}, u32[]{:S(2)}, u32[]{:S(2)}) collective-permute-start(f32[8,768]{1,0:T(8,128)S(1)} %get-tuple-element.86), channel_id=1, source_target_pairs={{0,6},{1,7},{2,4},{3,5},{4,2},{5,3},{6,0},{7,1},{8,14},{9,15},{10,... | collective-permute-start | bytes 73736 | tf_op jit(solution)/shard_map/ppermute | solution.py:634
  151.1 14.4 %copy-start.2 = (bf16[512,1536]{1,0:T(8,128)(2,1)S(1)}, bf16[512,1536]{1,0:T(8,128)(2,1)}, u32[]{:S(2)}) copy-start(bf16[512,1536]{1,0:T(8,128)(2,1)} %copy-done) | copy-start | bytes 4718596
  172.0 5.1 %collective-permute-start.10 = (f32[8,768]{1,0:T(8,128)S(1)}, f32[8,768]{1,0:T(8,128)S(1)}, u32[]{:S(2)}, u32[]{:S(2)}) collective-permute-start(f32[8,768]{1,0:T(8,128)S(1)} %fusion.5), channel_id=1, source_target_pairs={{0,16},{8,24},{16,0},{24,8},{32,48},{40,56},{48,32},{56,40},{64,80... | collective-permute-start | bytes 73736 | tf_op jit(solution)/shard_map/ppermute | solution.py:634
  174.3 3.9 %collective-permute-start.11 = (f32[8,768]{1,0:T(8,128)S(1)}, f32[8,768]{1,0:T(8,128)S(1)}, u32[]{:S(2)}, u32[]{:S(2)}) collective-permute-start(f32[8,768]{1,0:T(8,128)S(1)} %fusion.5), channel_id=1, source_target_pairs={{0,24},{8,16},{16,8},{24,0},{32,56},{40,48},{48,40},{56,32},{64,88... | collective-permute-start | bytes 73736 | tf_op jit(solution)/shard_map/ppermute | solution.py:634
  175.2 3.0 %collective-permute-start.9 = (f32[8,768]{1,0:T(8,128)S(1)}, f32[8,768]{1,0:T(8,128)S(1)}, u32[]{:S(2)}, u32[]{:S(2)}) collective-permute-start(f32[8,768]{1,0:T(8,128)S(1)} %fusion.5), channel_id=1, source_target_pairs={{0,8},{8,0},{16,24},{24,16},{32,40},{40,32},{48,56},{56,48},{64,72... | collective-permute-start | bytes 73736 | tf_op jit(solution)/shard_map/ppermute | solution.py:634
  178.2 4.0 %collective-permute-start.12 = (f32[8,768]{1,0:T(8,128)S(1)}, f32[8,768]{1,0:T(8,128)S(1)}, u32[]{:S(2)}, u32[]{:S(2)}) collective-permute-start(f32[8,768]{1,0:T(8,128)S(1)} %add_add_fusion.1), channel_id=1, source_target_pairs={{0,32},{8,40},{16,48},{24,56},{32,0},{40,8},{48,16},{56,24},{64,96... | collective-permute-start | bytes 73736 | tf_op jit(solution)/shard_map/ppermute | solution.py:634
  179.4 4.2 %collective-permute-start.13 = (f32[8,768]{1,0:T(8,128)S(1)}, f32[8,768]{1,0:T(8,128)S(1)}, u32[]{:S(2)}, u32[]{:S(2)}) collective-permute-start(f32[8,768]{1,0:T(8,128)S(1)} %add_add_fusion.1), channel_id=1, source_target_pairs={{0,64},{8,72},{16,80},{24,88},{32,96},{40,104},{48,112},{56,120},{... | collective-permute-start | bytes 73736 | tf_op jit(solution)/shard_map/ppermute | solution.py:634
  181.8 3.9 %collective-permute-start.14 = (f32[8,768]{1,0:T(8,128)S(1)}, f32[8,768]{1,0:T(8,128)S(1)}, u32[]{:S(2)}, u32[]{:S(2)}) collective-permute-start(f32[8,768]{1,0:T(8,128)S(1)} %add_add_fusion.1), channel_id=1, source_target_pairs={{0,96},{8,104},{16,112},{24,120},{32,64},{40,72},{48,80},{56,88},{... | collective-permute-start | bytes 73736 | tf_op jit(solution)/shard_map/ppermute | solution.py:634
  186.6 19.6 %all-to-all-start.3 = ((f32[8,20,768]{2,1,0:T(8,128)}), f32[8,20,768]{2,1,0:T(8,128)S(1)}, u32[]{:S(2)}, u32[]{:S(2)}) async-start(f32[8,20,768]{2,1,0:T(8,128)} %pad_maximum_fusion.1), calls=%async_computation.3 | async-start | bytes 1179648 | tf_op jit(solution)/shard_map/all_to_all | solution.py:660
Sparse Core Ops, SparseCore 0:
  9.7 57.7 all-gather.2
  69.1 34.5 all-gather.4

commit v5 on v4

--- a/solution.py
+++ b/solution.py
@@ -582,23 +582,43 @@
     )(meta, in_hbm(grad_conv), taps, in_hbm(gate), in_hbm(slope), in_hbm(far))
 
 
-def input_kernel(gain_ref, grad_ref, w_ref, normed_ref, inverse_ref, out_ref, hidden):
+def folded(values):
+    return functools.reduce(
+        lambda a, b: a + b, [values[:, t] for t in tiles(values.shape[1])]
+    )
+
+
+def input_kernel(
+    gain_ref, grad_ref, w_ref, normed_ref, inverse_ref, out_ref, incoming, normed, first, second
+):
     n = pl.program_id(0)
-    rows, width = hidden.shape
+    rows, width = incoming.shape
     tile = w_ref.shape[0]
     at = pl.ds(pl.multiple_of(n * tile, tile), tile)
-    hidden[:, at] = gain_ref[:, at] * lax.dot_general(
+
+    @pl.when(n == 0)
+    def _():
+        first[...] = jnp.zeros_like(first)
+        second[...] = jnp.zeros_like(second)
+
+    g = gain_ref[:, at] * lax.dot_general(
         grad_ref[...], w_ref[...], (((1,), (1,)), ((), ())), preferred_element_type=F32
     )
+    incoming[:, at] = g
+    normed[:, at] = normed_ref[...]
+    first[...] += folded(g)
+    second[...] += folded(g * normed_ref[...].astype(F32))
 
     @pl.when(n == pl.num_programs(0) - 1)
     def _():
-        for at in range(0, rows, BLOCK):
-            part = slice(at, at + BLOCK)
-            for t, back in norm_back(
-                lambda t, part=part: hidden[part, t], normed_ref, inverse_ref, part, width
-            ):
-                out_ref[part, t] = back.astype(BF16)
+        for start in range(0, rows, BLOCK):
+            part = slice(start, start + BLOCK)
+            one = jnp.sum(first[part], axis=1, keepdims=True) * (1.0 / width)
+            two = jnp.sum(second[part], axis=1, keepdims=True) * (1.0 / width)
+            inverse = inverse_ref[part]
+            for t in tiles(width):
+                back = incoming[part, t] - one - normed[part, t].astype(F32) * two
+                out_ref[part, t] = (back * inverse).astype(BF16)
 
 
 def input_gradient(gain, grad_proj, weight, normed, inverse, tile=512):
@@ -612,11 +632,16 @@
             whole((1, width)),
             whole(grad_proj.shape),
             pl.BlockSpec((tile, weight.shape[1]), lambda n: (n, 0)),
-            whole(normed.shape),
+            pl.BlockSpec((rows, tile), lambda n: (0, n)),
             whole(inverse.shape),
         ],
         out_specs=whole((rows, width)),
-        scratch_shapes=[pltpu.VMEM((rows, width), F32)],
+        scratch_shapes=[
+            pltpu.VMEM((rows, width), F32),
+            pltpu.VMEM((rows, width), BF16),
+            pltpu.VMEM((rows, LANES), F32),
+            pltpu.VMEM((rows, LANES), F32),
+        ],
         compiler_params=params(28),
         cost_estimate=cost(),
         name="input_gradient",
@@ -762,6 +787,7 @@
     beyond = halves_of_neighbours(upstream[:HALF], upstream[rows - HALF :])
     order, beyond = lax.optimization_barrier((order, beyond))
     around = jnp.concatenate([upstream, *beyond])
+    meta, around = lax.optimization_barrier((meta, around))
     arrived = spread(reorder(order, quarters), "dp")
 
     normed_in, inverse_in, gate, gate_slope, glu, low, high = project(

time: 215 us -> 213 us (level)
  no operation moved by 1% of the time
where the time goes in v5:
time: 213 us; the launch traced here: 212 us
  Pallas kernels  83.6 us (39%)
  starting transfers between devices  51.5 us (24%)
  waiting for transfers between devices  45.1 us (21%)
  between operations  15.1 us (7%)
  matrix products  7.48 us (4%)
  other arithmetic  7.1 us (3%)
  local copies, waits for them, and re-layouts  2.34 us (1%)
    all_to_all x4, starting transfers between devices, spread(): return lax.all_to_all(values, axis, split_axis=0, concat_axis=0, tiled=True)  30.3 us
    all_to_all x4, waiting for transfers between devices, spread(): return lax.all_to_all(values, axis, split_axis=0, concat_axis=0, tiled=True)  25.5 us
    pallas_call x2, Pallas kernels, split_call(): pl.pallas_call(functools.partial(kernel, inner), out_shape=[o[2](*o[:2])...  17.3 us
    pallas_call x1, Pallas kernels, conv_backward(): pl.pallas_call(back_kernel, out_shape=pltpu.HBM((rows, 2 * width), BF16),...  14.3 us
    ppermute x11, starting transfers between devices, swap(): lax.ppermute(values, axis, [(i, i ^ bits) for i in range(lax.axis_size(ax...  13.3 us
    pallas_call x1, Pallas kernels, project(): pl.pallas_call(project_kernel, out_shape=[pltpu.HBM((rows, width), BF16),...  12.5 us
    ppermute x2, waiting for transfers between devices, halves_of_neighbours(): lax.ppermute(high, 'dp', forward)  12.1 us
    pallas_call x1, Pallas kernels, taps_gradient(): pl.pallas_call(functools.partial(taps_kernel, scale), out_shape=jax.Shape...  11.3 us
  transfers between devices with their start and end apart: 21, of which 9 were waited for; matrix products, arithmetic and copies ran while one was open for 4% of the time, Pallas kernels for 39%

profile of v5, /device:TPU:1, one launch (start us, length us, event | category | flops | bytes accessed | tf_op | source)
XLA Modules:
  0.0 212.2 jit_solution(14248276185228597278)
XLA Ops:
  7.2 0.0 all-gather.3.cloned.1.call-start
  7.2 0.7 all-gather.3.cloned.1.call-update
  7.9 0.0 all-gather.5.cloned.1.call-start
  7.9 0.7 all-gather.5.cloned.1.call-update
  8.7 8.7 %all-to-all-start = ((bf16[16,32,1536]{2,1,0:T(8,128)(2,1)}), bf16[16,32,1536]{2,1,0:T(8,128)(2,1)S(1)}, u32[]{:S(2)}, u32[]{:S(2)}) async-start(bf16[16,32,1536]{2,1,0:T(8,128)(2,1)} %bitcast.10), calls=%async_computation | async-start | bytes 3145728 | tf_op jit(solution)/shard_map/all_to_all | solution.py:685
  17.4 0.8 slice_bitcast_fusion.2
  18.3 3.3 %collective-permute-start = (bf16[16,1536]{1,0:T(8,128)(2,1)S(1)}, bf16[16,1536]{1,0:T(8,128)(2,1)S(1)}, u32[]{:S(2)}, u32[]{:S(2)}) collective-permute-start(bf16[16,1536]{1,0:T(8,128)(2,1)S(1)} %get-tuple-element.84), channel_id=1, source_target_pairs={{0,8},{8,16},{16,24},{24,32},{32,40},{40,48},{48,56},{56,64},{64,7... | collective-permute-start | bytes 147464 | tf_op jit(solution)/shard_map/ppermute | solution.py:655
  21.5 1.3 collective-permute-start.1
  22.9 0.1 select_reduce_fusion.1.order
  23.0 0.1 select_reduce_fusion
  23.1 0.6 fusion.11
  24.4 12.1 %collective-permute-done = bf16[16,1536]{1,0:T(8,128)(2,1)S(1)} collective-permute-done((bf16[16,1536]{1,0:T(8,128)(2,1)S(1)}, bf16[16,1536]{1,0:T(8,128)(2,1)S(1)}, u32[]{:S(2)}, u32[]{:S(2)}) %collective-permute-start) | collective-permute-done | bytes 49184 | tf_op jit(solution)/shard_map/ppermute | solution.py:655
  36.5 0.6 collective-permute-done.1
  37.1 3.2 %all-to-all-done.x_ref = bf16[16,32,1536]{2,1,0:T(8,128)(2,1)S(1)} async-done(((bf16[16,32,1536]{2,1,0:T(8,128)(2,1)}), bf16[16,32,1536]{2,1,0:T(8,128)(2,1)S(1)}, u32[]{:S(2)}, u32[]{:S(2)}) %all-to-all-start) | async-done | bytes 1572896 | tf_op jit(solution)/shard_map/all_to_all | solution.py:685
  40.3 1.8 reorder.1
  42.1 5.7 %all-to-all-start.1 = ((bf16[16,32,1536]{2,1,0:T(8,128)(2,1)}), bf16[16,32,1536]{2,1,0:T(8,128)(2,1)S(1)}, u32[]{:S(2)}, u32[]{:S(2)}) async-start(bf16[16,32,1536]{2,1,0:T(8,128)(2,1)} %reorder.1), calls=%async_computation.1 | async-start | bytes 3145728 | tf_op jit(solution)/shard_map/all_to_all | solution.py:685
  47.8 0.2 select_reduce_fusion.2
  48.0 0.2 fusion.8
  48.3 0.1 concatenate.15.meta
  48.3 1.5 pad_maximum_fusion.grad_ref
  49.9 0.0 copy-start.8
  49.9 0.0 copy-start.3
  49.9 21.6 %all-to-all-done.1.x_ref = bf16[16,32,1536]{2,1,0:T(8,128)(2,1)S(1)} async-done(((bf16[16,32,1536]{2,1,0:T(8,128)(2,1)}), bf16[16,32,1536]{2,1,0:T(8,128)(2,1)S(1)}, u32[]{:S(2)}, u32[]{:S(2)}) %all-to-all-start.1) | async-done | bytes 1572896 | tf_op jit(solution)/shard_map/all_to_all | solution.py:685
  71.5 1.1 copy-done.4
  72.7 12.5 %project.1 = (bf16[512,1536]{1,0:T(8,128)(2,1)}, f32[512,1]{1,0:T(8,128)}, f32[512,1536]{1,0:T(8,128)}, f32[512,1536]{1,0:T(8,128)}, bf16[512,1536]{1,0:T(8,128)...) custom-call(s32[17]{0:T(128)S(1)} %concatenate.15.meta, bf16[16,32,1536]{2,1,0:T(8,128)(2,1)} %copy-done.4, ...), custom_call_target="tpu_custom_call" | custom-call | flops 1000 | bytes 1000 | tf_op jit(solution)/shard_map/project/pallas_call | solution.py:142
  85.2 1.9 collective-permute-start.2
  87.1 1.3 collective-permute-start.3
  88.4 7.7 %conv_kernel_inner.1 = (bf16[512,1536]{1,0:T(8,128)(2,1)}, f32[512,1]{1,0:T(8,128)}, f32[512,1536]{1,0:T(8,128)}, bf16[512,1536]{1,0:T(8,128)(2,1)S(1)}) custom-call(s32[17]{0:T(128)S(1)} %concatenate.15.meta, bf16[512,1536]{1,0:T(8,128)(2,1)S(1)} %get-tuple-element.46.refs_0_.src, f32[32,1536]{1,0:T(8,128)S(1)} %copy-done.3, f32[1,1536]{1,0:T(1,128)S(1)} %reshape.93.refs_2_), custom_call_target="tpu_custom_call" | custom-call | flops 1000 | bytes 1000 | tf_op jit(solution)/shard_map/conv_kernel_inner/pallas_call | solution.py:321
  96.1 0.0 collective-permute-done.2.refs_3_.low
  96.1 0.0 collective-permute-done.3.refs_4_.high
  96.2 9.6 %conv_kernel_edges.1 = (bf16[512,1536]{1,0:T(8,128)(2,1)}, f32[512,1]{1,0:T(8,128)}, f32[512,1536]{1,0:T(8,128)}, bf16[512,1536]{1,0:T(8,128)(2,1)S(1)}, bf16[32...) custom-call(s32[17]{0:T(128)S(1)} %concatenate.15.meta, ...), custom_call_target="tpu_custom_call", output_to_operand_aliasing={{0}: (6, {}), {1}: (7, {}), {2}: (8, {}), {3}: (9, {})} | custom-call | flops 1000 | bytes 1000 | tf_op jit(solution)/shard_map/conv_kernel_edges/pallas_call | solution.py:321
  105.7 2.9 %convolution_convert_fusion = bf16[1536,768]{1,0:T(8,128)(2,1)} fusion(bf16[512,1536]{1,0:T(8,128)(2,1)S(1)} %get-tuple-element.70.x_ref, bf16[1,1,512,1536]{3,2,1,0:T(8,128)(2,1)S(1)} %copy-done.5, s32[]{:T(128)S(6)} %select_n.103), kind=kOutput, calls=%fused_computation.2 | convolution fusion | flops 1209139200 | bytes 4718596 | tf_op jit(solution)/shard_map/dot_general | solution.py:689
  108.6 1.8 collective-permute-start.4
  110.5 9.6 %grad_conv.1 = (bf16[512,1536]{1,0:T(8,128)(2,1)}, bf16[32,1536]{1,0:T(8,128)(2,1)}) custom-call(s32[17]{0:T(128)S(1)} %concatenate.15.meta, bf16[544,1536]{1,0:T(8,128)(2,1)S(1)} %pad_maximum_fusion.grad_ref, bf16[1536,1536]{1,0:T(8,128)(2,1)} %all-gather.5.cloned.1.call-done.w_ref, bf16[512,1536]{1,0:T(8,128)(2,1)} %get-tuple-element.55.normed_ref, ...), custom_call_target="tpu_custom_call" | custom-call | flops 1000 | bytes 1000 | tf_op jit(solution)/shard_map/grad_conv/pallas_call | solution.py:438
  120.0 0.0 collective-permute-done.4
  120.0 4.6 %add_convert_fusion = bf16[1536,768]{1,0:T(8,128)(2,1)} fusion(bf16[1536,768]{1,0:T(8,128)(2,1)} %collective-permute-done.4, bf16[512,1536]{1,0:T(8,128)(2,1)S(1)} %copy-done.1, bf16[1,1,512,1536]{3,2,1,0:T(8,128)(2,1)S(1)} %copy-done.6, s32[]{:T(128)S(6)} %select_n.111), kind=kOutput, calls=%fused_computation.1 | convolution fusion | flops 1211498496 | bytes 7077892 | tf_op jit(solution)/shard_map/dot_general | solution.py:689
  124.6 7.6 %all-to-all-start.2 = ((bf16[16,96,768]{2,1,0:T(8,128)(2,1)}), bf16[16,96,768]{2,1,0:T(8,128)(2,1)}, u32[]{:S(2)}, u32[]{:S(2)}) async-start(bf16[16,96,768]{2,1,0:T(8,128)(2,1)} %bitcast.56), calls=%async_computation.2 | async-start | bytes 4718592 | tf_op jit(solution)/shard_map/all_to_all | solution.py:685
  132.2 11.3 %taps_gradient.1 = f32[8,8,768]{2,1,0:T(8,128)S(1)} custom-call(s32[17]{0:T(128)S(1)} %concatenate.15.meta, bf16[512,1536]{1,0:T(8,128)(2,1)S(1)} %get-tuple-element.46.refs_0_.src, bf16[512,1536]{1,0:T(8,128)(2,1)} %get-tuple-element.64.grad_ref.src, bf16[32,1536]{1,0:T(8,128)(2,1)} %collective-permute-done.2.refs_3_.low, ...), custom_call_target="tpu_custom_call" | custom-call | flops 1000 | bytes 1000 | tf_op jit(solution)/shard_map/taps_gradient/pallas_call | solution.py:519
  143.6 0.4 collective-permute-start.5
  144.0 1.0 collective-permute-done.5
  145.0 1.3 collective-permute-start.6
  146.3 2.4 %collective-permute-start.7 = (f32[8,768]{1,0:T(8,128)S(1)}, f32[8,768]{1,0:T(8,128)S(1)}, u32[]{:S(2)}, u32[]{:S(2)}) collective-permute-start(f32[8,768]{1,0:T(8,128)S(1)} %get-tuple-element.91), channel_id=1, source_target_pairs={{0,4},{1,5},{2,6},{3,7},{4,0},{5,1},{6,2},{7,3},{8,12},{9,13},{10,... | collective-permute-start | bytes 73736 | tf_op jit(solution)/shard_map/ppermute | solution.py:659
  148.7 0.3 collective-permute-start.8
  149.0 14.3 %conv_backward.1.grad_ref = bf16[512,3072]{1,0:T(8,128)(2,1)} custom-call(s32[17]{0:T(128)S(1)} %concatenate.15.meta, bf16[512,1536]{1,0:T(8,128)(2,1)} %get-tuple-element.64.grad_ref.src, f32[32,1536]{1,0:T(8,128)S(1)} %copy-done.3, f32[512,1536]{1,0:T(8,128)} %get-tuple-element.65.gate_ref, f32[512,1536]{1,0:T(8,128)} %get-tuple-element.66.slope_ref, ...), custom_call_target="tpu_custom_call" | custom-call | flops 1000 | bytes 1000 | tf_op jit(solution)/shard_map/conv_backward/pallas_call | solution.py:563
  163.3 0.0 collective-permute-done.6
  163.3 0.0 collective-permute-done.8
  163.4 5.8 %multiply.1 = bf16[512,1536]{1,0:T(8,128)(2,1)} custom-call(bf16[512,1536]{1,0:T(8,128)(2,1)S(1)} %copy-done.2, bf16[1536,1536]{1,0:T(8,128)(2,1)} %all-gather.5.cloned.1.call-done.w_ref), custom_call_target="tpu_custom_call" | custom-call | flops 1000 | bytes 1000 | tf_op jit(solution)/shard_map/multiply/pallas_call | solution.py:378
  169.2 0.7 all-to-all-done.2
  169.8 2.3 %collective-permute-start.10 = (f32[8,768]{1,0:T(8,128)S(1)}, f32[8,768]{1,0:T(8,128)S(1)}, u32[]{:S(2)}, u32[]{:S(2)}) collective-permute-start(f32[8,768]{1,0:T(8,128)S(1)} %fusion.5), channel_id=1, source_target_pairs={{0,16},{8,24},{16,0},{24,8},{32,48},{40,56},{48,32},{56,40},{64,80... | collective-permute-start | bytes 73736 | tf_op jit(solution)/shard_map/ppermute | solution.py:659
  172.2 0.9 collective-permute-start.11
  173.1 2.0 convert_reduce_fusion
  175.1 0.0 collective-permute-done.10
  175.1 1.0 collective-permute-done.11
  176.1 1.3 collective-permute-start.12
  177.3 2.4 %collective-permute-start.13 = (f32[8,768]{1,0:T(8,128)S(1)}, f32[8,768]{1,0:T(8,128)S(1)}, u32[]{:S(2)}, u32[]{:S(2)}) collective-permute-start(f32[8,768]{1,0:T(8,128)S(1)} %add_add_fusion.1), channel_id=1, source_target_pairs={{0,64},{8,72},{16,80},{24,88},{32,96},{40,104},{48,112},{56,120},{... | collective-permute-start | bytes 73736 | tf_op jit(solution)/shard_map/ppermute | solution.py:659
  179.7 0.3 collective-permute-start.14
  180.1 1.4 collective-permute-done.13
  181.5 2.1 collective-permute-done.14
  183.7 0.9 pad_maximum_fusion.1
  184.5 8.3 %all-to-all-start.3 = ((f32[8,20,768]{2,1,0:T(8,128)}), f32[8,20,768]{2,1,0:T(8,128)S(1)}, u32[]{:S(2)}, u32[]{:S(2)}) async-start(f32[8,20,768]{2,1,0:T(8,128)} %pad_maximum_fusion.1), calls=%async_computation.3 | async-start | bytes 1179648 | tf_op jit(solution)/shard_map/all_to_all | solution.py:685
  192.8 11.0 %input_gradient.1 = bf16[512,1536]{1,0:T(8,128)(2,1)} custom-call(f32[1,1536]{1,0:T(1,128)S(1)} %reshape.92.gain_ref, bf16[512,3072]{1,0:T(8,128)(2,1)} %conv_backward.1.grad_ref, bf16[1536,3072]{1,0:T(8,128)(2,1)} %all-gather.3.cloned.1.call-done.wl_ref.wg_ref.w_ref, bf16[512,1536]{1,0:T(8,128)(2,1)} %get-tuple-element.76.normed_ref, ...), custom_call_target="tpu_custom_call" | custom-call | flops 1000 | bytes 1000 | tf_op jit(solution)/shard_map/input_gradient/pallas_call | solution.py:627
  203.8 0.0 all-to-all-done.3
  204.0 0.7 pad_maximum_fusion.2
  204.7 0.6 pad_maximum_fusion.3
  (53 shorter events, 0.4 us)
Async XLA Ops:
  7.2 65.5 %all-gather.3.cloned.1.call-start = ((), (), s32[]{:S(2)}) async-start(), calls=%async_computation.4 | async-start | bytes 10616832 | tf_op jit(solution)/shard_map/all_gather | solution.py:778
  7.9 102.6 %all-gather.5.cloned.1.call-start = ((), (), s32[]{:S(2)}) async-start(), calls=%async_computation.5 | async-start | bytes 5308416 | tf_op jit(solution)/shard_map/all_gather | solution.py:779
  8.6 14.2 %copy-start.10 = (s32[1,64]{1,0:T(1,128)S(1)}, s32[1,64]{1,0:T(1,128)}, u32[]{:S(2)}) copy-start(s32[1,64]{1,0:T(1,128)} %param.17) | copy-start | bytes 772
  8.7 14.4 %copy-start.11 = (s32[1,32]{1,0:T(1,128)S(1)}, s32[1,32]{1,0:T(1,128)}, u32[]{:S(2)}) copy-start(s32[1,32]{1,0:T(1,128)} %param.18) | copy-start | bytes 388
  8.7 14.4 %copy-start.9 = (s32[1,32]{1,0:T(1,128)S(1)}, s32[1,32]{1,0:T(1,128)}, u32[]{:S(2)}) copy-start(s32[1,32]{1,0:T(1,128)} %param.19) | copy-start | bytes 388
  8.7 15.1 %copy-start.7 = (f32[1536]{0:T(1024)S(1)}, f32[1536]{0:T(1024)}, u32[]{:S(2)}) copy-start(f32[1536]{0:T(1024)} %param.11) | copy-start | bytes 18436
  8.7 31.6 %all-to-all-start = ((bf16[16,32,1536]{2,1,0:T(8,128)(2,1)}), bf16[16,32,1536]{2,1,0:T(8,128)(2,1)S(1)}, u32[]{:S(2)}, u32[]{:S(2)}) async-start(bf16[16,32,1536]{2,1,0:T(8,128)(2,1)} %bitcast.10), calls=%async_computation | async-start | bytes 3145728 | tf_op jit(solution)/shard_map/all_to_all | solution.py:685
  18.3 18.2 %collective-permute-start = (bf16[16,1536]{1,0:T(8,128)(2,1)S(1)}, bf16[16,1536]{1,0:T(8,128)(2,1)S(1)}, u32[]{:S(2)}, u32[]{:S(2)}) collective-permute-start(bf16[16,1536]{1,0:T(8,128)(2,1)S(1)} %get-tuple-element.84), channel_id=1, source_target_pairs={{0,8},{8,16},{16,24},{24,32},{32,40},{40,48},{48,56},{56,64},{64,7... | collective-permute-start | bytes 147464 | tf_op jit(solution)/shard_map/ppermute | solution.py:655
  21.5 15.6 %collective-permute-start.1 = (bf16[16,1536]{1,0:T(8,128)(2,1)S(1)}, bf16[16,1536]{1,0:T(8,128)(2,1)S(1)}, u32[]{:S(2)}, u32[]{:S(2)}) collective-permute-start(bf16[16,1536]{1,0:T(8,128)(2,1)S(1)} %get-tuple-element.83), channel_id=1, source_target_pairs={{8,0},{16,8},{24,16},{32,24},{40,32},{48,40},{56,48},{64,56},{72,6... | collective-permute-start | bytes 147464 | tf_op jit(solution)/shard_map/ppermute | solution.py:655
  42.1 29.4 %all-to-all-start.1 = ((bf16[16,32,1536]{2,1,0:T(8,128)(2,1)}), bf16[16,32,1536]{2,1,0:T(8,128)(2,1)S(1)}, u32[]{:S(2)}, u32[]{:S(2)}) async-start(bf16[16,32,1536]{2,1,0:T(8,128)(2,1)} %reorder.1), calls=%async_computation.1 | async-start | bytes 3145728 | tf_op jit(solution)/shard_map/all_to_all | solution.py:685
  49.9 38.5 %copy-start.8 = (f32[1536]{0:T(1024)S(1)}, f32[1536]{0:T(1024)}, u32[]{:S(2)}) copy-start(f32[1536]{0:T(1024)} %param.14) | copy-start | bytes 18436
  49.9 38.5 %copy-start.3 = (f32[32,1536]{1,0:T(8,128)S(1)}, f32[32,1536]{1,0:T(8,128)}, u32[]{:S(2)}) copy-start(f32[32,1536]{1,0:T(8,128)} %taps.1) | copy-start | bytes 589828
  71.5 1.1 copy-start.4
  85.2 11.0 %collective-permute-start.2 = (bf16[32,1536]{1,0:T(8,128)(2,1)}, bf16[32,1536]{1,0:T(8,128)(2,1)}, u32[]{:S(2)}, u32[]{:S(2)}) collective-permute-start(bf16[32,1536]{1,0:T(8,128)(2,1)} %get-tuple-element.47), channel_id=1, source_target_pairs={{0,8},{8,16},{16,24},{24,32},{32,40},{40,48},{48,56},{56,64},{64,7... | collective-permute-start | bytes 294920 | tf_op jit(solution)/shard_map/ppermute | solution.py:655
  87.1 9.1 %collective-permute-start.3 = (bf16[32,1536]{1,0:T(8,128)(2,1)}, bf16[32,1536]{1,0:T(8,128)(2,1)}, u32[]{:S(2)}, u32[]{:S(2)}) collective-permute-start(bf16[32,1536]{1,0:T(8,128)(2,1)} %get-tuple-element.48), channel_id=1, source_target_pairs={{8,0},{16,8},{24,16},{32,24},{40,32},{48,40},{56,48},{64,56},{72,6... | collective-permute-start | bytes 294920 | tf_op jit(solution)/shard_map/ppermute | solution.py:655
  96.2 9.6 %copy-start.5 = (bf16[1,1,512,1536]{3,2,1,0:T(8,128)(2,1)S(1)}, bf16[1,1,512,1536]{3,2,1,0:T(8,128)(2,1)}, u32[]{:S(2)}) copy-start(bf16[1,1,512,1536]{3,2,1,0:T(8,128)(2,1)} %param.16) | copy-start | bytes 4718596
  105.7 2.9 %copy-start = (bf16[512,1536]{1,0:T(8,128)(2,1)}, bf16[512,1536]{1,0:T(8,128)(2,1)S(1)}, u32[]{:S(2)}) copy-start(bf16[512,1536]{1,0:T(8,128)(2,1)S(1)} %get-tuple-element.70.x_ref) | copy-start | bytes 4718596
  108.6 11.4 %collective-permute-start.4 = (bf16[1536,768]{1,0:T(8,128)(2,1)}, bf16[1536,768]{1,0:T(8,128)(2,1)}, u32[]{:S(2)}, u32[]{:S(2)}) collective-permute-start(bf16[1536,768]{1,0:T(8,128)(2,1)} %convolution_convert_fusion), channel_id=1, source_target_pairs={{0,1},{1,0},{2,3},{3,2},{4,5},{5,4},{6,7},{7,6},{8,9},{9,8},{10,11... | collective-permute-start | bytes 7077896 | tf_op jit(solution)/shard_map/ppermute | solution.py:659
  110.5 9.6 %copy-start.1 = (bf16[512,1536]{1,0:T(8,128)(2,1)S(1)}, bf16[512,1536]{1,0:T(8,128)(2,1)}, u32[]{:S(2)}) copy-start(bf16[512,1536]{1,0:T(8,128)(2,1)} %copy-done) | copy-start | bytes 4718596
  110.5 9.6 %copy-start.6 = (bf16[1,1,512,1536]{3,2,1,0:T(8,128)(2,1)S(1)}, bf16[1,1,512,1536]{3,2,1,0:T(8,128)(2,1)}, u32[]{:S(2)}) copy-start(bf16[1,1,512,1536]{3,2,1,0:T(8,128)(2,1)} %param.16) | copy-start | bytes 4718596
  124.6 45.2 %all-to-all-start.2 = ((bf16[16,96,768]{2,1,0:T(8,128)(2,1)}), bf16[16,96,768]{2,1,0:T(8,128)(2,1)}, u32[]{:S(2)}, u32[]{:S(2)}) async-start(bf16[16,96,768]{2,1,0:T(8,128)(2,1)} %bitcast.56), calls=%async_computation.2 | async-start | bytes 4718592 | tf_op jit(solution)/shard_map/all_to_all | solution.py:685
  143.6 1.4 collective-permute-start.5
  145.0 18.3 %collective-permute-start.6 = (f32[8,768]{1,0:T(8,128)S(1)}, f32[8,768]{1,0:T(8,128)S(1)}, u32[]{:S(2)}, u32[]{:S(2)}) collective-permute-start(f32[8,768]{1,0:T(8,128)S(1)} %get-tuple-element.89), channel_id=1, source_target_pairs={{0,2},{1,3},{2,0},{3,1},{4,6},{5,7},{6,4},{7,5},{8,10},{9,11},{10,... | collective-permute-start | bytes 73736 | tf_op jit(solution)/shard_map/ppermute | solution.py:659
  146.3 17.0 %collective-permute-start.7 = (f32[8,768]{1,0:T(8,128)S(1)}, f32[8,768]{1,0:T(8,128)S(1)}, u32[]{:S(2)}, u32[]{:S(2)}) collective-permute-start(f32[8,768]{1,0:T(8,128)S(1)} %get-tuple-element.91), channel_id=1, source_target_pairs={{0,4},{1,5},{2,6},{3,7},{4,0},{5,1},{6,2},{7,3},{8,12},{9,13},{10,... | collective-permute-start | bytes 73736 | tf_op jit(solution)/shard_map/ppermute | solution.py:659
  148.7 14.6 %collective-permute-start.8 = (f32[8,768]{1,0:T(8,128)S(1)}, f32[8,768]{1,0:T(8,128)S(1)}, u32[]{:S(2)}, u32[]{:S(2)}) collective-permute-start(f32[8,768]{1,0:T(8,128)S(1)} %get-tuple-element.90), channel_id=1, source_target_pairs={{0,6},{1,7},{2,4},{3,5},{4,2},{5,3},{6,0},{7,1},{8,14},{9,15},{10,... | collective-permute-start | bytes 73736 | tf_op jit(solution)/shard_map/ppermute | solution.py:659
  149.0 14.4 %copy-start.2 = (bf16[512,1536]{1,0:T(8,128)(2,1)S(1)}, bf16[512,1536]{1,0:T(8,128)(2,1)}, u32[]{:S(2)}) copy-start(bf16[512,1536]{1,0:T(8,128)(2,1)} %copy-done) | copy-start | bytes 4718596
  169.8 5.3 %collective-permute-start.10 = (f32[8,768]{1,0:T(8,128)S(1)}, f32[8,768]{1,0:T(8,128)S(1)}, u32[]{:S(2)}, u32[]{:S(2)}) collective-permute-start(f32[8,768]{1,0:T(8,128)S(1)} %fusion.5), channel_id=1, source_target_pairs={{0,16},{8,24},{16,0},{24,8},{32,48},{40,56},{48,32},{56,40},{64,80... | collective-permute-start | bytes 73736 | tf_op jit(solution)/shard_map/ppermute | solution.py:659
  172.2 3.9 %collective-permute-start.11 = (f32[8,768]{1,0:T(8,128)S(1)}, f32[8,768]{1,0:T(8,128)S(1)}, u32[]{:S(2)}, u32[]{:S(2)}) collective-permute-start(f32[8,768]{1,0:T(8,128)S(1)} %fusion.5), channel_id=1, source_target_pairs={{0,24},{8,16},{16,8},{24,0},{32,56},{40,48},{48,40},{56,32},{64,88... | collective-permute-start | bytes 73736 | tf_op jit(solution)/shard_map/ppermute | solution.py:659
  173.1 3.0 %collective-permute-start.9 = (f32[8,768]{1,0:T(8,128)S(1)}, f32[8,768]{1,0:T(8,128)S(1)}, u32[]{:S(2)}, u32[]{:S(2)}) collective-permute-start(f32[8,768]{1,0:T(8,128)S(1)} %fusion.5), channel_id=1, source_target_pairs={{0,8},{8,0},{16,24},{24,16},{32,40},{40,32},{48,56},{56,48},{64,72... | collective-permute-start | bytes 73736 | tf_op jit(solution)/shard_map/ppermute | solution.py:659
  176.1 4.0 %collective-permute-start.12 = (f32[8,768]{1,0:T(8,128)S(1)}, f32[8,768]{1,0:T(8,128)S(1)}, u32[]{:S(2)}, u32[]{:S(2)}) collective-permute-start(f32[8,768]{1,0:T(8,128)S(1)} %add_add_fusion.1), channel_id=1, source_target_pairs={{0,32},{8,40},{16,48},{24,56},{32,0},{40,8},{48,16},{56,24},{64,96... | collective-permute-start | bytes 73736 | tf_op jit(solution)/shard_map/ppermute | solution.py:659
  177.3 4.2 %collective-permute-start.13 = (f32[8,768]{1,0:T(8,128)S(1)}, f32[8,768]{1,0:T(8,128)S(1)}, u32[]{:S(2)}, u32[]{:S(2)}) collective-permute-start(f32[8,768]{1,0:T(8,128)S(1)} %add_add_fusion.1), channel_id=1, source_target_pairs={{0,64},{8,72},{16,80},{24,88},{32,96},{40,104},{48,112},{56,120},{... | collective-permute-start | bytes 73736 | tf_op jit(solution)/shard_map/ppermute | solution.py:659
  179.7 3.9 %collective-permute-start.14 = (f32[8,768]{1,0:T(8,128)S(1)}, f32[8,768]{1,0:T(8,128)S(1)}, u32[]{:S(2)}, u32[]{:S(2)}) collective-permute-start(f32[8,768]{1,0:T(8,128)S(1)} %add_add_fusion.1), channel_id=1, source_target_pairs={{0,96},{8,104},{16,112},{24,120},{32,64},{40,72},{48,80},{56,88},{... | collective-permute-start | bytes 73736 | tf_op jit(solution)/shard_map/ppermute | solution.py:659
  184.5 19.3 %all-to-all-start.3 = ((f32[8,20,768]{2,1,0:T(8,128)}), f32[8,20,768]{2,1,0:T(8,128)S(1)}, u32[]{:S(2)}, u32[]{:S(2)}) async-start(f32[8,20,768]{2,1,0:T(8,128)} %pad_maximum_fusion.1), calls=%async_computation.3 | async-start | bytes 1179648 | tf_op jit(solution)/shard_map/all_to_all | solution.py:685
Sparse Core Ops, SparseCore 0:
  9.7 57.7 all-gather.2
  69.1 34.5 all-gather.4
